TPU v7x, 512 devices: a whole 4x4x16 slice. The times are simulated.
512 devices in a mesh: slab: 64 (over z, y), pencil: 8 (over x, core).
Axes of the slice: x: 4, y: 4, z: 16, core: 2. Of those that a mesh axis runs over, the one named last changes fastest.
Arguments:
- cells: int32 [512, 5632], P(('slab', 'pencil')), may hold values from 0 to 32767
- fractions: float32 [3, 512, 5632], P(None, ('slab', 'pencil')), may hold values from 0 to 1
- adjoint_pos: float32 [3, 512, 5632], P(None, ('slab', 'pencil')), may hold values from -6 to 6
- adjoint_vel: float32 [3, 512, 5632], P(None, ('slab', 'pencil')), may hold values from -6 to 6
- counts: int32 [512, 521], P(('slab', 'pencil')), may hold values from 0 to 512, as said below
Outputs:
- mode_grad: float32 [2, 256, 256, 256], P(None, 'slab', 'pencil')
Inputs may be any that keep to these rules, and one draw needn't show every extreme that they name: Live slots come first in each group; slots at or past the count hold unused values. Near counts are at most 512 and tail counts at most 2. In every draw some owner receives 512 live slots in every near group aimed at it, and some tail count equals 2.
All inputs are finite; a program needn't handle non-finite values.
Results may differ from a plain program's by a relative error of at most 0.004.
Values sent between devices are 32-bit elements; how exact they have to be, the bound alone decides.
No kernel may reach another device: no remote copies, remote signals or barrier semaphores. Data moves between devices by JAX's collectives and lax.ppermute only.
A program may use at most 64 MiB of HBM per device.

v0:
```python
import functools

import jax
import jax.numpy as jnp
import ml_dtypes
import numpy as np
from jax import lax
from jax.experimental import pallas as pl
from jax.experimental.pallas import tpu as pltpu
from jax.sharding import PartitionSpec as P

NG = 256
CAP = 512
TAIL = 2
N_SLAB = 64
N_PENCIL = 8
OWNERS = 512
NEAR = 9 * CAP
TAILS = OWNERS * TAIL
CX = 4
CY = 32
STRIDE = 40
MAIN = CX * STRIDE
PAINT_ROWS = MAIN + STRIDE
CHUNK = 6 * CY + 8

kick_factor = 0.8
drift_factor = 1.25
out_scale = 3.0

f32 = jnp.float32
bf16 = jnp.bfloat16
VMEM = pl.BlockSpec(memory_space=pltpu.VMEM)
SMEM = pl.BlockSpec(memory_space=pltpu.SMEM)
PARAMS = pltpu.CompilerParams(vmem_limit_bytes=24 * 1024 * 1024)


def split_table(table):
    high = table.astype(ml_dtypes.bfloat16)
    low = (table - high.astype(np.float64)).astype(ml_dtypes.bfloat16)
    return high, low


@functools.cache
def host_tables():
    idx = np.arange(NG)
    angles = (idx[:, None] * idx[None, :] % NG) * (2.0 * np.pi / NG)
    cosine, sine = np.cos(angles), np.sin(angles)
    wave = np.where(idx < NG // 2, idx, idx - NG).astype(np.float64)
    table_z = np.concatenate([cosine, -sine], axis=1)
    table_kz = np.concatenate([cosine * wave[None, :], -sine * wave[None, :]], axis=1)
    table_k = np.concatenate([cosine * wave[:, None], sine * wave[:, None], cosine, sine], axis=1)
    order = np.array([4 * s + r for r in range(4) for s in range(N_SLAB)])
    return (
        split_table(table_z),
        split_table(table_kz),
        split_table(table_k[order]),
        split_table(table_k),
    )


def shifted(block, axis, distance):
    devices = range(lax.axis_size(axis))
    route = [((i - distance) % len(devices), i) for i in devices]
    return lax.ppermute(block, axis, route)


def product(table_high, table_low, data):
    high = data.astype(bf16)
    low = (data - high.astype(f32)).astype(bf16)
    dot = functools.partial(jnp.dot, preferred_element_type=f32)
    return dot(table_high, high) + (dot(table_high, low) + dot(table_low, high))


def pack_kernel(counts_ref, counts_vec_ref, cells_ref, frac_ref, pos_ref, vel_ref, down_ref, mid_ref, up_ref, tail_ref, rows, columns):
    for group in range(9):
        out = (down_ref, mid_ref, up_ref)[group // 3]
        src = pl.ds(group * CAP, CAP)
        dst = pl.ds(group % 3 * CAP, CAP)
        live = lax.broadcasted_iota(jnp.int32, (1, CAP), 1) < counts_ref[0, group]
        out[0:1, dst] = cells_ref[:, src].astype(f32)
        for i in range(3):
            out[1 + i : 2 + i, dst] = frac_ref[i, :, src]
            weight = kick_factor * (vel_ref[i, :, src] + drift_factor * pos_ref[i, :, src])
            out[4 + i : 5 + i, dst] = jnp.where(live, weight, 0.0)
        out[7:8, dst] = jnp.zeros((1, CAP), f32)
    width = counts_vec_ref.shape[1]
    slot_of = lax.broadcasted_iota(jnp.int32, (width, TAILS), 1)
    entry = lax.broadcasted_iota(jnp.int32, (width, TAILS), 0)
    spread = jnp.where(slot_of // TAIL + 9 == entry, 1.0, 0.0).astype(bf16)
    counts = jnp.broadcast_to(counts_vec_ref[...].astype(f32), (8, width)).astype(bf16)
    tail_count = jnp.dot(counts, spread, preferred_element_type=f32)[0:1]
    live = (lax.broadcasted_iota(jnp.int32, (1, TAILS), 1) % TAIL).astype(f32) < tail_count
    src = pl.ds(NEAR, TAILS)
    rows[0:1] = cells_ref[:, src].astype(f32)
    for i in range(3):
        rows[1 + i : 2 + i] = frac_ref[i, :, src]
        weight = kick_factor * (vel_ref[i, :, src] + drift_factor * pos_ref[i, :, src])
        rows[4 + i : 5 + i] = jnp.where(live, weight, 0.0)
    rows[7:8] = jnp.zeros((1, TAILS), f32)
    columns[...] = rows[...].T
    for k in range(16):
        tail_ref[:, 8 * k : 8 * k + 8] = columns[pl.ds(k, N_SLAB, stride=16), :]


def pack(counts, cells, fractions, adjoint_pos, adjoint_vel):
    side = jax.ShapeDtypeStruct((8, 3 * CAP), f32)
    return pl.pallas_call(
        pack_kernel,
        out_shape=(side, side, side, jax.ShapeDtypeStruct((N_SLAB, 128), f32)),
        in_specs=[SMEM] + [VMEM] * 5,
        out_specs=(VMEM,) * 4,
        scratch_shapes=[pltpu.VMEM((8, TAILS), f32), pltpu.VMEM((TAILS, 8), f32)],
        compiler_params=PARAMS,
        name="pack",
    )(counts, counts, cells, fractions, adjoint_pos, adjoint_vel)


def repack_kernel(in_ref, out_ref):
    for p in range(N_PENCIL):
        for k in range(8):
            out_ref[p, :, 16 * k : 16 * k + 16] = in_ref[8 * k : 8 * k + 8, 16 * p : 16 * p + 16]


def repack(tail):
    return pl.pallas_call(
        repack_kernel,
        out_shape=jax.ShapeDtypeStruct((N_PENCIL, 8, 128), f32),
        in_specs=[VMEM],
        out_specs=VMEM,
        compiler_params=PARAMS,
        name="repack",
    )(tail)


def paint(values, acc_ref):
    slots = values.shape[1]
    cell = values[0:1].astype(jnp.int32)
    row = lax.shift_right_logical(cell, 13) * STRIDE + (lax.shift_right_logical(cell, 8) & 31)
    base_z = cell & 255
    next_z = (base_z + 1) & 255
    frac_x, frac_y, frac_z = values[1:2], values[2:3], values[3:4]
    rest_x, rest_y, rest_z = 1.0 - frac_x, 1.0 - frac_y, 1.0 - frac_z

    def rounded(value):
        return value.astype(bf16).astype(f32)

    row_ids = lax.broadcasted_iota(jnp.int32, (PAINT_ROWS, slots), 0)
    corner = jnp.where(row_ids == row, rounded(rest_x * rest_y), 0.0)
    corner = jnp.where(row_ids == row + 1, rounded(rest_x * frac_y), corner)
    corner = jnp.where(row_ids == row + STRIDE, rounded(frac_x * rest_y), corner)
    corner = jnp.where(row_ids == row + STRIDE + 1, rounded(frac_x * frac_y), corner).astype(bf16)
    z_ids = lax.broadcasted_iota(jnp.int32, (NG, slots), 0)
    at_low, at_high = z_ids == base_z, z_ids == next_z
    for i in range(3):
        weight = values[4 + i : 5 + i]
        line = jnp.where(at_low, rounded(weight * rest_z), 0.0)
        line = jnp.where(at_high, rounded(weight * frac_z), line).astype(bf16)
        acc_ref[:, i * NG : (i + 1) * NG] += lax.dot_general(
            corner, line, (((1,), (1,)), ((), ())), preferred_element_type=f32
        )


def near_kernel(down_ref, left_ref, mid_ref, right_ref, up_ref, out_ref):
    out_ref[...] = jnp.zeros_like(out_ref)
    for ref in (left_ref, mid_ref, right_ref):
        paint(ref[:, CAP : 2 * CAP], out_ref)

    def body(step, carry):
        at = pl.ds(pl.multiple_of(step * CAP, CAP), CAP)
        paint(down_ref[:, at], out_ref)
        paint(up_ref[:, at], out_ref)
        return carry

    lax.fori_loop(0, 3, body, 0)


def paint_near(down, left, mid, right, up):
    return pl.pallas_call(
        near_kernel,
        out_shape=jax.ShapeDtypeStruct((PAINT_ROWS, 3 * NG), f32),
        in_specs=[VMEM] * 5,
        out_specs=VMEM,
        compiler_params=PARAMS,
        cost_estimate=pl.CostEstimate(flops=2 * NEAR * PAINT_ROWS * 3 * NG, bytes_accessed=2_000_000, transcendentals=0),
        name="paint_near",
    )(down, left, mid, right, up)


def tail_kernel(tail_ref, near_ref, main_ref, spill_ref, values, acc):
    turned = tail_ref[...].T
    for k in range(16):
        values[:, 64 * k : 64 * k + 64] = turned[8 * k : 8 * k + 8, :]
    acc[...] = near_ref[...]
    for half in range(2):
        paint(values[:, half * 512 : half * 512 + 512], acc)
    main_ref[...] = acc[:MAIN]
    spill_ref[...] = acc[MAIN:]


def paint_tail(tail, near):
    return pl.pallas_call(
        tail_kernel,
        out_shape=(jax.ShapeDtypeStruct((MAIN, 3 * NG), f32), jax.ShapeDtypeStruct((STRIDE, 3 * NG), f32)),
        in_specs=[VMEM] * 2,
        out_specs=(VMEM,) * 2,
        scratch_shapes=[pltpu.VMEM((8, TAILS), f32), pltpu.VMEM((PAINT_ROWS, 3 * NG), f32)],
        compiler_params=PARAMS,
        name="paint_tail",
    )(tail, near)


def z_kernel(main_ref, spill_ref, plain_high, plain_low, scaled_high, scaled_low, out_ref):
    for i in range(3):
        columns = pl.ds(i * NG, NG)
        data = jnp.concatenate(
            [main_ref[:STRIDE, columns] + spill_ref[:, columns], main_ref[STRIDE:, columns]], axis=0
        )
        high = data.astype(bf16)
        low = (data - high.astype(f32)).astype(bf16)
        table_high, table_low = (scaled_high, scaled_low) if i == 2 else (plain_high, plain_low)
        dot = functools.partial(jnp.dot, preferred_element_type=f32)
        result = dot(high, table_high[...]) + (dot(low, table_high[...]) + dot(high, table_low[...]))
        for part in range(2):
            block = 2 * i + part
            for p in range(N_PENCIL):
                at = part * NG + p * 32
                chunk = jnp.concatenate(
                    [result[x * STRIDE : (x + 1) * STRIDE, at : at + 32] for x in range(CX)], axis=1
                )
                out_ref[p, block * CY : (block + 1) * CY, :] = chunk[:CY]
                out_ref[p, 6 * CY + block : 6 * CY + block + 1, :] = chunk[CY : CY + 1]
    out_ref[:, 6 * CY + 6 :, :] = jnp.zeros((N_PENCIL, 2, 128), f32)


def transform_z(main, spill, plain, scaled):
    return pl.pallas_call(
        z_kernel,
        out_shape=jax.ShapeDtypeStruct((N_PENCIL, CHUNK, 128), f32),
        in_specs=[VMEM] * 6,
        out_specs=VMEM,
        compiler_params=PARAMS,
        name="transform_z",
    )(main, spill, *plain, *scaled)


def mixed_rhs(real, imag):
    return jnp.concatenate(
        [jnp.concatenate([real, imag], axis=1), jnp.concatenate([imag, -real], axis=1)], axis=0
    )


def y_kernel(in_ref, table_high, table_low, out_ref):
    first = lax.broadcasted_iota(jnp.int32, (CY, 128), 0) == 0
    blocks = []
    for block in range(6):
        parts = []
        for src in range(N_PENCIL):
            spilled = in_ref[(src - 1) % N_PENCIL, 6 * CY + block : 6 * CY + block + 1, :]
            parts.append(in_ref[src, block * CY : (block + 1) * CY, :] + jnp.where(first, spilled, 0.0))
        blocks.append(jnp.concatenate(parts, axis=0))
    field = product(table_high[:, 2 * NG :], table_low[:, 2 * NG :], mixed_rhs(blocks[0], blocks[1]))
    sides = jnp.concatenate([mixed_rhs(blocks[2], blocks[3]), mixed_rhs(blocks[4], blocks[5])], axis=0)
    mixed = product(table_high[...], table_low[...], sides)
    for f, result in enumerate((field, mixed)):
        for part in range(2):
            for x in range(CX):
                at = part * 128 + x * 32
                chunk = jnp.concatenate(
                    [result[r * N_SLAB : (r + 1) * N_SLAB, at : at + 32] for r in range(4)], axis=1
                )
                out_ref[pl.ds(x * 4 + f * 2 + part, N_SLAB, stride=16), :] = chunk


def transform_y(by_rows, table):
    return pl.pallas_call(
        y_kernel,
        out_shape=jax.ShapeDtypeStruct((N_SLAB * 16, 128), f32),
        in_specs=[VMEM] * 3,
        out_specs=VMEM,
        compiler_params=PARAMS,
        name="transform_y",
    )(by_rows, *table)


def wavenumber(position):
    return jnp.where(position < NG // 2, position, position - NG).astype(f32)


def x_kernel(place_ref, in_ref, table_high, table_low, out_ref):
    lines = [in_ref[pl.ds(block, NG, stride=4), :] for block in range(4)]
    data = jnp.concatenate([mixed_rhs(lines[0], lines[1]), mixed_rhs(lines[2], lines[3])], axis=0)
    mixed = product(table_high[...], table_low[...], data)
    lane = lax.broadcasted_iota(jnp.int32, (1, 128), 1)
    wave_y = wavenumber(place_ref[0] * 4 + lane // 32)
    wave_z = wavenumber(place_ref[1] * 32 + lane % 32)
    wave_x = wavenumber(lax.broadcasted_iota(jnp.int32, (NG, 1), 0))
    wave_sq = wave_x * wave_x + wave_y * wave_y + wave_z * wave_z
    factor = jnp.where(wave_sq > 0, out_scale / jnp.sqrt(jnp.maximum(wave_sq, 1.0)), 0.0) / NG**1.5
    out_ref[0] = (mixed[:, 128:] * factor).T
    out_ref[1] = (mixed[:, :128] * -factor).T


def transform_x(place, by_cols, table):
    return pl.pallas_call(
        x_kernel,
        out_shape=jax.ShapeDtypeStruct((2, 128, NG), f32),
        in_specs=[SMEM] + [VMEM] * 3,
        out_specs=VMEM,
        compiler_params=PARAMS,
        name="transform_x",
    )(place, by_cols, *table)


def local(cells, fractions, adjoint_pos, adjoint_vel, counts):
    plain, scaled, table_y, table_x = [tuple(jnp.asarray(t) for t in pair) for pair in host_tables()]
    to_below, own, to_above, tail = pack(counts, cells, fractions, adjoint_pos, adjoint_vel)
    tail = lax.all_to_all(tail.reshape(N_SLAB, 1, 128), "slab", 0, 0, tiled=True)
    from_above = shifted(to_below, "slab", -1)
    from_below = shifted(to_above, "slab", 1)
    tail = repack(tail.reshape(N_SLAB, 128))
    tail = lax.all_to_all(tail, "pencil", 0, 0, tiled=True)
    bands = (from_above, own, from_below)
    to_left = jnp.concatenate([band[:, :CAP] for band in bands], axis=1)
    to_right = jnp.concatenate([band[:, 2 * CAP :] for band in bands], axis=1)
    from_right = shifted(to_left, "pencil", -1)
    from_left = shifted(to_right, "pencil", 1)
    near = paint_near(from_left, from_above, own, from_below, from_right)
    main, spill = paint_tail(tail.reshape(N_SLAB, 128), near)
    spill = shifted(spill, "slab", 1)
    by_rows = transform_z(main, spill, plain, scaled)
    by_rows = lax.all_to_all(by_rows, "pencil", 0, 0, tiled=True)
    by_cols = transform_y(by_rows, table_y)
    by_cols = lax.all_to_all(by_cols.reshape(N_SLAB, 16, 128), "slab", 0, 0, tiled=True)
    place = jnp.stack([lax.axis_index("slab"), lax.axis_index("pencil")]).astype(jnp.int32)
    result = transform_x(place, by_cols.reshape(N_SLAB * 16, 128), table_x)
    return result.reshape(2, CX, 32, NG)


def solution(mesh):
    in_specs = (
        P(("slab", "pencil"), None),
        P(None, ("slab", "pencil"), None),
        P(None, ("slab", "pencil"), None),
        P(None, ("slab", "pencil"), None),
        P(("slab", "pencil"), None),
    )
    out_specs = P(None, "slab", "pencil", None)
    return jax.shard_map(local, mesh=mesh, in_specs=in_specs, out_specs=out_specs, check_vma=False)
```

profile of v0, /device:TPU:8, one launch (start us, length us, event | category | flops | bytes accessed | tf_op | source)
XLA Modules:
  0.0 130.7 jit_solution(10512745071083835136)
XLA Ops:
  0.0 0.9 copy-done.8
  0.9 0.9 copy-done.9
  1.8 0.9 copy-done.10
  2.7 0.7 copy-done.11
  3.4 0.7 copy-done.12
  4.1 1.9 %pack.1 = (f32[8,1536]{1,0:T(8,128)S(1)}, f32[8,1536]{1,0:T(8,128)S(1)}, f32[8,1536]{1,0:T(8,128)S(1)}, f32[64,128]{1,0:T(8,128)}) custom-call(s32[1,521]{1,0:T(1,128)S(1)} %copy-done.12, s32[1,521]{1,0:T(1,128)S(1)} %copy-done.12, s32[1,5632]{1,0:T(1,128)S(1)} %copy-done.11, f32[3,1,5632]{2,1,0:T(1,128)S(1)} %copy-done.8, f32[3,1,5632]{2,1,0:T(1,128)S(1)} %copy-done.9, ...), custom_call_target="tpu_custom_call" | custom-call | tf_op jit(solution)/shard_map/pack/pallas_call | solution.py:108
  6.0 7.7 %collective-permute-start = (f32[8,1536]{1,0:T(8,128)S(1)}, f32[8,1536]{1,0:T(8,128)S(1)}, u32[]{:S(2)}, u32[]{:S(2)}) collective-permute-start(f32[8,1536]{1,0:T(8,128)S(1)} %get-tuple-element.12), channel_id=1, source_target_pairs={{8,0},{16,8},{24,16},{32,24},{40,32},{48,40},{56,48},{64,56},{72,6... | collective-permute-start | bytes 147464 | tf_op jit(solution)/shard_map/ppermute | solution.py:65
  13.7 1.9 %collective-permute-start.1 = (f32[8,1536]{1,0:T(8,128)S(1)}, f32[8,1536]{1,0:T(8,128)S(1)}, u32[]{:S(2)}, u32[]{:S(2)}) collective-permute-start(f32[8,1536]{1,0:T(8,128)S(1)} %get-tuple-element.14), channel_id=1, source_target_pairs={{504,0},{0,8},{8,16},{16,24},{24,32},{32,40},{40,48},{48,56},{56,6... | collective-permute-start | bytes 147464 | tf_op jit(solution)/shard_map/ppermute | solution.py:65
  15.6 16.9 %all-to-all-start = ((f32[64,1,128]{2,1,0:T(1,128)}), f32[64,1,128]{2,1,0:T(1,128)S(1)}, u32[]{:S(2)}, u32[]{:S(2)}) async-start(f32[64,1,128]{2,1,0:T(1,128)} %bitcast.3), calls=%async_computation | async-start | bytes 65536 | tf_op jit(solution)/shard_map/all_to_all | solution.py:318
  32.6 1.1 collective-permute-start.3
  33.7 12.6 %all-to-all-done = f32[64,1,128]{2,1,0:T(1,128)S(1)} async-done(((f32[64,1,128]{2,1,0:T(1,128)}), f32[64,1,128]{2,1,0:T(1,128)S(1)}, u32[]{:S(2)}, u32[]{:S(2)}) %all-to-all-start) | async-done | bytes 32800 | tf_op jit(solution)/shard_map/all_to_all | solution.py:318
  46.2 0.7 repack.1
  47.0 4.3 %all-to-all-start.1 = ((f32[8,8,128]{2,1,0:T(8,128)}), f32[8,8,128]{2,1,0:T(8,128)S(1)}, u32[]{:S(2)}, u32[]{:S(2)}) async-start(f32[8,8,128]{2,1,0:T(8,128)} %repack.1), calls=%async_computation.1 | async-start | bytes 65536 | tf_op jit(solution)/shard_map/all_to_all | solution.py:322
  51.3 5.4 %paint_near.1.near_ref = f32[200,768]{1,0:T(8,128)S(1)} custom-call(f32[8,1536]{1,0:T(8,128)S(1)} %collective-permute-done.2.down_ref, f32[8,1536]{1,0:T(8,128)S(1)} %collective-permute-done.left_ref, f32[8,1536]{1,0:T(8,128)S(1)} %get-tuple-element.13.mid_ref, f32[8,1536]{1,0:T(8,128)S(1)} %collective-permute-done.1.right_ref, ...), custom_call_target="tpu_custom_call" | custom-call | flops 1415577600 | bytes 2000000 | tf_op jit(solution)/shard_map/paint_near/pallas_call | solution.py:179
  56.8 1.4 %paint_tail.1 = (f32[160,768]{1,0:T(8,128)S(1)}, f32[40,768]{1,0:T(8,128)S(1)}) custom-call(f32[64,128]{1,0:T(8,128)S(1)} %bitcast.11, f32[200,768]{1,0:T(8,128)S(1)} %paint_near.1.near_ref), custom_call_target="tpu_custom_call" | custom-call | tf_op jit(solution)/shard_map/paint_tail/pallas_call | solution.py:202
  58.2 2.5 %collective-permute-start.4 = (f32[40,768]{1,0:T(8,128)S(1)}, f32[40,768]{1,0:T(8,128)S(1)}, u32[]{:S(2)}, u32[]{:S(2)}) collective-permute-start(f32[40,768]{1,0:T(8,128)S(1)} %get-tuple-element.16), channel_id=1, source_target_pairs={{504,0},{0,8},{8,16},{16,24},{24,32},{32,40},{40,48},{48,56},{56,6... | collective-permute-start | bytes 368648 | tf_op jit(solution)/shard_map/ppermute | solution.py:65
  60.7 5.1 %collective-permute-done.4.spill_ref = f32[40,768]{1,0:T(8,128)S(1)} collective-permute-done((f32[40,768]{1,0:T(8,128)S(1)}, f32[40,768]{1,0:T(8,128)S(1)}, u32[]{:S(2)}, u32[]{:S(2)}) %collective-permute-start.4) | collective-permute-done | bytes 122912 | tf_op jit(solution)/shard_map/ppermute | solution.py:65
  65.8 1.1 transform_z.1
  66.9 18.0 %all_to_all.20.in_ref = f32[8,200,128]{2,1,0:T(8,128)S(1)} all-to-all(f32[8,200,128]{2,1,0:T(8,128)S(1)} %transform_z.1), channel_id=1, replica_groups=mesh['slab'=64,'pencil'=8] {'pencil'}, dimensions={0} | all-to-all | bytes 1638400 | tf_op jit(solution)/shard_map/all_to_all | solution.py:332
  84.9 1.9 %transform_y.1 = f32[1024,128]{1,0:T(8,128)} custom-call(f32[8,200,128]{2,1,0:T(8,128)S(1)} %all_to_all.20.in_ref, bf16[256,1024]{1,0:T(8,128)(2,1)S(1)} %copy-done.2, bf16[256,1024]{1,0:T(8,128)(2,1)S(1)} %copy-done.3), custom_call_target="tpu_custom_call" | custom-call | tf_op jit(solution)/shard_map/transform_y/pallas_call | solution.py:276
  86.8 8.8 %all-to-all-start.3 = ((f32[64,16,128]{2,1,0:T(8,128)}), f32[64,16,128]{2,1,0:T(8,128)S(1)}, u32[]{:S(2)}, u32[]{:S(2)}) async-start(f32[64,16,128]{2,1,0:T(8,128)} %bitcast.6), calls=%async_computation.3 | async-start | bytes 1048576 | tf_op jit(solution)/shard_map/all_to_all | solution.py:334
  95.6 0.1 pad_add_fusion.place_ref
  95.7 33.1 %all-to-all-done.3 = f32[64,16,128]{2,1,0:T(8,128)S(1)} async-done(((f32[64,16,128]{2,1,0:T(8,128)}), f32[64,16,128]{2,1,0:T(8,128)S(1)}, u32[]{:S(2)}, u32[]{:S(2)}) %all-to-all-start.3) | async-done | bytes 524320 | tf_op jit(solution)/shard_map/all_to_all | solution.py:334
  128.8 1.9 %transform_x.1 = f32[2,128,256]{2,1,0:T(8,128)} custom-call(s32[2]{0:T(128)S(1)} %pad_add_fusion.place_ref, f32[1024,128]{1,0:T(8,128)S(1)} %bitcast.10, bf16[256,1024]{1,0:T(8,128)(2,1)S(1)} %copy-done, bf16[256,1024]{1,0:T(8,128)(2,1)S(1)} %copy-done.1), custom_call_target="tpu_custom_call" | custom-call | tf_op jit(solution)/shard_map/transform_x/pallas_call | solution.py:305
  (32 shorter events, 0.1 us)
Async XLA Ops:
  0.0 0.9 copy-start.8
  0.9 0.9 copy-start.9
  1.8 0.9 copy-start.10
  2.6 0.7 copy-start.11
  3.4 0.7 copy-start.12
  6.0 26.5 %collective-permute-start = (f32[8,1536]{1,0:T(8,128)S(1)}, f32[8,1536]{1,0:T(8,128)S(1)}, u32[]{:S(2)}, u32[]{:S(2)}) collective-permute-start(f32[8,1536]{1,0:T(8,128)S(1)} %get-tuple-element.12), channel_id=1, source_target_pairs={{8,0},{16,8},{24,16},{32,24},{40,32},{48,40},{56,48},{64,56},{72,6... | collective-permute-start | bytes 147464 | tf_op jit(solution)/shard_map/ppermute | solution.py:65
  13.7 18.8 %collective-permute-start.1 = (f32[8,1536]{1,0:T(8,128)S(1)}, f32[8,1536]{1,0:T(8,128)S(1)}, u32[]{:S(2)}, u32[]{:S(2)}) collective-permute-start(f32[8,1536]{1,0:T(8,128)S(1)} %get-tuple-element.14), channel_id=1, source_target_pairs={{504,0},{0,8},{8,16},{16,24},{24,32},{32,40},{40,48},{48,56},{56,6... | collective-permute-start | bytes 147464 | tf_op jit(solution)/shard_map/ppermute | solution.py:65
  15.6 30.6 %all-to-all-start = ((f32[64,1,128]{2,1,0:T(1,128)}), f32[64,1,128]{2,1,0:T(1,128)S(1)}, u32[]{:S(2)}, u32[]{:S(2)}) async-start(f32[64,1,128]{2,1,0:T(1,128)} %bitcast.3), calls=%async_computation | async-start | bytes 65536 | tf_op jit(solution)/shard_map/all_to_all | solution.py:318
  32.6 18.7 %collective-permute-start.3 = (f32[8,1536]{1,0:T(8,128)S(1)}, f32[8,1536]{1,0:T(8,128)S(1)}, u32[]{:S(2)}, u32[]{:S(2)}) collective-permute-start(f32[8,1536]{1,0:T(8,128)S(1)} %pad_maximum_fusion.1), channel_id=1, source_target_pairs={{1,0},{2,1},{3,2},{4,3},{5,4},{6,5},{7,6},{0,7},{9,8},{10,9},{11,1... | collective-permute-start | bytes 147464 | tf_op jit(solution)/shard_map/ppermute | solution.py:65
  33.7 17.6 %collective-permute-start.2 = (f32[8,1536]{1,0:T(8,128)S(1)}, f32[8,1536]{1,0:T(8,128)S(1)}, u32[]{:S(2)}, u32[]{:S(2)}) collective-permute-start(f32[8,1536]{1,0:T(8,128)S(1)} %pad_maximum_fusion), channel_id=1, source_target_pairs={{7,0},{0,1},{1,2},{2,3},{3,4},{4,5},{5,6},{6,7},{15,8},{8,9},{9,10... | collective-permute-start | bytes 147464 | tf_op jit(solution)/shard_map/ppermute | solution.py:65
  47.0 9.8 %all-to-all-start.1 = ((f32[8,8,128]{2,1,0:T(8,128)}), f32[8,8,128]{2,1,0:T(8,128)S(1)}, u32[]{:S(2)}, u32[]{:S(2)}) async-start(f32[8,8,128]{2,1,0:T(8,128)} %repack.1), calls=%async_computation.1 | async-start | bytes 65536 | tf_op jit(solution)/shard_map/all_to_all | solution.py:322
  51.3 14.5 %copy-start.6 = (bf16[256,512]{1,0:T(8,128)(2,1)S(1)}, bf16[256,512]{1,0:T(8,128)(2,1)}, u32[]{:S(2)}) copy-start(bf16[256,512]{1,0:T(8,128)(2,1)} %constant.27.clone.scaled_high) | copy-start | bytes 786436
  51.3 14.5 %copy-start.7 = (bf16[256,512]{1,0:T(8,128)(2,1)S(1)}, bf16[256,512]{1,0:T(8,128)(2,1)}, u32[]{:S(2)}) copy-start(bf16[256,512]{1,0:T(8,128)(2,1)} %constant.28.clone.scaled_low) | copy-start | bytes 786436
  56.8 9.0 %copy-start.4 = (bf16[256,512]{1,0:T(8,128)(2,1)S(1)}, bf16[256,512]{1,0:T(8,128)(2,1)}, u32[]{:S(2)}) copy-start(bf16[256,512]{1,0:T(8,128)(2,1)} %constant.25.clone.plain_high) | copy-start | bytes 786436
  56.8 9.0 %copy-start.5 = (bf16[256,512]{1,0:T(8,128)(2,1)S(1)}, bf16[256,512]{1,0:T(8,128)(2,1)}, u32[]{:S(2)}) copy-start(bf16[256,512]{1,0:T(8,128)(2,1)} %constant.26.clone.plain_low) | copy-start | bytes 786436
  58.2 7.6 %collective-permute-start.4 = (f32[40,768]{1,0:T(8,128)S(1)}, f32[40,768]{1,0:T(8,128)S(1)}, u32[]{:S(2)}, u32[]{:S(2)}) collective-permute-start(f32[40,768]{1,0:T(8,128)S(1)} %get-tuple-element.16), channel_id=1, source_target_pairs={{504,0},{0,8},{8,16},{16,24},{24,32},{32,40},{40,48},{48,56},{56,6... | collective-permute-start | bytes 368648 | tf_op jit(solution)/shard_map/ppermute | solution.py:65
  66.9 18.0 %copy-start.2 = (bf16[256,1024]{1,0:T(8,128)(2,1)S(1)}, bf16[256,1024]{1,0:T(8,128)(2,1)}, u32[]{:S(2)}) copy-start(bf16[256,1024]{1,0:T(8,128)(2,1)} %constant.29.clone.table_high) | copy-start | bytes 1572868
  66.9 18.0 %copy-start.3 = (bf16[256,1024]{1,0:T(8,128)(2,1)S(1)}, bf16[256,1024]{1,0:T(8,128)(2,1)}, u32[]{:S(2)}) copy-start(bf16[256,1024]{1,0:T(8,128)(2,1)} %constant.30.clone.table_low) | copy-start | bytes 1572868
  86.8 42.0 %copy-start = (bf16[256,1024]{1,0:T(8,128)(2,1)S(1)}, bf16[256,1024]{1,0:T(8,128)(2,1)}, u32[]{:S(2)}) copy-start(bf16[256,1024]{1,0:T(8,128)(2,1)} %constant.31.clone.table_high) | copy-start | bytes 1572868
  86.8 42.0 %copy-start.1 = (bf16[256,1024]{1,0:T(8,128)(2,1)S(1)}, bf16[256,1024]{1,0:T(8,128)(2,1)}, u32[]{:S(2)}) copy-start(bf16[256,1024]{1,0:T(8,128)(2,1)} %constant.32.clone.table_low) | copy-start | bytes 1572868
  86.8 42.0 %all-to-all-start.3 = ((f32[64,16,128]{2,1,0:T(8,128)}), f32[64,16,128]{2,1,0:T(8,128)S(1)}, u32[]{:S(2)}, u32[]{:S(2)}) async-start(f32[64,16,128]{2,1,0:T(8,128)} %bitcast.6), calls=%async_computation.3 | async-start | bytes 1048576 | tf_op jit(solution)/shard_map/all_to_all | solution.py:334
where the time goes:
time: 131 us
  waiting for transfers between devices  50.8 us (39%)
  starting transfers between devices  43.2 us (33%)
  blocking collectives  18 us (14%)
  Pallas kernels  14.4 us (11%)
  local copies, waits for them, and re-layouts  4.12 us (3%)
    all_to_all x1, waiting for transfers between devices, local(): lax.all_to_all(by_cols.reshape(N_SLAB, 16, 128), 'slab', 0, 0, tiled=True)  33.1 us
    all_to_all x1, blocking collectives, local(): by_rows = lax.all_to_all(by_rows, 'pencil', 0, 0, tiled=True)  18 us
    all_to_all x1, starting transfers between devices, local(): lax.all_to_all(tail.reshape(N_SLAB, 1, 128), 'slab', 0, 0, tiled=True)  16.9 us
    ppermute x5, starting transfers between devices, shifted(): return lax.ppermute(block, axis, route)  13.2 us
    all_to_all x1, waiting for transfers between devices, local(): lax.all_to_all(tail.reshape(N_SLAB, 1, 128), 'slab', 0, 0, tiled=True)  12.6 us
    all_to_all x1, starting transfers between devices, local(): lax.all_to_all(by_cols.reshape(N_SLAB, 16, 128), 'slab', 0, 0, tiled=True)  8.8 us
    pallas_call x1, Pallas kernels, paint_near(): pl.pallas_call(near_kernel, out_shape=jax.ShapeDtypeStruct((PAINT_ROWS, 3...  5.43 us
    ppermute x5, waiting for transfers between devices, shifted(): return lax.ppermute(block, axis, route)  5.13 us
  transfers between devices with their start and end apart: 8, of which 3 were waited for; matrix products, arithmetic and copies ran while one was open for 0% of the time, Pallas kernels for 5%

commit v1 on v0

--- a/solution.py
+++ b/solution.py
@@ -21,7 +21,6 @@
 CY = 32
 STRIDE = 40
 MAIN = CX * STRIDE
-PAINT_ROWS = MAIN + STRIDE
 CHUNK = 6 * CY + 8
 
 kick_factor = 0.8
@@ -32,6 +31,9 @@
 bf16 = jnp.bfloat16
 VMEM = pl.BlockSpec(memory_space=pltpu.VMEM)
 SMEM = pl.BlockSpec(memory_space=pltpu.SMEM)
+HBM = pl.BlockSpec(memory_space=pltpu.HBM)
+ANY = pl.BlockSpec(memory_space=pl.ANY)
+WIDE = pltpu.CompilerParams(vmem_limit_bytes=60 * 1024 * 1024)
 PARAMS = pltpu.CompilerParams(vmem_limit_bytes=24 * 1024 * 1024)
 
 
@@ -72,150 +74,190 @@
     return dot(table_high, high) + (dot(table_high, low) + dot(table_low, high))
 
 
-def pack_kernel(counts_ref, counts_vec_ref, cells_ref, frac_ref, pos_ref, vel_ref, down_ref, mid_ref, up_ref, tail_ref, rows, columns):
-    for group in range(9):
-        out = (down_ref, mid_ref, up_ref)[group // 3]
-        src = pl.ds(group * CAP, CAP)
-        dst = pl.ds(group % 3 * CAP, CAP)
-        live = lax.broadcasted_iota(jnp.int32, (1, CAP), 1) < counts_ref[0, group]
-        out[0:1, dst] = cells_ref[:, src].astype(f32)
-        for i in range(3):
-            out[1 + i : 2 + i, dst] = frac_ref[i, :, src]
-            weight = kick_factor * (vel_ref[i, :, src] + drift_factor * pos_ref[i, :, src])
-            out[4 + i : 5 + i, dst] = jnp.where(live, weight, 0.0)
-        out[7:8, dst] = jnp.zeros((1, CAP), f32)
-    width = counts_vec_ref.shape[1]
+def start_copies(pairs, sems):
+    copies = [pltpu.make_async_copy(src, dst, sems.at[i]) for i, (src, dst) in enumerate(pairs)]
+    for copy in copies:
+        copy.start()
+    return copies
+
+
+def particle_rows(out, lanes, live, cells, frac, pos, vel):
+    out[0:1, lanes] = cells.astype(f32)
+    for i in range(3):
+        out[1 + i : 2 + i, lanes] = frac[i]
+        weight = kick_factor * (vel[i] + drift_factor * pos[i])
+        out[4 + i : 5 + i, lanes] = jnp.where(live, weight, 0.0)
+    out[7:8, lanes] = jnp.zeros(cells.shape, f32)
+
+
+def pack_kernel(counts_smem, counts_hbm, cells_hbm, frac_hbm, pos_hbm, vel_hbm, tail_ref, left_ref, mid_ref, right_ref, counts_ref, cells_ref, frac_ref, pos_ref, vel_ref, rows, columns, flat, sems):
+    copies = start_copies(
+        [(counts_hbm, counts_ref), (cells_hbm, cells_ref), (frac_hbm, frac_ref), (pos_hbm, pos_ref), (vel_hbm, vel_ref)], sems
+    )
+    width = counts_ref.shape[1]
     slot_of = lax.broadcasted_iota(jnp.int32, (width, TAILS), 1)
     entry = lax.broadcasted_iota(jnp.int32, (width, TAILS), 0)
     spread = jnp.where(slot_of // TAIL + 9 == entry, 1.0, 0.0).astype(bf16)
-    counts = jnp.broadcast_to(counts_vec_ref[...].astype(f32), (8, width)).astype(bf16)
+    for copy in copies:
+        copy.wait()
+
+    def fill(out, lanes, src, live):
+        particle_rows(out, lanes, live, cells_ref[:, src], frac_ref[:, :, src], pos_ref[:, :, src], vel_ref[:, :, src])
+
+    counts = jnp.broadcast_to(counts_ref[...].astype(f32), (8, width)).astype(bf16)
     tail_count = jnp.dot(counts, spread, preferred_element_type=f32)[0:1]
     live = (lax.broadcasted_iota(jnp.int32, (1, TAILS), 1) % TAIL).astype(f32) < tail_count
-    src = pl.ds(NEAR, TAILS)
-    rows[0:1] = cells_ref[:, src].astype(f32)
-    for i in range(3):
-        rows[1 + i : 2 + i] = frac_ref[i, :, src]
-        weight = kick_factor * (vel_ref[i, :, src] + drift_factor * pos_ref[i, :, src])
-        rows[4 + i : 5 + i] = jnp.where(live, weight, 0.0)
-    rows[7:8] = jnp.zeros((1, TAILS), f32)
+    fill(rows, pl.ds(0, TAILS), pl.ds(NEAR, TAILS), live)
     columns[...] = rows[...].T
     for k in range(16):
-        tail_ref[:, 8 * k : 8 * k + 8] = columns[pl.ds(k, N_SLAB, stride=16), :]
+        flat[:, 8 * k : 8 * k + 8] = columns[pl.ds(k, N_SLAB, stride=16), :]
+    for p in range(N_PENCIL):
+        for k in range(8):
+            tail_ref[p, :, 16 * k : 16 * k + 16] = flat[8 * k : 8 * k + 8, 16 * p : 16 * p + 16]
+    for group in range(9):
+        live = lax.broadcasted_iota(jnp.int32, (1, CAP), 1) < counts_smem[0, group]
+        fill((left_ref, mid_ref, right_ref)[group % 3], pl.ds(group // 3 * CAP, CAP), pl.ds(group * CAP, CAP), live)
 
 
 def pack(counts, cells, fractions, adjoint_pos, adjoint_vel):
+    field = pltpu.VMEM(fractions.shape, f32)
     side = jax.ShapeDtypeStruct((8, 3 * CAP), f32)
     return pl.pallas_call(
         pack_kernel,
-        out_shape=(side, side, side, jax.ShapeDtypeStruct((N_SLAB, 128), f32)),
-        in_specs=[SMEM] + [VMEM] * 5,
+        out_shape=(jax.ShapeDtypeStruct((N_PENCIL, 8, 128), f32), side, side, side),
+        in_specs=[SMEM] + [HBM] * 5,
         out_specs=(VMEM,) * 4,
-        scratch_shapes=[pltpu.VMEM((8, TAILS), f32), pltpu.VMEM((TAILS, 8), f32)],
-        compiler_params=PARAMS,
+        scratch_shapes=[
+            pltpu.VMEM(counts.shape, jnp.int32),
+            pltpu.VMEM(cells.shape, jnp.int32),
+            field,
+            field,
+            field,
+            pltpu.VMEM((8, TAILS), f32),
+            pltpu.VMEM((TAILS, 8), f32),
+            pltpu.VMEM((N_SLAB, 128), f32),
+            pltpu.SemaphoreType.DMA((5,)),
+        ],
+        compiler_params=WIDE,
         name="pack",
     )(counts, counts, cells, fractions, adjoint_pos, adjoint_vel)
 
 
-def repack_kernel(in_ref, out_ref):
+def repack_kernel(in_ref, out_ref, flat):
     for p in range(N_PENCIL):
         for k in range(8):
-            out_ref[p, :, 16 * k : 16 * k + 16] = in_ref[8 * k : 8 * k + 8, 16 * p : 16 * p + 16]
+            flat[8 * k : 8 * k + 8, 16 * p : 16 * p + 16] = in_ref[p, :, 16 * k : 16 * k + 16]
+    out_ref[pl.ds(0, N_SLAB, stride=2), :] = flat[...]
+    out_ref[pl.ds(1, N_SLAB, stride=2), :] = jnp.concatenate([flat[N_SLAB - 1 :], flat[: N_SLAB - 1]], axis=0)
 
 
 def repack(tail):
     return pl.pallas_call(
         repack_kernel,
-        out_shape=jax.ShapeDtypeStruct((N_PENCIL, 8, 128), f32),
+        out_shape=jax.ShapeDtypeStruct((2 * N_SLAB, 128), f32),
         in_specs=[VMEM],
         out_specs=VMEM,
+        scratch_shapes=[pltpu.VMEM((N_SLAB, 128), f32)],
         compiler_params=PARAMS,
         name="repack",
     )(tail)
 
 
-def paint(values, acc_ref):
+def paint(values, acc_ref, below=None, spill=False):
     slots = values.shape[1]
     cell = values[0:1].astype(jnp.int32)
     row = lax.shift_right_logical(cell, 13) * STRIDE + (lax.shift_right_logical(cell, 8) & 31)
+    if spill:
+        row = row - MAIN
+    if below is not None:
+        row = row - below
     base_z = cell & 255
     next_z = (base_z + 1) & 255
     frac_x, frac_y, frac_z = values[1:2], values[2:3], values[3:4]
     rest_x, rest_y, rest_z = 1.0 - frac_x, 1.0 - frac_y, 1.0 - frac_z
-
-    def rounded(value):
-        return value.astype(bf16).astype(f32)
-
-    row_ids = lax.broadcasted_iota(jnp.int32, (PAINT_ROWS, slots), 0)
-    corner = jnp.where(row_ids == row, rounded(rest_x * rest_y), 0.0)
-    corner = jnp.where(row_ids == row + 1, rounded(rest_x * frac_y), corner)
-    corner = jnp.where(row_ids == row + STRIDE, rounded(frac_x * rest_y), corner)
-    corner = jnp.where(row_ids == row + STRIDE + 1, rounded(frac_x * frac_y), corner).astype(bf16)
-    z_ids = lax.broadcasted_iota(jnp.int32, (NG, slots), 0)
-    at_low, at_high = z_ids == base_z, z_ids == next_z
+    zero = jnp.zeros((), bf16)
+
+    def short(value):
+        return value.astype(f32).astype(bf16)
+
+    count = 48 if spill else MAIN
+    row_ids = short(lax.broadcasted_iota(jnp.int32, (count, slots), 0))
+    corner = jnp.where(row_ids == short(row + STRIDE), short(frac_x * rest_y), zero)
+    corner = jnp.where(row_ids == short(row + STRIDE + 1), short(frac_x * frac_y), corner)
+    if not spill:
+        corner = jnp.where(row_ids == short(row), short(rest_x * rest_y), corner)
+        corner = jnp.where(row_ids == short(row + 1), short(rest_x * frac_y), corner)
+    z_ids = short(lax.broadcasted_iota(jnp.int32, (NG, slots), 0))
+    at_low, at_high = z_ids == short(base_z), z_ids == short(next_z)
     for i in range(3):
         weight = values[4 + i : 5 + i]
-        line = jnp.where(at_low, rounded(weight * rest_z), 0.0)
-        line = jnp.where(at_high, rounded(weight * frac_z), line).astype(bf16)
-        acc_ref[:, i * NG : (i + 1) * NG] += lax.dot_general(
+        line = jnp.where(at_low, short(weight * rest_z), zero)
+        line = jnp.where(at_high, short(weight * frac_z), line)
+        acc_ref[:count, i * NG : (i + 1) * NG] += lax.dot_general(
             corner, line, (((1,), (1,)), ((), ())), preferred_element_type=f32
         )
 
 
-def near_kernel(down_ref, left_ref, mid_ref, right_ref, up_ref, out_ref):
+def near_kernel(below2_ref, below_ref, left_ref, mid_ref, right_ref, above_ref, out_ref):
     out_ref[...] = jnp.zeros_like(out_ref)
     for ref in (left_ref, mid_ref, right_ref):
         paint(ref[:, CAP : 2 * CAP], out_ref)
+        paint(ref[:, :CAP], out_ref, spill=True)
 
     def body(step, carry):
-        at = pl.ds(pl.multiple_of(step * CAP, CAP), CAP)
-        paint(down_ref[:, at], out_ref)
-        paint(up_ref[:, at], out_ref)
+        at = pl.multiple_of(step * CAP, CAP)
+        paint(above_ref[:, pl.ds(at, CAP)], out_ref)
+        paint(below2_ref[:, pl.ds(at, CAP)], out_ref, spill=True)
+        paint(below_ref[:, pl.ds(2 * at, CAP)], out_ref, spill=True)
+        paint(below_ref[:, pl.ds(2 * at + CAP, CAP)], out_ref)
         return carry
 
     lax.fori_loop(0, 3, body, 0)
 
 
-def paint_near(down, left, mid, right, up):
+def paint_near(below2, below, left, mid, right, above):
     return pl.pallas_call(
         near_kernel,
-        out_shape=jax.ShapeDtypeStruct((PAINT_ROWS, 3 * NG), f32),
-        in_specs=[VMEM] * 5,
-        out_specs=VMEM,
-        compiler_params=PARAMS,
-        cost_estimate=pl.CostEstimate(flops=2 * NEAR * PAINT_ROWS * 3 * NG, bytes_accessed=2_000_000, transcendentals=0),
+        out_shape=jax.ShapeDtypeStruct((MAIN, 3 * NG), f32),
+        in_specs=[VMEM] * 6,
+        out_specs=VMEM,
+        compiler_params=PARAMS,
+        cost_estimate=pl.CostEstimate(flops=4 * NEAR * MAIN * 3 * NG, bytes_accessed=2_000_000, transcendentals=0),
         name="paint_near",
-    )(down, left, mid, right, up)
-
-
-def tail_kernel(tail_ref, near_ref, main_ref, spill_ref, values, acc):
+    )(below2, below, left, mid, right, above)
+
+
+def tail_kernel(tail_ref, near_ref, out_ref, values):
     turned = tail_ref[...].T
     for k in range(16):
-        values[:, 64 * k : 64 * k + 64] = turned[8 * k : 8 * k + 8, :]
-    acc[...] = near_ref[...]
-    for half in range(2):
-        paint(values[:, half * 512 : half * 512 + 512], acc)
-    main_ref[...] = acc[:MAIN]
-    spill_ref[...] = acc[MAIN:]
+        values[:, 128 * k : 128 * k + 128] = turned[8 * k : 8 * k + 8, :]
+    out_ref[...] = near_ref[...]
+    below = lax.broadcasted_iota(jnp.int32, (1, CAP), 1) % 2 * MAIN
+
+    def body(step, carry):
+        for half in range(2):
+            at = pl.ds(pl.multiple_of((2 * step + half) * CAP, CAP), CAP)
+            paint(values[:, at], out_ref, below)
+        return carry
+
+    lax.fori_loop(0, 2, body, 0)
 
 
 def paint_tail(tail, near):
     return pl.pallas_call(
         tail_kernel,
-        out_shape=(jax.ShapeDtypeStruct((MAIN, 3 * NG), f32), jax.ShapeDtypeStruct((STRIDE, 3 * NG), f32)),
+        out_shape=jax.ShapeDtypeStruct((MAIN, 3 * NG), f32),
         in_specs=[VMEM] * 2,
-        out_specs=(VMEM,) * 2,
-        scratch_shapes=[pltpu.VMEM((8, TAILS), f32), pltpu.VMEM((PAINT_ROWS, 3 * NG), f32)],
+        out_specs=VMEM,
+        scratch_shapes=[pltpu.VMEM((8, 2 * TAILS), f32)],
         compiler_params=PARAMS,
         name="paint_tail",
     )(tail, near)
 
 
-def z_kernel(main_ref, spill_ref, plain_high, plain_low, scaled_high, scaled_low, out_ref):
+def z_kernel(main_ref, plain_high, plain_low, scaled_high, scaled_low, out_ref):
     for i in range(3):
-        columns = pl.ds(i * NG, NG)
-        data = jnp.concatenate(
-            [main_ref[:STRIDE, columns] + spill_ref[:, columns], main_ref[STRIDE:, columns]], axis=0
-        )
+        data = main_ref[:, i * NG : (i + 1) * NG]
         high = data.astype(bf16)
         low = (data - high.astype(f32)).astype(bf16)
         table_high, table_low = (scaled_high, scaled_low) if i == 2 else (plain_high, plain_low)
@@ -233,15 +275,15 @@
     out_ref[:, 6 * CY + 6 :, :] = jnp.zeros((N_PENCIL, 2, 128), f32)
 
 
-def transform_z(main, spill, plain, scaled):
+def transform_z(main, plain, scaled):
     return pl.pallas_call(
         z_kernel,
         out_shape=jax.ShapeDtypeStruct((N_PENCIL, CHUNK, 128), f32),
-        in_specs=[VMEM] * 6,
+        in_specs=[VMEM] * 5,
         out_specs=VMEM,
         compiler_params=PARAMS,
         name="transform_z",
-    )(main, spill, *plain, *scaled)
+    )(main, *plain, *scaled)
 
 
 def mixed_rhs(real, imag):
@@ -314,21 +356,19 @@
 
 def local(cells, fractions, adjoint_pos, adjoint_vel, counts):
     plain, scaled, table_y, table_x = [tuple(jnp.asarray(t) for t in pair) for pair in host_tables()]
-    to_below, own, to_above, tail = pack(counts, cells, fractions, adjoint_pos, adjoint_vel)
-    tail = lax.all_to_all(tail.reshape(N_SLAB, 1, 128), "slab", 0, 0, tiled=True)
-    from_above = shifted(to_below, "slab", -1)
-    from_below = shifted(to_above, "slab", 1)
-    tail = repack(tail.reshape(N_SLAB, 128))
-    tail = lax.all_to_all(tail, "pencil", 0, 0, tiled=True)
-    bands = (from_above, own, from_below)
-    to_left = jnp.concatenate([band[:, :CAP] for band in bands], axis=1)
-    to_right = jnp.concatenate([band[:, 2 * CAP :] for band in bands], axis=1)
+    arrays = (counts, cells, fractions, adjoint_pos, adjoint_vel)
+    tail, to_left, mid, to_right = pack(*arrays)
     from_right = shifted(to_left, "pencil", -1)
     from_left = shifted(to_right, "pencil", 1)
-    near = paint_near(from_left, from_above, own, from_below, from_right)
-    main, spill = paint_tail(tail.reshape(N_SLAB, 128), near)
-    spill = shifted(spill, "slab", 1)
-    by_rows = transform_z(main, spill, plain, scaled)
+    columns = (from_left, mid, from_right)
+    from_below2 = shifted(jnp.concatenate([column[:, 2 * CAP :] for column in columns], axis=1), "slab", 2)
+    from_below = shifted(jnp.concatenate([column[:, CAP:] for column in columns], axis=1), "slab", 1)
+    from_above = shifted(jnp.concatenate([column[:, :CAP] for column in columns], axis=1), "slab", -1)
+    tail = lax.all_to_all(tail, "pencil", 0, 0, tiled=True)
+    tail = lax.all_to_all(repack(tail).reshape(N_SLAB, 2, 128), "slab", 0, 0, tiled=True)
+    near = paint_near(from_below2, from_below, *columns, from_above)
+    main = paint_tail(tail.reshape(2 * N_SLAB, 128), near)
+    by_rows = transform_z(main, plain, scaled)
     by_rows = lax.all_to_all(by_rows, "pencil", 0, 0, tiled=True)
     by_cols = transform_y(by_rows, table_y)
     by_cols = lax.all_to_all(by_cols.reshape(N_SLAB, 16, 128), "slab", 0, 0, tiled=True)

time: 131 us -> 119 us (0.908)
  waiting for transfers between devices: 50.8 us -> 41.9 us
  local copies, waits for them, and re-layouts: 4.12 us -> 0.81 us
    ppermute x5, waiting for transfers between devices: 5.13 us -> 0.01 us  [shifted(): return lax.ppermute(block, axis, route)]
    unnamed x26 -> x22, local copies, waits for them, and re-layouts: 4.11 us -> 0.05 us
    all_to_all x1, waiting for transfers between devices: 12.6 us -> 9.12 us  [local(): lax.all_to_all(repack(tail).reshape(N_SLAB, 2, 128), 'slab', 0, 0, tiled=...]
    all_to_all x1, starting transfers between devices: 8.8 us -> 6.15 us  [local(): lax.all_to_all(by_cols.reshape(N_SLAB, 16, 128), 'slab', 0, 0, tiled=True)]
    ppermute x5, starting transfers between devices: 13.2 us -> 15.1 us  [shifted(): return lax.ppermute(block, axis, route)]
  transfers between devices with their start and end apart: 8 -> 8, of which waited for: 3 -> 2; matrix products, arithmetic and copies ran while one was open for 0% -> 0% of each run, Pallas kernels for 5% -> 5%
where the time goes in v1:
time: 119 us; the launch traced here: 118 us
  starting transfers between devices  41.9 us (35%)
  waiting for transfers between devices  41.9 us (35%)
  blocking collectives  18.2 us (15%)
  Pallas kernels  15.3 us (13%)
    all_to_all x1, waiting for transfers between devices, local(): lax.all_to_all(by_cols.reshape(N_SLAB, 16, 128), 'slab', 0, 0, tiled=True)  32.7 us
    all_to_all x1, blocking collectives, local(): by_rows = lax.all_to_all(by_rows, 'pencil', 0, 0, tiled=True)  18.2 us
    all_to_all x1, starting transfers between devices, local(): lax.all_to_all(repack(tail).reshape(N_SLAB, 2, 128), 'slab', 0, 0, tiled=...  17.2 us
    ppermute x5, starting transfers between devices, shifted(): return lax.ppermute(block, axis, route)  15.1 us
    all_to_all x1, waiting for transfers between devices, local(): lax.all_to_all(repack(tail).reshape(N_SLAB, 2, 128), 'slab', 0, 0, tiled=...  9.12 us
    all_to_all x1, starting transfers between devices, local(): lax.all_to_all(by_cols.reshape(N_SLAB, 16, 128), 'slab', 0, 0, tiled=True)  6.15 us
    pallas_call x1, Pallas kernels, paint_near(): pl.pallas_call(near_kernel, out_shape=jax.ShapeDtypeStruct((MAIN, 3 * NG)...  5.03 us
    all_to_all x1, starting transfers between devices, local(): tail = lax.all_to_all(tail, 'pencil', 0, 0, tiled=True)  3.33 us
  transfers between devices with their start and end apart: 8, of which 2 were waited for; matrix products, arithmetic and copies ran while one was open for 0% of the time, Pallas kernels for 5%

profile of v1, /device:TPU:8, one launch (start us, length us, event | category | flops | bytes accessed | tf_op | source)
XLA Modules:
  0.0 118.4 jit_solution(11590867466252530847)
XLA Ops:
  0.0 3.1 %pack.1 = (f32[8,8,128]{2,1,0:T(8,128)}, f32[8,1536]{1,0:T(8,128)}, f32[8,1536]{1,0:T(8,128)}, f32[8,1536]{1,0:T(8,128)}) custom-call(s32[1,521]{1,0:T(1,128)} %counts_hbm.1, s32[1,521]{1,0:T(1,128)} %counts_hbm.1, s32[1,5632]{1,0:T(1,128)} %cells_hbm.1, f32[3,1,5632]{2,1,0:T(1,128)} %frac_hbm.1, f32[3,1,5632]{2,1,0:T(1,128)} %pos_hbm.1, f32[3,1,5632]{2,1,0:T(1,128)} %vel_hbm.1), custom_call_target="tpu_custom_call" | custom-call | tf_op jit(solution)/shard_map/pack/pallas_call | solution.py:125
  3.1 0.0 collective-permute-start
  3.2 2.9 %collective-permute-start.1 = (f32[8,1536]{1,0:T(8,128)}, f32[8,1536]{1,0:T(8,128)S(1)}, u32[]{:S(2)}, u32[]{:S(2)}) collective-permute-start(f32[8,1536]{1,0:T(8,128)} %get-tuple-element.12), channel_id=1, source_target_pairs={{1,0},{2,1},{3,2},{4,3},{5,4},{6,5},{7,6},{0,7},{9,8},{10,9},{11,1... | collective-permute-start | bytes 147464 | tf_op jit(solution)/shard_map/ppermute | solution.py:67
  6.1 3.3 %all-to-all-start = ((f32[8,8,128]{2,1,0:T(8,128)}), f32[8,8,128]{2,1,0:T(8,128)S(1)}, u32[]{:S(2)}, u32[]{:S(2)}) async-start(f32[8,8,128]{2,1,0:T(8,128)} %get-tuple-element.9), calls=%async_computation | async-start | bytes 65536 | tf_op jit(solution)/shard_map/all_to_all | solution.py:367
  9.5 0.0 collective-permute-done.left_ref
  9.5 7.8 %collective-permute-start.4 = (f32[8,1536]{1,0:T(8,128)S(1)}, f32[8,1536]{1,0:T(8,128)S(1)}, u32[]{:S(2)}, u32[]{:S(2)}) collective-permute-start(f32[8,1536]{1,0:T(8,128)S(1)} %pad_maximum_fusion.2), channel_id=1, source_target_pairs={{8,0},{16,8},{24,16},{32,24},{40,32},{48,40},{56,48},{64,56},{72,6... | collective-permute-start | bytes 147464 | tf_op jit(solution)/shard_map/ppermute | solution.py:67
  17.3 0.0 slice-start
  17.4 0.7 slice-done
  18.1 1.9 %collective-permute-start.3 = (f32[8,3072]{1,0:T(8,128)S(1)}, f32[8,3072]{1,0:T(8,128)S(1)}, u32[]{:S(2)}, u32[]{:S(2)}) collective-permute-start(f32[8,3072]{1,0:T(8,128)S(1)} %pad_maximum_fusion), channel_id=1, source_target_pairs={{504,0},{0,8},{8,16},{16,24},{24,32},{32,40},{40,48},{48,56},{56,6... | collective-permute-start | bytes 294920 | tf_op jit(solution)/shard_map/ppermute | solution.py:67
  20.0 2.5 %collective-permute-start.2 = (f32[8,1536]{1,0:T(8,128)S(1)}, f32[8,1536]{1,0:T(8,128)S(1)}, u32[]{:S(2)}, u32[]{:S(2)}) collective-permute-start(f32[8,1536]{1,0:T(8,128)S(1)} %pad_maximum_fusion.1), channel_id=1, source_target_pairs={{496,0},{504,8},{0,16},{8,24},{16,32},{24,40},{32,48},{40,56},{48,... | collective-permute-start | bytes 147464 | tf_op jit(solution)/shard_map/ppermute | solution.py:67
  22.6 0.8 repack.1
  23.3 17.2 %all-to-all-start.1 = ((f32[64,2,128]{2,1,0:T(2,128)}), f32[64,2,128]{2,1,0:T(2,128)S(1)}, u32[]{:S(2)}, u32[]{:S(2)}) async-start(f32[64,2,128]{2,1,0:T(2,128)} %bitcast.2), calls=%async_computation.1 | async-start | bytes 131072 | tf_op jit(solution)/shard_map/all_to_all | solution.py:368
  40.6 5.0 %paint_near.1.near_ref = f32[160,768]{1,0:T(8,128)S(1)} custom-call(f32[8,1536]{1,0:T(8,128)S(1)} %collective-permute-done.2.below2_ref, f32[8,3072]{1,0:T(8,128)S(1)} %collective-permute-done.3.below_ref, f32[8,1536]{1,0:T(8,128)S(1)} %copy-done.10, f32[8,1536]{1,0:T(8,128)S(1)} %copy-done.8, f32[8,1536]{1,0:T(8,128)S(1)} %collective-permute-done.1.right_ref, ...), custom_call_target="tpu_custom_call" | custom-call | flops 2264924160 | bytes 2000000 | tf_op jit(solution)/shard_map/paint_near/pallas_call | solution.py:219
  45.6 9.1 %all-to-all-done.1 = f32[64,2,128]{2,1,0:T(2,128)S(1)} async-done(((f32[64,2,128]{2,1,0:T(2,128)}), f32[64,2,128]{2,1,0:T(2,128)S(1)}, u32[]{:S(2)}, u32[]{:S(2)}) %all-to-all-start.1) | async-done | bytes 65568 | tf_op jit(solution)/shard_map/all_to_all | solution.py:368
  54.8 1.5 %paint_tail.1.main_ref = f32[160,768]{1,0:T(8,128)S(1)} custom-call(f32[128,128]{1,0:T(8,128)S(1)} %bitcast.8, f32[160,768]{1,0:T(8,128)S(1)} %paint_near.1.near_ref), custom_call_target="tpu_custom_call" | custom-call | tf_op jit(solution)/shard_map/paint_tail/pallas_call | solution.py:247
  56.3 1.1 transform_z.1
  57.4 0.0 copy-start.2
  57.4 0.0 copy-start.3
  57.5 18.2 %all_to_all.20.in_ref = f32[8,200,128]{2,1,0:T(8,128)S(1)} all-to-all(f32[8,200,128]{2,1,0:T(8,128)S(1)} %transform_z.1), channel_id=1, replica_groups=mesh['slab'=64,'pencil'=8] {'pencil'}, dimensions={0} | all-to-all | bytes 1638400 | tf_op jit(solution)/shard_map/all_to_all | solution.py:372
  75.7 1.9 %transform_y.1 = f32[1024,128]{1,0:T(8,128)} custom-call(f32[8,200,128]{2,1,0:T(8,128)S(1)} %all_to_all.20.in_ref, bf16[256,1024]{1,0:T(8,128)(2,1)S(1)} %copy-done.2, bf16[256,1024]{1,0:T(8,128)(2,1)S(1)} %copy-done.3), custom_call_target="tpu_custom_call" | custom-call | tf_op jit(solution)/shard_map/transform_y/pallas_call | solution.py:318
  77.5 6.1 %all-to-all-start.3 = ((f32[64,16,128]{2,1,0:T(8,128)}), f32[64,16,128]{2,1,0:T(8,128)S(1)}, u32[]{:S(2)}, u32[]{:S(2)}) async-start(f32[64,16,128]{2,1,0:T(8,128)} %bitcast.4), calls=%async_computation.3 | async-start | bytes 1048576 | tf_op jit(solution)/shard_map/all_to_all | solution.py:374
  83.7 0.1 pad_add_fusion.place_ref
  83.8 32.7 %all-to-all-done.3 = f32[64,16,128]{2,1,0:T(8,128)S(1)} async-done(((f32[64,16,128]{2,1,0:T(8,128)}), f32[64,16,128]{2,1,0:T(8,128)S(1)}, u32[]{:S(2)}, u32[]{:S(2)}) %all-to-all-start.3) | async-done | bytes 524320 | tf_op jit(solution)/shard_map/all_to_all | solution.py:374
  116.5 1.9 %transform_x.1 = f32[2,128,256]{2,1,0:T(8,128)} custom-call(s32[2]{0:T(128)S(1)} %pad_add_fusion.place_ref, f32[1024,128]{1,0:T(8,128)S(1)} %bitcast.7, bf16[256,1024]{1,0:T(8,128)(2,1)S(1)} %copy-done, bf16[256,1024]{1,0:T(8,128)(2,1)S(1)} %copy-done.1), custom_call_target="tpu_custom_call" | custom-call | tf_op jit(solution)/shard_map/transform_x/pallas_call | solution.py:347
  (33 shorter events, 0.1 us)
Async XLA Ops:
  3.1 6.3 %copy-start.8 = (f32[8,1536]{1,0:T(8,128)S(1)}, f32[8,1536]{1,0:T(8,128)}, u32[]{:S(2)}) copy-start(f32[8,1536]{1,0:T(8,128)} %get-tuple-element.11.mid_ref) | copy-start | bytes 147460
  3.1 6.3 %collective-permute-start = (f32[8,1536]{1,0:T(8,128)}, f32[8,1536]{1,0:T(8,128)S(1)}, u32[]{:S(2)}, u32[]{:S(2)}) collective-permute-start(f32[8,1536]{1,0:T(8,128)} %get-tuple-element.10), channel_id=1, source_target_pairs={{7,0},{0,1},{1,2},{2,3},{3,4},{4,5},{5,6},{6,7},{15,8},{8,9},{9,10... | collective-permute-start | bytes 147464 | tf_op jit(solution)/shard_map/ppermute | solution.py:67
  3.2 6.4 %collective-permute-start.1 = (f32[8,1536]{1,0:T(8,128)}, f32[8,1536]{1,0:T(8,128)S(1)}, u32[]{:S(2)}, u32[]{:S(2)}) collective-permute-start(f32[8,1536]{1,0:T(8,128)} %get-tuple-element.12), channel_id=1, source_target_pairs={{1,0},{2,1},{3,2},{4,3},{5,4},{6,5},{7,6},{0,7},{9,8},{10,9},{11,1... | collective-permute-start | bytes 147464 | tf_op jit(solution)/shard_map/ppermute | solution.py:67
  6.1 16.4 %all-to-all-start = ((f32[8,8,128]{2,1,0:T(8,128)}), f32[8,8,128]{2,1,0:T(8,128)S(1)}, u32[]{:S(2)}, u32[]{:S(2)}) async-start(f32[8,8,128]{2,1,0:T(8,128)} %get-tuple-element.9), calls=%async_computation | async-start | bytes 65536 | tf_op jit(solution)/shard_map/all_to_all | solution.py:367
  9.5 7.8 %copy-start.9 = (f32[8,1536]{1,0:T(8,128)}, f32[8,1536]{1,0:T(8,128)S(1)}, u32[]{:S(2)}) copy-start(f32[8,1536]{1,0:T(8,128)S(1)} %collective-permute-done.left_ref) | copy-start | bytes 147460
  9.5 31.0 %collective-permute-start.4 = (f32[8,1536]{1,0:T(8,128)S(1)}, f32[8,1536]{1,0:T(8,128)S(1)}, u32[]{:S(2)}, u32[]{:S(2)}) collective-permute-start(f32[8,1536]{1,0:T(8,128)S(1)} %pad_maximum_fusion.2), channel_id=1, source_target_pairs={{8,0},{16,8},{24,16},{32,24},{40,32},{48,40},{56,48},{64,56},{72,6... | collective-permute-start | bytes 147464 | tf_op jit(solution)/shard_map/ppermute | solution.py:67
  17.3 0.8 slice-start
  18.1 22.5 %collective-permute-start.3 = (f32[8,3072]{1,0:T(8,128)S(1)}, f32[8,3072]{1,0:T(8,128)S(1)}, u32[]{:S(2)}, u32[]{:S(2)}) collective-permute-start(f32[8,3072]{1,0:T(8,128)S(1)} %pad_maximum_fusion), channel_id=1, source_target_pairs={{504,0},{0,8},{8,16},{16,24},{24,32},{32,40},{40,48},{48,56},{56,6... | collective-permute-start | bytes 294920 | tf_op jit(solution)/shard_map/ppermute | solution.py:67
  20.0 20.6 %collective-permute-start.2 = (f32[8,1536]{1,0:T(8,128)S(1)}, f32[8,1536]{1,0:T(8,128)S(1)}, u32[]{:S(2)}, u32[]{:S(2)}) collective-permute-start(f32[8,1536]{1,0:T(8,128)S(1)} %pad_maximum_fusion.1), channel_id=1, source_target_pairs={{496,0},{504,8},{0,16},{8,24},{16,32},{24,40},{32,48},{40,56},{48,... | collective-permute-start | bytes 147464 | tf_op jit(solution)/shard_map/ppermute | solution.py:67
  23.3 17.3 %copy-start.10 = (f32[8,1536]{1,0:T(8,128)S(1)}, f32[8,1536]{1,0:T(8,128)}, u32[]{:S(2)}) copy-start(f32[8,1536]{1,0:T(8,128)} %copy-done.9) | copy-start | bytes 147460
  23.3 31.4 %all-to-all-start.1 = ((f32[64,2,128]{2,1,0:T(2,128)}), f32[64,2,128]{2,1,0:T(2,128)S(1)}, u32[]{:S(2)}, u32[]{:S(2)}) async-start(f32[64,2,128]{2,1,0:T(2,128)} %bitcast.2), calls=%async_computation.1 | async-start | bytes 131072 | tf_op jit(solution)/shard_map/all_to_all | solution.py:368
  54.8 1.5 %copy-start.4 = (bf16[256,512]{1,0:T(8,128)(2,1)S(1)}, bf16[256,512]{1,0:T(8,128)(2,1)}, u32[]{:S(2)}) copy-start(bf16[256,512]{1,0:T(8,128)(2,1)} %constant.25.clone.plain_high) | copy-start | bytes 786436
  54.8 1.5 %copy-start.5 = (bf16[256,512]{1,0:T(8,128)(2,1)S(1)}, bf16[256,512]{1,0:T(8,128)(2,1)}, u32[]{:S(2)}) copy-start(bf16[256,512]{1,0:T(8,128)(2,1)} %constant.26.clone.plain_low) | copy-start | bytes 786436
  54.8 1.5 %copy-start.6 = (bf16[256,512]{1,0:T(8,128)(2,1)S(1)}, bf16[256,512]{1,0:T(8,128)(2,1)}, u32[]{:S(2)}) copy-start(bf16[256,512]{1,0:T(8,128)(2,1)} %constant.27.clone.scaled_high) | copy-start | bytes 786436
  54.8 1.6 %copy-start.7 = (bf16[256,512]{1,0:T(8,128)(2,1)S(1)}, bf16[256,512]{1,0:T(8,128)(2,1)}, u32[]{:S(2)}) copy-start(bf16[256,512]{1,0:T(8,128)(2,1)} %constant.28.clone.scaled_low) | copy-start | bytes 786436
  57.4 18.2 %copy-start.2 = (bf16[256,1024]{1,0:T(8,128)(2,1)S(1)}, bf16[256,1024]{1,0:T(8,128)(2,1)}, u32[]{:S(2)}) copy-start(bf16[256,1024]{1,0:T(8,128)(2,1)} %constant.29.clone.table_high) | copy-start | bytes 1572868
  57.4 18.2 %copy-start.3 = (bf16[256,1024]{1,0:T(8,128)(2,1)S(1)}, bf16[256,1024]{1,0:T(8,128)(2,1)}, u32[]{:S(2)}) copy-start(bf16[256,1024]{1,0:T(8,128)(2,1)} %constant.30.clone.table_low) | copy-start | bytes 1572868
  77.5 39.0 %copy-start = (bf16[256,1024]{1,0:T(8,128)(2,1)S(1)}, bf16[256,1024]{1,0:T(8,128)(2,1)}, u32[]{:S(2)}) copy-start(bf16[256,1024]{1,0:T(8,128)(2,1)} %constant.31.clone.table_high) | copy-start | bytes 1572868
  77.5 39.0 %copy-start.1 = (bf16[256,1024]{1,0:T(8,128)(2,1)S(1)}, bf16[256,1024]{1,0:T(8,128)(2,1)}, u32[]{:S(2)}) copy-start(bf16[256,1024]{1,0:T(8,128)(2,1)} %constant.32.clone.table_low) | copy-start | bytes 1572868
  77.5 39.0 %all-to-all-start.3 = ((f32[64,16,128]{2,1,0:T(8,128)}), f32[64,16,128]{2,1,0:T(8,128)S(1)}, u32[]{:S(2)}, u32[]{:S(2)}) async-start(f32[64,16,128]{2,1,0:T(8,128)} %bitcast.4), calls=%async_computation.3 | async-start | bytes 1048576 | tf_op jit(solution)/shard_map/all_to_all | solution.py:374

commit v2 on v1

--- a/solution.py
+++ b/solution.py
@@ -61,6 +61,12 @@
     )
 
 
+def swapped(block, first):
+    count = lax.axis_size("slab")
+    pairs = [((i + first) % count, (i + first + 1) % count) for i in range(0, count, 2)]
+    return lax.ppermute(block, "slab", pairs + [(b, a) for a, b in pairs])
+
+
 def shifted(block, axis, distance):
     devices = range(lax.axis_size(axis))
     route = [((i - distance) % len(devices), i) for i in devices]
@@ -90,9 +96,9 @@
     out[7:8, lanes] = jnp.zeros(cells.shape, f32)
 
 
-def pack_kernel(counts_smem, counts_hbm, cells_hbm, frac_hbm, pos_hbm, vel_hbm, tail_ref, left_ref, mid_ref, right_ref, counts_ref, cells_ref, frac_ref, pos_ref, vel_ref, rows, columns, flat, sems):
+def pack_kernel(counts_hbm, cells_hbm, frac_hbm, pos_hbm, vel_hbm, tail_ref, left_ref, mid_ref, right_ref, counts_ref, cells_ref, frac_ref, pos_ref, vel_ref, counts_smem, rows, columns, flat, sems):
     copies = start_copies(
-        [(counts_hbm, counts_ref), (cells_hbm, cells_ref), (frac_hbm, frac_ref), (pos_hbm, pos_ref), (vel_hbm, vel_ref)], sems
+        [(counts_hbm, counts_ref), (counts_hbm, counts_smem), (cells_hbm, cells_ref), (frac_hbm, frac_ref), (pos_hbm, pos_ref), (vel_hbm, vel_ref)], sems
     )
     width = counts_ref.shape[1]
     slot_of = lax.broadcasted_iota(jnp.int32, (width, TAILS), 1)
@@ -125,7 +131,7 @@
     return pl.pallas_call(
         pack_kernel,
         out_shape=(jax.ShapeDtypeStruct((N_PENCIL, 8, 128), f32), side, side, side),
-        in_specs=[SMEM] + [HBM] * 5,
+        in_specs=[HBM] * 5,
         out_specs=(VMEM,) * 4,
         scratch_shapes=[
             pltpu.VMEM(counts.shape, jnp.int32),
@@ -133,17 +139,18 @@
             field,
             field,
             field,
+            pltpu.SMEM(counts.shape, jnp.int32),
             pltpu.VMEM((8, TAILS), f32),
             pltpu.VMEM((TAILS, 8), f32),
             pltpu.VMEM((N_SLAB, 128), f32),
-            pltpu.SemaphoreType.DMA((5,)),
+            pltpu.SemaphoreType.DMA((6,)),
         ],
         compiler_params=WIDE,
         name="pack",
-    )(counts, counts, cells, fractions, adjoint_pos, adjoint_vel)
-
-
-def repack_kernel(in_ref, out_ref, flat):
+    )(counts, cells, fractions, adjoint_pos, adjoint_vel)
+
+
+def repack_kernel(in_ref, after_ref, out_ref, flat):
     for p in range(N_PENCIL):
         for k in range(8):
             flat[8 * k : 8 * k + 8, 16 * p : 16 * p + 16] = in_ref[p, :, 16 * k : 16 * k + 16]
@@ -151,16 +158,17 @@
     out_ref[pl.ds(1, N_SLAB, stride=2), :] = jnp.concatenate([flat[N_SLAB - 1 :], flat[: N_SLAB - 1]], axis=0)
 
 
-def repack(tail):
+def repack(tail, after):
     return pl.pallas_call(
         repack_kernel,
         out_shape=jax.ShapeDtypeStruct((2 * N_SLAB, 128), f32),
-        in_specs=[VMEM],
+        in_specs=[VMEM, ANY],
         out_specs=VMEM,
         scratch_shapes=[pltpu.VMEM((N_SLAB, 128), f32)],
         compiler_params=PARAMS,
+        cost_estimate=pl.CostEstimate(flops=3000000000, bytes_accessed=200_000, transcendentals=0),
         name="repack",
-    )(tail)
+    )(tail, after)
 
 
 def paint(values, acc_ref, below=None, spill=False):
@@ -198,66 +206,56 @@
         )
 
 
-def near_kernel(below2_ref, below_ref, left_ref, mid_ref, right_ref, above_ref, out_ref):
+def near_kernel(held_ref, inner_ref, outer_ref, below2_ref, out_ref):
     out_ref[...] = jnp.zeros_like(out_ref)
-    for ref in (left_ref, mid_ref, right_ref):
-        paint(ref[:, CAP : 2 * CAP], out_ref)
-        paint(ref[:, :CAP], out_ref, spill=True)
+    even = lax.axis_index("slab") % 2 == 0
 
     def body(step, carry):
-        at = pl.multiple_of(step * CAP, CAP)
-        paint(above_ref[:, pl.ds(at, CAP)], out_ref)
-        paint(below2_ref[:, pl.ds(at, CAP)], out_ref, spill=True)
-        paint(below_ref[:, pl.ds(2 * at, CAP)], out_ref, spill=True)
-        paint(below_ref[:, pl.ds(2 * at + CAP, CAP)], out_ref)
+        def group(ref, index):
+            return ref[:, pl.ds(pl.multiple_of((3 * step + index) * CAP, CAP), CAP)]
+
+        def pick(first, then, index):
+            return jnp.where(even, group(first, index), group(then, index))
+
+        paint(group(held_ref, 1), out_ref)
+        paint(group(held_ref, 0), out_ref, spill=True)
+        paint(pick(inner_ref, outer_ref, 0), out_ref)
+        paint(pick(outer_ref, inner_ref, 2), out_ref)
+        paint(pick(outer_ref, inner_ref, 1), out_ref, spill=True)
+        paint(group(below2_ref, 2), out_ref, spill=True)
         return carry
 
     lax.fori_loop(0, 3, body, 0)
 
 
-def paint_near(below2, below, left, mid, right, above):
+def paint_near(held, inner, outer, below2):
     return pl.pallas_call(
         near_kernel,
         out_shape=jax.ShapeDtypeStruct((MAIN, 3 * NG), f32),
-        in_specs=[VMEM] * 6,
+        in_specs=[VMEM] * 4,
         out_specs=VMEM,
         compiler_params=PARAMS,
         cost_estimate=pl.CostEstimate(flops=4 * NEAR * MAIN * 3 * NG, bytes_accessed=2_000_000, transcendentals=0),
         name="paint_near",
-    )(below2, below, left, mid, right, above)
-
-
-def tail_kernel(tail_ref, near_ref, out_ref, values):
+    )(held, inner, outer, below2)
+
+
+def tail_kernel(tail_ref, near_ref, plain_high, plain_low, scaled_high, scaled_low, out_ref, values, painted):
     turned = tail_ref[...].T
     for k in range(16):
         values[:, 128 * k : 128 * k + 128] = turned[8 * k : 8 * k + 8, :]
-    out_ref[...] = near_ref[...]
+    painted[...] = near_ref[...]
     below = lax.broadcasted_iota(jnp.int32, (1, CAP), 1) % 2 * MAIN
 
     def body(step, carry):
         for half in range(2):
             at = pl.ds(pl.multiple_of((2 * step + half) * CAP, CAP), CAP)
-            paint(values[:, at], out_ref, below)
+            paint(values[:, at], painted, below)
         return carry
 
     lax.fori_loop(0, 2, body, 0)
-
-
-def paint_tail(tail, near):
-    return pl.pallas_call(
-        tail_kernel,
-        out_shape=jax.ShapeDtypeStruct((MAIN, 3 * NG), f32),
-        in_specs=[VMEM] * 2,
-        out_specs=VMEM,
-        scratch_shapes=[pltpu.VMEM((8, 2 * TAILS), f32)],
-        compiler_params=PARAMS,
-        name="paint_tail",
-    )(tail, near)
-
-
-def z_kernel(main_ref, plain_high, plain_low, scaled_high, scaled_low, out_ref):
     for i in range(3):
-        data = main_ref[:, i * NG : (i + 1) * NG]
+        data = painted[:, i * NG : (i + 1) * NG]
         high = data.astype(bf16)
         low = (data - high.astype(f32)).astype(bf16)
         table_high, table_low = (scaled_high, scaled_low) if i == 2 else (plain_high, plain_low)
@@ -275,15 +273,16 @@
     out_ref[:, 6 * CY + 6 :, :] = jnp.zeros((N_PENCIL, 2, 128), f32)
 
 
-def transform_z(main, plain, scaled):
-    return pl.pallas_call(
-        z_kernel,
+def paint_tail_transform_z(tail, near, plain, scaled):
+    return pl.pallas_call(
+        tail_kernel,
         out_shape=jax.ShapeDtypeStruct((N_PENCIL, CHUNK, 128), f32),
-        in_specs=[VMEM] * 5,
-        out_specs=VMEM,
-        compiler_params=PARAMS,
-        name="transform_z",
-    )(main, *plain, *scaled)
+        in_specs=[VMEM] * 6,
+        out_specs=VMEM,
+        scratch_shapes=[pltpu.VMEM((8, 2 * TAILS), f32), pltpu.VMEM((MAIN, 3 * NG), f32)],
+        compiler_params=PARAMS,
+        name="paint_tail_transform_z",
+    )(tail, near, *plain, *scaled)
 
 
 def mixed_rhs(real, imag):
@@ -329,13 +328,13 @@
     return jnp.where(position < NG // 2, position, position - NG).astype(f32)
 
 
-def x_kernel(place_ref, in_ref, table_high, table_low, out_ref):
+def x_kernel(in_ref, table_high, table_low, out_ref):
     lines = [in_ref[pl.ds(block, NG, stride=4), :] for block in range(4)]
     data = jnp.concatenate([mixed_rhs(lines[0], lines[1]), mixed_rhs(lines[2], lines[3])], axis=0)
     mixed = product(table_high[...], table_low[...], data)
     lane = lax.broadcasted_iota(jnp.int32, (1, 128), 1)
-    wave_y = wavenumber(place_ref[0] * 4 + lane // 32)
-    wave_z = wavenumber(place_ref[1] * 32 + lane % 32)
+    wave_y = wavenumber(lax.axis_index("slab") * 4 + lane // 32)
+    wave_z = wavenumber(lax.axis_index("pencil") * 32 + lane % 32)
     wave_x = wavenumber(lax.broadcasted_iota(jnp.int32, (NG, 1), 0))
     wave_sq = wave_x * wave_x + wave_y * wave_y + wave_z * wave_z
     factor = jnp.where(wave_sq > 0, out_scale / jnp.sqrt(jnp.maximum(wave_sq, 1.0)), 0.0) / NG**1.5
@@ -343,15 +342,15 @@
     out_ref[1] = (mixed[:, :128] * -factor).T
 
 
-def transform_x(place, by_cols, table):
+def transform_x(by_cols, table):
     return pl.pallas_call(
         x_kernel,
         out_shape=jax.ShapeDtypeStruct((2, 128, NG), f32),
-        in_specs=[SMEM] + [VMEM] * 3,
+        in_specs=[VMEM] * 3,
         out_specs=VMEM,
         compiler_params=PARAMS,
         name="transform_x",
-    )(place, by_cols, *table)
+    )(by_cols, *table)
 
 
 def local(cells, fractions, adjoint_pos, adjoint_vel, counts):
@@ -361,19 +360,18 @@
     from_right = shifted(to_left, "pencil", -1)
     from_left = shifted(to_right, "pencil", 1)
     columns = (from_left, mid, from_right)
-    from_below2 = shifted(jnp.concatenate([column[:, 2 * CAP :] for column in columns], axis=1), "slab", 2)
-    from_below = shifted(jnp.concatenate([column[:, CAP:] for column in columns], axis=1), "slab", 1)
-    from_above = shifted(jnp.concatenate([column[:, :CAP] for column in columns], axis=1), "slab", -1)
+    held = jnp.concatenate(columns, axis=1)
+    inner = swapped(held, 0)
+    outer = swapped(held, 1)
+    from_below2 = shifted(held, "slab", 2)
     tail = lax.all_to_all(tail, "pencil", 0, 0, tiled=True)
-    tail = lax.all_to_all(repack(tail).reshape(N_SLAB, 2, 128), "slab", 0, 0, tiled=True)
-    near = paint_near(from_below2, from_below, *columns, from_above)
-    main = paint_tail(tail.reshape(2 * N_SLAB, 128), near)
-    by_rows = transform_z(main, plain, scaled)
+    tail = lax.all_to_all(repack(tail, inner).reshape(N_SLAB, 2, 128), "slab", 0, 0, tiled=True)
+    near = paint_near(held, inner, outer, from_below2)
+    by_rows = paint_tail_transform_z(tail.reshape(2 * N_SLAB, 128), near, plain, scaled)
     by_rows = lax.all_to_all(by_rows, "pencil", 0, 0, tiled=True)
     by_cols = transform_y(by_rows, table_y)
     by_cols = lax.all_to_all(by_cols.reshape(N_SLAB, 16, 128), "slab", 0, 0, tiled=True)
-    place = jnp.stack([lax.axis_index("slab"), lax.axis_index("pencil")]).astype(jnp.int32)
-    result = transform_x(place, by_cols.reshape(N_SLAB * 16, 128), table_x)
+    result = transform_x(by_cols.reshape(N_SLAB * 16, 128), table_x)
     return result.reshape(2, CX, 32, NG)
 
 

time: 119 us -> 118 us (level)
  blocking collectives: 18.2 us -> 57 us
  waiting for transfers between devices: 41.9 us -> 12.8 us
  starting transfers between devices: 41.9 us -> 34.6 us
  Pallas kernels: 15.3 us -> 13.1 us
    all_to_all x0 -> x1, blocking collectives: none -> 38.6 us  [local(): lax.all_to_all(by_cols.reshape(N_SLAB, 16, 128), 'slab', 0, 0, tiled=True)]
    all_to_all x2 -> x1, waiting for transfers between devices: 41.8 us -> 9.18 us  [local(): lax.all_to_all(repack(tail, inner).reshape(N_SLAB, 2, 128), 'slab', 0, 0,...]
    ppermute x5 -> x3, starting transfers between devices: 15.1 us -> 4.86 us  [shifted(): return lax.ppermute(block, axis, route)]
    ppermute x0 -> x2, starting transfers between devices: none -> 9.64 us  [swapped(): return lax.ppermute(block, 'slab', pairs + [(b, a) for a, b in pairs])]
    all_to_all x2 -> x1, starting transfers between devices: 23.4 us -> 16.3 us  [local(): lax.all_to_all(repack(tail, inner).reshape(N_SLAB, 2, 128), 'slab', 0, 0,...]
    ppermute x5 -> x3, waiting for transfers between devices: 0.01 us -> 2.05 us  [shifted(): return lax.ppermute(block, axis, route)]
    all_to_all x1, waiting for transfers between devices: 0.01 us -> 1.6 us  [local(): tail = lax.all_to_all(tail, 'pencil', 0, 0, tiled=True)]
    pallas_call x2 -> x1, Pallas kernels: 2.61 us -> 2.59 us  [paint_tail_transform_z(): pl.pallas_call(tail_kernel, out_shape=jax.ShapeDtypeStruct((N_PENCIL, CHU...]
  transfers between devices with their start and end apart: 8 -> 7, of which waited for: 2 -> 4; matrix products, arithmetic and copies ran while one was open for 0% -> 0% of each run, Pallas kernels for 5% -> 5%
where the time goes in v2:
time: 118 us
  blocking collectives  57 us (48%)
  starting transfers between devices  34.6 us (29%)
  Pallas kernels  13.1 us (11%)
  waiting for transfers between devices  12.8 us (11%)
    all_to_all x1, blocking collectives, local(): lax.all_to_all(by_cols.reshape(N_SLAB, 16, 128), 'slab', 0, 0, tiled=True)  38.6 us
    all_to_all x1, blocking collectives, local(): by_rows = lax.all_to_all(by_rows, 'pencil', 0, 0, tiled=True)  18.4 us
    all_to_all x1, starting transfers between devices, local(): lax.all_to_all(repack(tail, inner).reshape(N_SLAB, 2, 128), 'slab', 0, 0,...  16.3 us
    ppermute x2, starting transfers between devices, swapped(): return lax.ppermute(block, 'slab', pairs + [(b, a) for a, b in pairs])  9.64 us
    all_to_all x1, waiting for transfers between devices, local(): lax.all_to_all(repack(tail, inner).reshape(N_SLAB, 2, 128), 'slab', 0, 0,...  9.18 us
    pallas_call x1, Pallas kernels, paint_near(): pl.pallas_call(near_kernel, out_shape=jax.ShapeDtypeStruct((MAIN, 3 * NG)...  4.87 us
    ppermute x3, starting transfers between devices, shifted(): return lax.ppermute(block, axis, route)  4.86 us
    all_to_all x1, starting transfers between devices, local(): tail = lax.all_to_all(tail, 'pencil', 0, 0, tiled=True)  3.88 us
  transfers between devices with their start and end apart: 7, of which 4 were waited for; matrix products, arithmetic and copies ran while one was open for 0% of the time, Pallas kernels for 5%

profile of v2, /device:TPU:8, one launch (start us, length us, event | category | flops | bytes accessed | tf_op | source)
XLA Modules:
  0.0 117.8 jit_solution(13706247713237897552)
XLA Ops:
  0.0 2.4 %pack.1 = (f32[8,8,128]{2,1,0:T(8,128)}, f32[8,1536]{1,0:T(8,128)}, f32[8,1536]{1,0:T(8,128)}, f32[8,1536]{1,0:T(8,128)}) custom-call(s32[1,521]{1,0:T(1,128)} %counts_hbm.1, s32[1,5632]{1,0:T(1,128)} %cells_hbm.1, f32[3,1,5632]{2,1,0:T(1,128)} %frac_hbm.1, f32[3,1,5632]{2,1,0:T(1,128)} %pos_hbm.1, f32[3,1,5632]{2,1,0:T(1,128)} %vel_hbm.1), custom_call_target="tpu_custom_call" | custom-call | tf_op jit(solution)/shard_map/pack/pallas_call | solution.py:131
  2.4 0.0 collective-permute-start
  2.5 2.9 %collective-permute-start.1 = (f32[8,1536]{1,0:T(8,128)}, f32[8,1536]{1,0:T(8,128)S(1)}, u32[]{:S(2)}, u32[]{:S(2)}) collective-permute-start(f32[8,1536]{1,0:T(8,128)} %get-tuple-element.12), channel_id=1, source_target_pairs={{1,0},{2,1},{3,2},{4,3},{5,4},{6,5},{7,6},{0,7},{9,8},{10,9},{11,1... | collective-permute-start | bytes 147464 | tf_op jit(solution)/shard_map/ppermute | solution.py:73
  5.4 2.0 %collective-permute-done = f32[8,1536]{1,0:T(8,128)S(1)} collective-permute-done((f32[8,1536]{1,0:T(8,128)}, f32[8,1536]{1,0:T(8,128)S(1)}, u32[]{:S(2)}, u32[]{:S(2)}) %collective-permute-start) | collective-permute-done | bytes 49184 | tf_op jit(solution)/shard_map/ppermute | solution.py:73
  7.4 0.1 collective-permute-done.1
  7.5 7.7 %collective-permute-start.2 = (f32[8,4608]{1,0:T(8,128)S(1)}, f32[8,4608]{1,0:T(8,128)S(1)}, u32[]{:S(2)}, u32[]{:S(2)}) collective-permute-start(f32[8,4608]{1,0:T(8,128)S(1)} %constant_dynamic-update-slice_fusion.held_ref), channel_id=1, source_target_pairs={{0,8},{16,24},{32,40},{48,56},{64,72},{80,88},{96,104},{112,120},{... | collective-permute-start | bytes 442376 | tf_op jit(solution)/shard_map/ppermute | solution.py:67
  15.2 3.9 %all-to-all-start = ((f32[8,8,128]{2,1,0:T(8,128)}), f32[8,8,128]{2,1,0:T(8,128)S(1)}, u32[]{:S(2)}, u32[]{:S(2)}) async-start(f32[8,8,128]{2,1,0:T(8,128)} %get-tuple-element.9), calls=%async_computation | async-start | bytes 65536 | tf_op jit(solution)/shard_map/all_to_all | solution.py:367
  19.1 1.9 %collective-permute-start.4 = (f32[8,4608]{1,0:T(8,128)S(1)}, f32[8,4608]{1,0:T(8,128)S(1)}, u32[]{:S(2)}, u32[]{:S(2)}) collective-permute-start(f32[8,4608]{1,0:T(8,128)S(1)} %constant_dynamic-update-slice_fusion.held_ref), channel_id=1, source_target_pairs={{496,0},{504,8},{0,16},{8,24},{16,32},{24,40},{32,48},{40,56},{48,... | collective-permute-start | bytes 442376 | tf_op jit(solution)/shard_map/ppermute | solution.py:73
  21.0 1.9 %collective-permute-start.3 = (f32[8,4608]{1,0:T(8,128)S(1)}, f32[8,4608]{1,0:T(8,128)S(1)}, u32[]{:S(2)}, u32[]{:S(2)}) collective-permute-start(f32[8,4608]{1,0:T(8,128)S(1)} %constant_dynamic-update-slice_fusion.held_ref), channel_id=1, source_target_pairs={{8,16},{24,32},{40,48},{56,64},{72,80},{88,96},{104,112},{120,128}... | collective-permute-start | bytes 442376 | tf_op jit(solution)/shard_map/ppermute | solution.py:67
  22.9 1.6 %all-to-all-done.in_ref = f32[8,8,128]{2,1,0:T(8,128)S(1)} async-done(((f32[8,8,128]{2,1,0:T(8,128)}), f32[8,8,128]{2,1,0:T(8,128)S(1)}, u32[]{:S(2)}, u32[]{:S(2)}) %all-to-all-start) | async-done | bytes 32800 | tf_op jit(solution)/shard_map/all_to_all | solution.py:367
  24.5 0.8 repack.1
  25.3 16.3 %all-to-all-start.1 = ((f32[64,2,128]{2,1,0:T(2,128)}), f32[64,2,128]{2,1,0:T(2,128)S(1)}, u32[]{:S(2)}, u32[]{:S(2)}) async-start(f32[64,2,128]{2,1,0:T(2,128)} %bitcast), calls=%async_computation.1 | async-start | bytes 131072 | tf_op jit(solution)/shard_map/all_to_all | solution.py:368
  41.6 0.0 copy-start.4
  41.6 0.0 copy-start.5
  41.6 0.0 copy-start.6
  41.6 0.0 copy-start.7
  41.7 4.9 %paint_near.1.near_ref = f32[160,768]{1,0:T(8,128)S(1)} custom-call(f32[8,4608]{1,0:T(8,128)S(1)} %constant_dynamic-update-slice_fusion.held_ref, f32[8,4608]{1,0:T(8,128)S(1)} %collective-permute-done.2.after_ref.inner_ref, f32[8,4608]{1,0:T(8,128)S(1)} %collective-permute-done.3.outer_ref, f32[8,4608]{1,0:T(8,128)S(1)} %collective-permute-done.4.below2_ref), custom_call_target="tpu_custom_call" | custom-call | flops 2264924160 | bytes 2000000 | tf_op jit(solution)/shard_map/paint_near/pallas_call | solution.py:232
  46.5 9.2 %all-to-all-done.1 = f32[64,2,128]{2,1,0:T(2,128)S(1)} async-done(((f32[64,2,128]{2,1,0:T(2,128)}), f32[64,2,128]{2,1,0:T(2,128)S(1)}, u32[]{:S(2)}, u32[]{:S(2)}) %all-to-all-start.1) | async-done | bytes 65568 | tf_op jit(solution)/shard_map/all_to_all | solution.py:368
  55.7 2.6 %paint_tail_transform_z.1 = f32[8,200,128]{2,1,0:T(8,128)S(1)} custom-call(f32[128,128]{1,0:T(8,128)S(1)} %bitcast.7, f32[160,768]{1,0:T(8,128)S(1)} %paint_near.1.near_ref, bf16[256,512]{1,0:T(8,128)(2,1)S(1)} %copy-done.7, bf16[256,512]{1,0:T(8,128)(2,1)S(1)} %copy-done.6, bf16[256,512]{1,0:T(8,128)(2,1)S(1)} %copy-done.5, bf16[256,512]{1,0:T(8,128)(2,1)S(1)} %copy-done.4), custom_call_target="tpu_custom_call" | custom-call | tf_op jit(solution)/shard_map/paint_tail_transform_z/pallas_call | solution.py:277
  58.3 0.0 copy-start.2
  58.4 18.4 %all_to_all.20.in_ref = f32[8,200,128]{2,1,0:T(8,128)S(1)} all-to-all(f32[8,200,128]{2,1,0:T(8,128)S(1)} %paint_tail_transform_z.1), channel_id=1, replica_groups=mesh['slab'=64,'pencil'=8] {'pencil'}, dimensions={0} | all-to-all | bytes 1638400 | tf_op jit(solution)/shard_map/all_to_all | solution.py:371
  76.8 1.0 transform_y.1
  77.8 38.6 %all_to_all.21 = f32[64,16,128]{2,1,0:T(8,128)S(1)} all-to-all(f32[64,16,128]{2,1,0:T(8,128)S(1)} %bitcast.6), channel_id=1, replica_groups=mesh['slab'=64,'pencil'=8] {'slab'}, dimensions={0} | all-to-all | bytes 1048576 | tf_op jit(solution)/shard_map/all_to_all | solution.py:373
  116.4 1.4 %transform_x.1 = f32[2,128,256]{2,1,0:T(8,128)} custom-call(f32[1024,128]{1,0:T(8,128)S(1)} %bitcast.5, bf16[256,1024]{1,0:T(8,128)(2,1)S(1)} %copy-done.1, bf16[256,1024]{1,0:T(8,128)(2,1)S(1)} %copy-done), custom_call_target="tpu_custom_call" | custom-call | tf_op jit(solution)/shard_map/transform_x/pallas_call | solution.py:346
  (19 shorter events, 0.1 us)
Async XLA Ops:
  2.4 4.9 %collective-permute-start = (f32[8,1536]{1,0:T(8,128)}, f32[8,1536]{1,0:T(8,128)S(1)}, u32[]{:S(2)}, u32[]{:S(2)}) collective-permute-start(f32[8,1536]{1,0:T(8,128)} %get-tuple-element.10), channel_id=1, source_target_pairs={{7,0},{0,1},{1,2},{2,3},{3,4},{4,5},{5,6},{6,7},{15,8},{8,9},{9,10... | collective-permute-start | bytes 147464 | tf_op jit(solution)/shard_map/ppermute | solution.py:73
  2.5 4.9 %copy-start.8 = (f32[8,1536]{1,0:T(8,128)S(1)}, f32[8,1536]{1,0:T(8,128)}, u32[]{:S(2)}) copy-start(f32[8,1536]{1,0:T(8,128)} %get-tuple-element.11) | copy-start | bytes 147460
  2.5 5.0 %collective-permute-start.1 = (f32[8,1536]{1,0:T(8,128)}, f32[8,1536]{1,0:T(8,128)S(1)}, u32[]{:S(2)}, u32[]{:S(2)}) collective-permute-start(f32[8,1536]{1,0:T(8,128)} %get-tuple-element.12), channel_id=1, source_target_pairs={{1,0},{2,1},{3,2},{4,3},{5,4},{6,5},{7,6},{0,7},{9,8},{10,9},{11,1... | collective-permute-start | bytes 147464 | tf_op jit(solution)/shard_map/ppermute | solution.py:73
  7.5 17.1 %collective-permute-start.2 = (f32[8,4608]{1,0:T(8,128)S(1)}, f32[8,4608]{1,0:T(8,128)S(1)}, u32[]{:S(2)}, u32[]{:S(2)}) collective-permute-start(f32[8,4608]{1,0:T(8,128)S(1)} %constant_dynamic-update-slice_fusion.held_ref), channel_id=1, source_target_pairs={{0,8},{16,24},{32,40},{48,56},{64,72},{80,88},{96,104},{112,120},{... | collective-permute-start | bytes 442376 | tf_op jit(solution)/shard_map/ppermute | solution.py:67
  15.2 9.3 %all-to-all-start = ((f32[8,8,128]{2,1,0:T(8,128)}), f32[8,8,128]{2,1,0:T(8,128)S(1)}, u32[]{:S(2)}, u32[]{:S(2)}) async-start(f32[8,8,128]{2,1,0:T(8,128)} %get-tuple-element.9), calls=%async_computation | async-start | bytes 65536 | tf_op jit(solution)/shard_map/all_to_all | solution.py:367
  19.1 22.5 %collective-permute-start.4 = (f32[8,4608]{1,0:T(8,128)S(1)}, f32[8,4608]{1,0:T(8,128)S(1)}, u32[]{:S(2)}, u32[]{:S(2)}) collective-permute-start(f32[8,4608]{1,0:T(8,128)S(1)} %constant_dynamic-update-slice_fusion.held_ref), channel_id=1, source_target_pairs={{496,0},{504,8},{0,16},{8,24},{16,32},{24,40},{32,48},{40,56},{48,... | collective-permute-start | bytes 442376 | tf_op jit(solution)/shard_map/ppermute | solution.py:73
  21.0 20.6 %collective-permute-start.3 = (f32[8,4608]{1,0:T(8,128)S(1)}, f32[8,4608]{1,0:T(8,128)S(1)}, u32[]{:S(2)}, u32[]{:S(2)}) collective-permute-start(f32[8,4608]{1,0:T(8,128)S(1)} %constant_dynamic-update-slice_fusion.held_ref), channel_id=1, source_target_pairs={{8,16},{24,32},{40,48},{56,64},{72,80},{88,96},{104,112},{120,128}... | collective-permute-start | bytes 442376 | tf_op jit(solution)/shard_map/ppermute | solution.py:67
  25.3 30.4 %all-to-all-start.1 = ((f32[64,2,128]{2,1,0:T(2,128)}), f32[64,2,128]{2,1,0:T(2,128)S(1)}, u32[]{:S(2)}, u32[]{:S(2)}) async-start(f32[64,2,128]{2,1,0:T(2,128)} %bitcast), calls=%async_computation.1 | async-start | bytes 131072 | tf_op jit(solution)/shard_map/all_to_all | solution.py:368
  41.6 14.1 %copy-start.4 = (bf16[256,512]{1,0:T(8,128)(2,1)S(1)}, bf16[256,512]{1,0:T(8,128)(2,1)}, u32[]{:S(2)}) copy-start(bf16[256,512]{1,0:T(8,128)(2,1)} %constant.19.clone.scaled_low) | copy-start | bytes 786436
  41.6 14.1 %copy-start.5 = (bf16[256,512]{1,0:T(8,128)(2,1)S(1)}, bf16[256,512]{1,0:T(8,128)(2,1)}, u32[]{:S(2)}) copy-start(bf16[256,512]{1,0:T(8,128)(2,1)} %constant.18.clone.scaled_high) | copy-start | bytes 786436
  41.6 14.1 %copy-start.6 = (bf16[256,512]{1,0:T(8,128)(2,1)S(1)}, bf16[256,512]{1,0:T(8,128)(2,1)}, u32[]{:S(2)}) copy-start(bf16[256,512]{1,0:T(8,128)(2,1)} %constant.17.clone.plain_low) | copy-start | bytes 786436
  41.6 14.1 %copy-start.7 = (bf16[256,512]{1,0:T(8,128)(2,1)S(1)}, bf16[256,512]{1,0:T(8,128)(2,1)}, u32[]{:S(2)}) copy-start(bf16[256,512]{1,0:T(8,128)(2,1)} %constant.16.clone.plain_high) | copy-start | bytes 786436
  58.3 18.4 %copy-start.2 = (bf16[256,1024]{1,0:T(8,128)(2,1)S(1)}, bf16[256,1024]{1,0:T(8,128)(2,1)}, u32[]{:S(2)}) copy-start(bf16[256,1024]{1,0:T(8,128)(2,1)} %constant.21.clone.table_low) | copy-start | bytes 1572868
  58.3 18.4 %copy-start.3 = (bf16[256,1024]{1,0:T(8,128)(2,1)S(1)}, bf16[256,1024]{1,0:T(8,128)(2,1)}, u32[]{:S(2)}) copy-start(bf16[256,1024]{1,0:T(8,128)(2,1)} %constant.20.clone.table_high) | copy-start | bytes 1572868
  77.8 38.6 %copy-start = (bf16[256,1024]{1,0:T(8,128)(2,1)S(1)}, bf16[256,1024]{1,0:T(8,128)(2,1)}, u32[]{:S(2)}) copy-start(bf16[256,1024]{1,0:T(8,128)(2,1)} %constant.23.clone.table_low) | copy-start | bytes 1572868
  77.8 38.6 %copy-start.1 = (bf16[256,1024]{1,0:T(8,128)(2,1)S(1)}, bf16[256,1024]{1,0:T(8,128)(2,1)}, u32[]{:S(2)}) copy-start(bf16[256,1024]{1,0:T(8,128)(2,1)} %constant.22.clone.table_high) | copy-start | bytes 1572868

commit v3 on v2

--- a/solution.py
+++ b/solution.py
@@ -222,7 +222,7 @@
         paint(pick(inner_ref, outer_ref, 0), out_ref)
         paint(pick(outer_ref, inner_ref, 2), out_ref)
         paint(pick(outer_ref, inner_ref, 1), out_ref, spill=True)
-        paint(group(below2_ref, 2), out_ref, spill=True)
+        paint(below2_ref[:, pl.ds(pl.multiple_of(step * CAP, CAP), CAP)], out_ref, spill=True)
         return carry
 
     lax.fori_loop(0, 3, body, 0)
@@ -235,7 +235,7 @@
         in_specs=[VMEM] * 4,
         out_specs=VMEM,
         compiler_params=PARAMS,
-        cost_estimate=pl.CostEstimate(flops=4 * NEAR * MAIN * 3 * NG, bytes_accessed=2_000_000, transcendentals=0),
+        cost_estimate=pl.CostEstimate(flops=9059696640, bytes_accessed=2_000_000, transcendentals=0),
         name="paint_near",
     )(held, inner, outer, below2)
 
@@ -363,9 +363,9 @@
     held = jnp.concatenate(columns, axis=1)
     inner = swapped(held, 0)
     outer = swapped(held, 1)
-    from_below2 = shifted(held, "slab", 2)
+    from_below2 = shifted(jnp.concatenate([held[:, (3 * c + 2) * CAP : (3 * c + 3) * CAP] for c in range(3)], axis=1), "slab", 2)
     tail = lax.all_to_all(tail, "pencil", 0, 0, tiled=True)
-    tail = lax.all_to_all(repack(tail, inner).reshape(N_SLAB, 2, 128), "slab", 0, 0, tiled=True)
+    tail = lax.all_to_all(repack(tail, from_below2).reshape(N_SLAB, 2, 128), "slab", 0, 0, tiled=True)
     near = paint_near(held, inner, outer, from_below2)
     by_rows = paint_tail_transform_z(tail.reshape(2 * N_SLAB, 128), near, plain, scaled)
     by_rows = lax.all_to_all(by_rows, "pencil", 0, 0, tiled=True)

time: 118 us -> 116 us (0.983)
  waiting for transfers between devices: 12.8 us -> 9.26 us
  starting transfers between devices: 34.6 us -> 36 us
    all_to_all x1, starting transfers between devices: 16.3 us -> 11.5 us  [local(): lax.all_to_all(repack(tail, from_below2).reshape(N_SLAB, 2, 128), 'slab',...]
    ppermute x2, starting transfers between devices: 9.64 us -> 13.9 us  [swapped(): return lax.ppermute(block, 'slab', pairs + [(b, a) for a, b in pairs])]
    ppermute x3, starting transfers between devices: 4.86 us -> 7.19 us  [shifted(): return lax.ppermute(block, axis, route)]
    ppermute x3, waiting for transfers between devices: 2.05 us -> 0.01 us  [shifted(): return lax.ppermute(block, axis, route)]
    all_to_all x1, waiting for transfers between devices: 1.6 us -> 0.01 us  [local(): tail = lax.all_to_all(tail, 'pencil', 0, 0, tiled=True)]
  transfers between devices with their start and end apart: 7 -> 7, of which waited for: 4 -> 1; matrix products, arithmetic and copies ran while one was open for 0% -> 0% of each run, Pallas kernels for 5% -> 5%
where the time goes in v3:
time: 116 us; the launch traced here: 115 us
  blocking collectives  56.8 us (49%)
  starting transfers between devices  36 us (31%)
  Pallas kernels  13.1 us (11%)
  waiting for transfers between devices  9.26 us (8%)
    all_to_all x1, blocking collectives, local(): lax.all_to_all(by_cols.reshape(N_SLAB, 16, 128), 'slab', 0, 0, tiled=True)  38.6 us
    all_to_all x1, blocking collectives, local(): by_rows = lax.all_to_all(by_rows, 'pencil', 0, 0, tiled=True)  18.2 us
    ppermute x2, starting transfers between devices, swapped(): return lax.ppermute(block, 'slab', pairs + [(b, a) for a, b in pairs])  13.9 us
    all_to_all x1, starting transfers between devices, local(): lax.all_to_all(repack(tail, from_below2).reshape(N_SLAB, 2, 128), 'slab',...  11.5 us
    all_to_all x1, waiting for transfers between devices, local(): lax.all_to_all(repack(tail, from_below2).reshape(N_SLAB, 2, 128), 'slab',...  9.24 us
    ppermute x3, starting transfers between devices, shifted(): return lax.ppermute(block, axis, route)  7.19 us
    pallas_call x1, Pallas kernels, paint_near(): pl.pallas_call(near_kernel, out_shape=jax.ShapeDtypeStruct((MAIN, 3 * NG)...  4.87 us
    all_to_all x1, starting transfers between devices, local(): tail = lax.all_to_all(tail, 'pencil', 0, 0, tiled=True)  3.32 us
  transfers between devices with their start and end apart: 7, of which 1 were waited for; matrix products, arithmetic and copies ran while one was open for 0% of the time, Pallas kernels for 5%

profile of v3, /device:TPU:8, one launch (start us, length us, event | category | flops | bytes accessed | tf_op | source)
XLA Modules:
  0.0 115.5 jit_solution(4260069844561081974)
XLA Ops:
  0.0 2.4 %pack.1 = (f32[8,8,128]{2,1,0:T(8,128)}, f32[8,1536]{1,0:T(8,128)}, f32[8,1536]{1,0:T(8,128)}, f32[8,1536]{1,0:T(8,128)}) custom-call(s32[1,521]{1,0:T(1,128)} %counts_hbm.1, s32[1,5632]{1,0:T(1,128)} %cells_hbm.1, f32[3,1,5632]{2,1,0:T(1,128)} %frac_hbm.1, f32[3,1,5632]{2,1,0:T(1,128)} %pos_hbm.1, f32[3,1,5632]{2,1,0:T(1,128)} %vel_hbm.1), custom_call_target="tpu_custom_call" | custom-call | tf_op jit(solution)/shard_map/pack/pallas_call | solution.py:131
  2.5 0.0 collective-permute-start
  2.5 2.9 %collective-permute-start.1 = (f32[8,1536]{1,0:T(8,128)}, f32[8,1536]{1,0:T(8,128)S(1)}, u32[]{:S(2)}, u32[]{:S(2)}) collective-permute-start(f32[8,1536]{1,0:T(8,128)} %get-tuple-element.12), channel_id=1, source_target_pairs={{1,0},{2,1},{3,2},{4,3},{5,4},{6,5},{7,6},{0,7},{9,8},{10,9},{11,1... | collective-permute-start | bytes 147464 | tf_op jit(solution)/shard_map/ppermute | solution.py:73
  5.4 3.3 %all-to-all-start = ((f32[8,8,128]{2,1,0:T(8,128)}), f32[8,8,128]{2,1,0:T(8,128)S(1)}, u32[]{:S(2)}, u32[]{:S(2)}) async-start(f32[8,8,128]{2,1,0:T(8,128)} %get-tuple-element.9), calls=%async_computation | async-start | bytes 65536 | tf_op jit(solution)/shard_map/all_to_all | solution.py:367
  8.8 4.2 %collective-permute-start.2 = (f32[8,1536]{1,0:T(8,128)S(1)}, f32[8,1536]{1,0:T(8,128)S(1)}, u32[]{:S(2)}, u32[]{:S(2)}) collective-permute-start(f32[8,1536]{1,0:T(8,128)S(1)} %pad_maximum_fusion), channel_id=1, source_target_pairs={{496,0},{504,8},{0,16},{8,24},{16,32},{24,40},{32,48},{40,56},{48,... | collective-permute-start | bytes 147464 | tf_op jit(solution)/shard_map/ppermute | solution.py:73
  13.1 2.9 %collective-permute-start.4 = (f32[8,4608]{1,0:T(8,128)S(1)}, f32[8,4608]{1,0:T(8,128)S(1)}, u32[]{:S(2)}, u32[]{:S(2)}) collective-permute-start(f32[8,4608]{1,0:T(8,128)S(1)} %constant_dynamic-update-slice_fusion.held_ref), channel_id=1, source_target_pairs={{8,16},{24,32},{40,48},{56,64},{72,80},{88,96},{104,112},{120,128}... | collective-permute-start | bytes 442376 | tf_op jit(solution)/shard_map/ppermute | solution.py:67
  16.0 11.1 %collective-permute-start.3 = (f32[8,4608]{1,0:T(8,128)S(1)}, f32[8,4608]{1,0:T(8,128)S(1)}, u32[]{:S(2)}, u32[]{:S(2)}) collective-permute-start(f32[8,4608]{1,0:T(8,128)S(1)} %constant_dynamic-update-slice_fusion.held_ref), channel_id=1, source_target_pairs={{0,8},{16,24},{32,40},{48,56},{64,72},{80,88},{96,104},{112,120},{... | collective-permute-start | bytes 442376 | tf_op jit(solution)/shard_map/ppermute | solution.py:67
  27.1 0.8 repack.1
  27.8 11.5 %all-to-all-start.1 = ((f32[64,2,128]{2,1,0:T(2,128)}), f32[64,2,128]{2,1,0:T(2,128)S(1)}, u32[]{:S(2)}, u32[]{:S(2)}) async-start(f32[64,2,128]{2,1,0:T(2,128)} %bitcast), calls=%async_computation.1 | async-start | bytes 131072 | tf_op jit(solution)/shard_map/all_to_all | solution.py:368
  39.4 0.0 copy-start.4
  39.4 0.0 copy-start.5
  39.4 0.0 copy-start.6
  39.4 0.0 copy-start.7
  39.4 4.9 %paint_near.1.near_ref = f32[160,768]{1,0:T(8,128)S(1)} custom-call(f32[8,4608]{1,0:T(8,128)S(1)} %constant_dynamic-update-slice_fusion.held_ref, f32[8,4608]{1,0:T(8,128)S(1)} %collective-permute-done.3.inner_ref, f32[8,4608]{1,0:T(8,128)S(1)} %collective-permute-done.4.outer_ref, f32[8,1536]{1,0:T(8,128)S(1)} %collective-permute-done.2.after_ref.below2_ref), custom_call_target="tpu_custom_call" | custom-call | flops 9059696640 | bytes 2000000 | tf_op jit(solution)/shard_map/paint_near/pallas_call | solution.py:232
  44.3 9.2 %all-to-all-done.1 = f32[64,2,128]{2,1,0:T(2,128)S(1)} async-done(((f32[64,2,128]{2,1,0:T(2,128)}), f32[64,2,128]{2,1,0:T(2,128)S(1)}, u32[]{:S(2)}, u32[]{:S(2)}) %all-to-all-start.1) | async-done | bytes 65568 | tf_op jit(solution)/shard_map/all_to_all | solution.py:368
  53.6 2.6 %paint_tail_transform_z.1 = f32[8,200,128]{2,1,0:T(8,128)S(1)} custom-call(f32[128,128]{1,0:T(8,128)S(1)} %bitcast.7, f32[160,768]{1,0:T(8,128)S(1)} %paint_near.1.near_ref, bf16[256,512]{1,0:T(8,128)(2,1)S(1)} %copy-done.7, bf16[256,512]{1,0:T(8,128)(2,1)S(1)} %copy-done.6, bf16[256,512]{1,0:T(8,128)(2,1)S(1)} %copy-done.5, bf16[256,512]{1,0:T(8,128)(2,1)S(1)} %copy-done.4), custom_call_target="tpu_custom_call" | custom-call | tf_op jit(solution)/shard_map/paint_tail_transform_z/pallas_call | solution.py:277
  56.2 0.0 copy-start.2
  56.2 0.0 copy-start.3
  56.2 18.2 %all_to_all.20.in_ref = f32[8,200,128]{2,1,0:T(8,128)S(1)} all-to-all(f32[8,200,128]{2,1,0:T(8,128)S(1)} %paint_tail_transform_z.1), channel_id=1, replica_groups=mesh['slab'=64,'pencil'=8] {'pencil'}, dimensions={0} | all-to-all | bytes 1638400 | tf_op jit(solution)/shard_map/all_to_all | solution.py:371
  74.4 1.0 transform_y.1
  75.5 0.0 copy-start
  75.5 0.0 copy-start.1
  75.5 38.6 %all_to_all.21 = f32[64,16,128]{2,1,0:T(8,128)S(1)} all-to-all(f32[64,16,128]{2,1,0:T(8,128)S(1)} %bitcast.6), channel_id=1, replica_groups=mesh['slab'=64,'pencil'=8] {'slab'}, dimensions={0} | all-to-all | bytes 1048576 | tf_op jit(solution)/shard_map/all_to_all | solution.py:373
  114.1 1.4 %transform_x.1 = f32[2,128,256]{2,1,0:T(8,128)} custom-call(f32[1024,128]{1,0:T(8,128)S(1)} %bitcast.5, bf16[256,1024]{1,0:T(8,128)(2,1)S(1)} %copy-done.1, bf16[256,1024]{1,0:T(8,128)(2,1)S(1)} %copy-done), custom_call_target="tpu_custom_call" | custom-call | tf_op jit(solution)/shard_map/transform_x/pallas_call | solution.py:346
  (23 shorter events, 0.1 us)
Async XLA Ops:
  2.4 6.3 %copy-start.8 = (f32[8,1536]{1,0:T(8,128)S(1)}, f32[8,1536]{1,0:T(8,128)}, u32[]{:S(2)}) copy-start(f32[8,1536]{1,0:T(8,128)} %get-tuple-element.11) | copy-start | bytes 147460
  2.5 6.3 %collective-permute-start = (f32[8,1536]{1,0:T(8,128)}, f32[8,1536]{1,0:T(8,128)S(1)}, u32[]{:S(2)}, u32[]{:S(2)}) collective-permute-start(f32[8,1536]{1,0:T(8,128)} %get-tuple-element.10), channel_id=1, source_target_pairs={{7,0},{0,1},{1,2},{2,3},{3,4},{4,5},{5,6},{6,7},{15,8},{8,9},{9,10... | collective-permute-start | bytes 147464 | tf_op jit(solution)/shard_map/ppermute | solution.py:73
  2.5 6.3 %collective-permute-start.1 = (f32[8,1536]{1,0:T(8,128)}, f32[8,1536]{1,0:T(8,128)S(1)}, u32[]{:S(2)}, u32[]{:S(2)}) collective-permute-start(f32[8,1536]{1,0:T(8,128)} %get-tuple-element.12), channel_id=1, source_target_pairs={{1,0},{2,1},{3,2},{4,3},{5,4},{6,5},{7,6},{0,7},{9,8},{10,9},{11,1... | collective-permute-start | bytes 147464 | tf_op jit(solution)/shard_map/ppermute | solution.py:73
  5.4 21.6 %all-to-all-start = ((f32[8,8,128]{2,1,0:T(8,128)}), f32[8,8,128]{2,1,0:T(8,128)S(1)}, u32[]{:S(2)}, u32[]{:S(2)}) async-start(f32[8,8,128]{2,1,0:T(8,128)} %get-tuple-element.9), calls=%async_computation | async-start | bytes 65536 | tf_op jit(solution)/shard_map/all_to_all | solution.py:367
  8.8 18.2 %collective-permute-start.2 = (f32[8,1536]{1,0:T(8,128)S(1)}, f32[8,1536]{1,0:T(8,128)S(1)}, u32[]{:S(2)}, u32[]{:S(2)}) collective-permute-start(f32[8,1536]{1,0:T(8,128)S(1)} %pad_maximum_fusion), channel_id=1, source_target_pairs={{496,0},{504,8},{0,16},{8,24},{16,32},{24,40},{32,48},{40,56},{48,... | collective-permute-start | bytes 147464 | tf_op jit(solution)/shard_map/ppermute | solution.py:73
  13.1 26.3 %collective-permute-start.4 = (f32[8,4608]{1,0:T(8,128)S(1)}, f32[8,4608]{1,0:T(8,128)S(1)}, u32[]{:S(2)}, u32[]{:S(2)}) collective-permute-start(f32[8,4608]{1,0:T(8,128)S(1)} %constant_dynamic-update-slice_fusion.held_ref), channel_id=1, source_target_pairs={{8,16},{24,32},{40,48},{56,64},{72,80},{88,96},{104,112},{120,128}... | collective-permute-start | bytes 442376 | tf_op jit(solution)/shard_map/ppermute | solution.py:67
  16.0 23.4 %collective-permute-start.3 = (f32[8,4608]{1,0:T(8,128)S(1)}, f32[8,4608]{1,0:T(8,128)S(1)}, u32[]{:S(2)}, u32[]{:S(2)}) collective-permute-start(f32[8,4608]{1,0:T(8,128)S(1)} %constant_dynamic-update-slice_fusion.held_ref), channel_id=1, source_target_pairs={{0,8},{16,24},{32,40},{48,56},{64,72},{80,88},{96,104},{112,120},{... | collective-permute-start | bytes 442376 | tf_op jit(solution)/shard_map/ppermute | solution.py:67
  27.8 25.7 %all-to-all-start.1 = ((f32[64,2,128]{2,1,0:T(2,128)}), f32[64,2,128]{2,1,0:T(2,128)S(1)}, u32[]{:S(2)}, u32[]{:S(2)}) async-start(f32[64,2,128]{2,1,0:T(2,128)} %bitcast), calls=%async_computation.1 | async-start | bytes 131072 | tf_op jit(solution)/shard_map/all_to_all | solution.py:368
  39.4 14.2 %copy-start.4 = (bf16[256,512]{1,0:T(8,128)(2,1)S(1)}, bf16[256,512]{1,0:T(8,128)(2,1)}, u32[]{:S(2)}) copy-start(bf16[256,512]{1,0:T(8,128)(2,1)} %constant.19.clone.scaled_low) | copy-start | bytes 786436
  39.4 14.2 %copy-start.5 = (bf16[256,512]{1,0:T(8,128)(2,1)S(1)}, bf16[256,512]{1,0:T(8,128)(2,1)}, u32[]{:S(2)}) copy-start(bf16[256,512]{1,0:T(8,128)(2,1)} %constant.18.clone.scaled_high) | copy-start | bytes 786436
  39.4 14.2 %copy-start.6 = (bf16[256,512]{1,0:T(8,128)(2,1)S(1)}, bf16[256,512]{1,0:T(8,128)(2,1)}, u32[]{:S(2)}) copy-start(bf16[256,512]{1,0:T(8,128)(2,1)} %constant.17.clone.plain_low) | copy-start | bytes 786436
  39.4 14.2 %copy-start.7 = (bf16[256,512]{1,0:T(8,128)(2,1)S(1)}, bf16[256,512]{1,0:T(8,128)(2,1)}, u32[]{:S(2)}) copy-start(bf16[256,512]{1,0:T(8,128)(2,1)} %constant.16.clone.plain_high) | copy-start | bytes 786436
  56.2 18.2 %copy-start.2 = (bf16[256,1024]{1,0:T(8,128)(2,1)S(1)}, bf16[256,1024]{1,0:T(8,128)(2,1)}, u32[]{:S(2)}) copy-start(bf16[256,1024]{1,0:T(8,128)(2,1)} %constant.21.clone.table_low) | copy-start | bytes 1572868
  56.2 18.2 %copy-start.3 = (bf16[256,1024]{1,0:T(8,128)(2,1)S(1)}, bf16[256,1024]{1,0:T(8,128)(2,1)}, u32[]{:S(2)}) copy-start(bf16[256,1024]{1,0:T(8,128)(2,1)} %constant.20.clone.table_high) | copy-start | bytes 1572868
  75.5 38.6 %copy-start = (bf16[256,1024]{1,0:T(8,128)(2,1)S(1)}, bf16[256,1024]{1,0:T(8,128)(2,1)}, u32[]{:S(2)}) copy-start(bf16[256,1024]{1,0:T(8,128)(2,1)} %constant.23.clone.table_low) | copy-start | bytes 1572868
  75.5 38.6 %copy-start.1 = (bf16[256,1024]{1,0:T(8,128)(2,1)S(1)}, bf16[256,1024]{1,0:T(8,128)(2,1)}, u32[]{:S(2)}) copy-start(bf16[256,1024]{1,0:T(8,128)(2,1)} %constant.22.clone.table_high) | copy-start | bytes 1572868

commit v4 on v3

--- a/solution.py
+++ b/solution.py
@@ -117,9 +117,8 @@
     columns[...] = rows[...].T
     for k in range(16):
         flat[:, 8 * k : 8 * k + 8] = columns[pl.ds(k, N_SLAB, stride=16), :]
-    for p in range(N_PENCIL):
-        for k in range(8):
-            tail_ref[p, :, 16 * k : 16 * k + 16] = flat[8 * k : 8 * k + 8, 16 * p : 16 * p + 16]
+    tail_ref[pl.ds(0, N_SLAB, stride=2), :] = flat[...]
+    tail_ref[pl.ds(1, N_SLAB, stride=2), :] = jnp.concatenate([flat[N_SLAB - 1 :], flat[: N_SLAB - 1]], axis=0)
     for group in range(9):
         live = lax.broadcasted_iota(jnp.int32, (1, CAP), 1) < counts_smem[0, group]
         fill((left_ref, mid_ref, right_ref)[group % 3], pl.ds(group // 3 * CAP, CAP), pl.ds(group * CAP, CAP), live)
@@ -130,7 +129,7 @@
     side = jax.ShapeDtypeStruct((8, 3 * CAP), f32)
     return pl.pallas_call(
         pack_kernel,
-        out_shape=(jax.ShapeDtypeStruct((N_PENCIL, 8, 128), f32), side, side, side),
+        out_shape=(jax.ShapeDtypeStruct((2 * N_SLAB, 128), f32), side, side, side),
         in_specs=[HBM] * 5,
         out_specs=(VMEM,) * 4,
         scratch_shapes=[
@@ -150,35 +149,32 @@
     )(counts, cells, fractions, adjoint_pos, adjoint_vel)
 
 
-def repack_kernel(in_ref, after_ref, out_ref, flat):
-    for p in range(N_PENCIL):
-        for k in range(8):
-            flat[8 * k : 8 * k + 8, 16 * p : 16 * p + 16] = in_ref[p, :, 16 * k : 16 * k + 16]
-    out_ref[pl.ds(0, N_SLAB, stride=2), :] = flat[...]
-    out_ref[pl.ds(1, N_SLAB, stride=2), :] = jnp.concatenate([flat[N_SLAB - 1 :], flat[: N_SLAB - 1]], axis=0)
+def repack_kernel(in_ref, after_ref, out_ref):
+    for which in range(2):
+        rows = in_ref[pl.ds(which, N_SLAB, stride=2), :]
+        for p in range(N_PENCIL):
+            for k in range(8):
+                out_ref[p, 8 * which : 8 * which + 8, 16 * k : 16 * k + 16] = rows[8 * k : 8 * k + 8, 16 * p : 16 * p + 16]
 
 
 def repack(tail, after):
     return pl.pallas_call(
         repack_kernel,
-        out_shape=jax.ShapeDtypeStruct((2 * N_SLAB, 128), f32),
+        out_shape=jax.ShapeDtypeStruct((N_PENCIL, 16, 128), f32),
         in_specs=[VMEM, ANY],
         out_specs=VMEM,
-        scratch_shapes=[pltpu.VMEM((N_SLAB, 128), f32)],
         compiler_params=PARAMS,
         cost_estimate=pl.CostEstimate(flops=3000000000, bytes_accessed=200_000, transcendentals=0),
         name="repack",
     )(tail, after)
 
 
-def paint(values, acc_ref, below=None, spill=False):
+def paint(values, acc_ref, spill=False):
     slots = values.shape[1]
     cell = values[0:1].astype(jnp.int32)
     row = lax.shift_right_logical(cell, 13) * STRIDE + (lax.shift_right_logical(cell, 8) & 31)
     if spill:
         row = row - MAIN
-    if below is not None:
-        row = row - below
     base_z = cell & 255
     next_z = (base_z + 1) & 255
     frac_x, frac_y, frac_z = values[1:2], values[2:3], values[3:4]
@@ -241,19 +237,15 @@
 
 
 def tail_kernel(tail_ref, near_ref, plain_high, plain_low, scaled_high, scaled_low, out_ref, values, painted):
-    turned = tail_ref[...].T
-    for k in range(16):
-        values[:, 128 * k : 128 * k + 128] = turned[8 * k : 8 * k + 8, :]
+    for which in range(2):
+        turned = tail_ref[:, 8 * which : 8 * which + 8, :].reshape(N_SLAB, 128).T
+        for k in range(0, 16, 2):
+            values[which, :, 64 * k : 64 * k + 128] = jnp.concatenate(
+                [turned[8 * k : 8 * k + 8, :], turned[8 * k + 8 : 8 * k + 16, :]], axis=1
+            )
     painted[...] = near_ref[...]
-    below = lax.broadcasted_iota(jnp.int32, (1, CAP), 1) % 2 * MAIN
-
-    def body(step, carry):
-        for half in range(2):
-            at = pl.ds(pl.multiple_of((2 * step + half) * CAP, CAP), CAP)
-            paint(values[:, at], painted, below)
-        return carry
-
-    lax.fori_loop(0, 2, body, 0)
+    paint(values[0], painted)
+    paint(values[1], painted, spill=True)
     for i in range(3):
         data = painted[:, i * NG : (i + 1) * NG]
         high = data.astype(bf16)
@@ -279,7 +271,7 @@
         out_shape=jax.ShapeDtypeStruct((N_PENCIL, CHUNK, 128), f32),
         in_specs=[VMEM] * 6,
         out_specs=VMEM,
-        scratch_shapes=[pltpu.VMEM((8, 2 * TAILS), f32), pltpu.VMEM((MAIN, 3 * NG), f32)],
+        scratch_shapes=[pltpu.VMEM((2, 8, TAILS), f32), pltpu.VMEM((MAIN, 3 * NG), f32)],
         compiler_params=PARAMS,
         name="paint_tail_transform_z",
     )(tail, near, *plain, *scaled)
@@ -364,10 +356,10 @@
     inner = swapped(held, 0)
     outer = swapped(held, 1)
     from_below2 = shifted(jnp.concatenate([held[:, (3 * c + 2) * CAP : (3 * c + 3) * CAP] for c in range(3)], axis=1), "slab", 2)
-    tail = lax.all_to_all(tail, "pencil", 0, 0, tiled=True)
-    tail = lax.all_to_all(repack(tail, from_below2).reshape(N_SLAB, 2, 128), "slab", 0, 0, tiled=True)
+    tail = lax.all_to_all(tail.reshape(N_SLAB, 2, 128), "slab", 0, 0, tiled=True)
+    tail = lax.all_to_all(repack(tail.reshape(2 * N_SLAB, 128), from_below2), "pencil", 0, 0, tiled=True)
     near = paint_near(held, inner, outer, from_below2)
-    by_rows = paint_tail_transform_z(tail.reshape(2 * N_SLAB, 128), near, plain, scaled)
+    by_rows = paint_tail_transform_z(tail, near, plain, scaled)
     by_rows = lax.all_to_all(by_rows, "pencil", 0, 0, tiled=True)
     by_cols = transform_y(by_rows, table_y)
     by_cols = lax.all_to_all(by_cols.reshape(N_SLAB, 16, 128), "slab", 0, 0, tiled=True)

time: 116 us -> 116 us (level)
  waiting for transfers between devices: 9.26 us -> 2.24 us
  blocking collectives: 56.8 us -> 62.4 us
  starting transfers between devices: 36 us -> 37.7 us
    all_to_all x2, starting transfers between devices: 14.8 us -> 22.2 us  [the longest x1 18.9 us: local(): lax.all_to_all(tail.reshape(N_SLAB, 2, 128), 'slab', 0, 0, tiled=True)]
    all_to_all x2, waiting for transfers between devices: 9.25 us -> 2.23 us  [the longest x1 1.63 us: local(): lax.all_to_all(tail.reshape(N_SLAB, 2, 128), 'slab', 0, 0, tiled=True)]
    all_to_all x1, blocking collectives: 38.6 us -> 44.7 us  [local(): lax.all_to_all(by_cols.reshape(N_SLAB, 16, 128), 'slab', 0, 0, tiled=True)]
    ppermute x2, starting transfers between devices: 13.9 us -> 8.56 us  [swapped(): return lax.ppermute(block, 'slab', pairs + [(b, a) for a, b in pairs])]
  transfers between devices with their start and end apart: 7 -> 7, of which waited for: 1 -> 2; matrix products, arithmetic and copies ran while one was open for 0% -> 0% of each run, Pallas kernels for 5% -> 5%
where the time goes in v4:
time: 116 us; the launch traced here: 115 us
  blocking collectives  62.4 us (54%)
  starting transfers between devices  37.7 us (33%)
  Pallas kernels  12.8 us (11%)
  waiting for transfers between devices  2.24 us (2%)
    all_to_all x1, blocking collectives, local(): lax.all_to_all(by_cols.reshape(N_SLAB, 16, 128), 'slab', 0, 0, tiled=True)  44.7 us
    all_to_all x1, starting transfers between devices, local(): lax.all_to_all(tail.reshape(N_SLAB, 2, 128), 'slab', 0, 0, tiled=True)  18.9 us
    all_to_all x1, blocking collectives, local(): by_rows = lax.all_to_all(by_rows, 'pencil', 0, 0, tiled=True)  17.7 us
    ppermute x2, starting transfers between devices, swapped(): return lax.ppermute(block, 'slab', pairs + [(b, a) for a, b in pairs])  8.56 us
    ppermute x3, starting transfers between devices, shifted(): return lax.ppermute(block, axis, route)  6.94 us
    pallas_call x1, Pallas kernels, paint_near(): pl.pallas_call(near_kernel, out_shape=jax.ShapeDtypeStruct((MAIN, 3 * NG)...  4.87 us
    all_to_all x1, starting transfers between devices, local(): lax.all_to_all(repack(tail.reshape(2 * N_SLAB, 128), from_below2), 'penci...  3.35 us
    pallas_call x1, Pallas kernels, paint_tail_transform_z(): pl.pallas_call(tail_kernel, out_shape=jax.ShapeDtypeStruct((N_PENCIL, CHU...  2.38 us
  transfers between devices with their start and end apart: 7, of which 2 were waited for; matrix products, arithmetic and copies ran while one was open for 0% of the time, Pallas kernels for 5%

profile of v4, /device:TPU:8, one launch (start us, length us, event | category | flops | bytes accessed | tf_op | source)
XLA Modules:
  0.0 115.5 jit_solution(11401260082508290089)
XLA Ops:
  0.0 2.3 %pack.1 = (f32[128,128]{1,0:T(8,128)}, f32[8,1536]{1,0:T(8,128)}, f32[8,1536]{1,0:T(8,128)}, f32[8,1536]{1,0:T(8,128)}) custom-call(s32[1,521]{1,0:T(1,128)} %counts_hbm.1, s32[1,5632]{1,0:T(1,128)} %cells_hbm.1, f32[3,1,5632]{2,1,0:T(1,128)} %frac_hbm.1, f32[3,1,5632]{2,1,0:T(1,128)} %pos_hbm.1, f32[3,1,5632]{2,1,0:T(1,128)} %vel_hbm.1), custom_call_target="tpu_custom_call" | custom-call | tf_op jit(solution)/shard_map/pack/pallas_call | solution.py:130
  2.3 0.0 collective-permute-start
  2.4 2.9 %collective-permute-start.1 = (f32[8,1536]{1,0:T(8,128)}, f32[8,1536]{1,0:T(8,128)S(1)}, u32[]{:S(2)}, u32[]{:S(2)}) collective-permute-start(f32[8,1536]{1,0:T(8,128)} %get-tuple-element.12), channel_id=1, source_target_pairs={{1,0},{2,1},{3,2},{4,3},{5,4},{6,5},{7,6},{0,7},{9,8},{10,9},{11,1... | collective-permute-start | bytes 147464 | tf_op jit(solution)/shard_map/ppermute | solution.py:73
  5.3 18.9 %all-to-all-start = ((f32[64,2,128]{2,1,0:T(2,128)}), f32[64,2,128]{2,1,0:T(2,128)S(1)}, u32[]{:S(2)}, u32[]{:S(2)}) async-start(f32[64,2,128]{2,1,0:T(2,128)} %bitcast.8), calls=%async_computation | async-start | bytes 131072 | tf_op jit(solution)/shard_map/all_to_all | solution.py:359
  24.3 4.0 %collective-permute-start.2 = (f32[8,1536]{1,0:T(8,128)S(1)}, f32[8,1536]{1,0:T(8,128)S(1)}, u32[]{:S(2)}, u32[]{:S(2)}) collective-permute-start(f32[8,1536]{1,0:T(8,128)S(1)} %pad_maximum_fusion), channel_id=1, source_target_pairs={{496,0},{504,8},{0,16},{8,24},{16,32},{24,40},{32,48},{40,56},{48,... | collective-permute-start | bytes 147464 | tf_op jit(solution)/shard_map/ppermute | solution.py:73
  28.3 2.8 %collective-permute-start.4 = (f32[8,4608]{1,0:T(8,128)S(1)}, f32[8,4608]{1,0:T(8,128)S(1)}, u32[]{:S(2)}, u32[]{:S(2)}) collective-permute-start(f32[8,4608]{1,0:T(8,128)S(1)} %constant_dynamic-update-slice_fusion.held_ref), channel_id=1, source_target_pairs={{8,16},{24,32},{40,48},{56,64},{72,80},{88,96},{104,112},{120,128}... | collective-permute-start | bytes 442376 | tf_op jit(solution)/shard_map/ppermute | solution.py:67
  31.1 5.8 %collective-permute-start.3 = (f32[8,4608]{1,0:T(8,128)S(1)}, f32[8,4608]{1,0:T(8,128)S(1)}, u32[]{:S(2)}, u32[]{:S(2)}) collective-permute-start(f32[8,4608]{1,0:T(8,128)S(1)} %constant_dynamic-update-slice_fusion.held_ref), channel_id=1, source_target_pairs={{0,8},{16,24},{32,40},{48,56},{64,72},{80,88},{96,104},{112,120},{... | collective-permute-start | bytes 442376 | tf_op jit(solution)/shard_map/ppermute | solution.py:67
  36.9 1.6 %all-to-all-done = f32[64,2,128]{2,1,0:T(2,128)S(1)} async-done(((f32[64,2,128]{2,1,0:T(2,128)}), f32[64,2,128]{2,1,0:T(2,128)S(1)}, u32[]{:S(2)}, u32[]{:S(2)}) %all-to-all-start) | async-done | bytes 65568 | tf_op jit(solution)/shard_map/all_to_all | solution.py:359
  38.5 0.8 repack.1
  39.3 3.4 %all-to-all-start.1 = ((f32[8,16,128]{2,1,0:T(8,128)}), f32[8,16,128]{2,1,0:T(8,128)S(1)}, u32[]{:S(2)}, u32[]{:S(2)}) async-start(f32[8,16,128]{2,1,0:T(8,128)} %repack.1), calls=%async_computation.1 | async-start | bytes 131072 | tf_op jit(solution)/shard_map/all_to_all | solution.py:360
  42.7 0.0 copy-start.4
  42.7 0.0 copy-start.5
  42.7 0.0 copy-start.6
  42.7 0.0 copy-start.7
  42.7 4.9 %paint_near.1.near_ref = f32[160,768]{1,0:T(8,128)S(1)} custom-call(f32[8,4608]{1,0:T(8,128)S(1)} %constant_dynamic-update-slice_fusion.held_ref, f32[8,4608]{1,0:T(8,128)S(1)} %collective-permute-done.3.inner_ref, f32[8,4608]{1,0:T(8,128)S(1)} %collective-permute-done.4.outer_ref, f32[8,1536]{1,0:T(8,128)S(1)} %collective-permute-done.2.after_ref.below2_ref), custom_call_target="tpu_custom_call" | custom-call | flops 9059696640 | bytes 2000000 | tf_op jit(solution)/shard_map/paint_near/pallas_call | solution.py:228
  47.6 0.6 all-to-all-done.1.tail_ref
  48.2 2.4 %paint_tail_transform_z.1 = f32[8,200,128]{2,1,0:T(8,128)S(1)} custom-call(f32[8,16,128]{2,1,0:T(8,128)S(1)} %all-to-all-done.1.tail_ref, f32[160,768]{1,0:T(8,128)S(1)} %paint_near.1.near_ref, bf16[256,512]{1,0:T(8,128)(2,1)S(1)} %copy-done.7, bf16[256,512]{1,0:T(8,128)(2,1)S(1)} %copy-done.6, bf16[256,512]{1,0:T(8,128)(2,1)S(1)} %copy-done.5, ...), custom_call_target="tpu_custom_call" | custom-call | tf_op jit(solution)/shard_map/paint_tail_transform_z/pallas_call | solution.py:269
  50.6 0.0 copy-start.2
  50.6 0.0 copy-start.3
  50.6 17.7 %all_to_all.20.in_ref = f32[8,200,128]{2,1,0:T(8,128)S(1)} all-to-all(f32[8,200,128]{2,1,0:T(8,128)S(1)} %paint_tail_transform_z.1), channel_id=1, replica_groups=mesh['slab'=64,'pencil'=8] {'pencil'}, dimensions={0} | all-to-all | bytes 1638400 | tf_op jit(solution)/shard_map/all_to_all | solution.py:363
  68.3 1.0 transform_y.1
  69.4 0.0 copy-start
  69.4 44.7 %all_to_all.21 = f32[64,16,128]{2,1,0:T(8,128)S(1)} all-to-all(f32[64,16,128]{2,1,0:T(8,128)S(1)} %bitcast.6), channel_id=1, replica_groups=mesh['slab'=64,'pencil'=8] {'slab'}, dimensions={0} | all-to-all | bytes 1048576 | tf_op jit(solution)/shard_map/all_to_all | solution.py:365
  114.1 1.4 %transform_x.1 = f32[2,128,256]{2,1,0:T(8,128)} custom-call(f32[1024,128]{1,0:T(8,128)S(1)} %bitcast.5, bf16[256,1024]{1,0:T(8,128)(2,1)S(1)} %copy-done.1, bf16[256,1024]{1,0:T(8,128)(2,1)S(1)} %copy-done), custom_call_target="tpu_custom_call" | custom-call | tf_op jit(solution)/shard_map/transform_x/pallas_call | solution.py:338
  (23 shorter events, 0.1 us)
Async XLA Ops:
  2.3 21.9 %collective-permute-start = (f32[8,1536]{1,0:T(8,128)}, f32[8,1536]{1,0:T(8,128)S(1)}, u32[]{:S(2)}, u32[]{:S(2)}) collective-permute-start(f32[8,1536]{1,0:T(8,128)} %get-tuple-element.10), channel_id=1, source_target_pairs={{7,0},{0,1},{1,2},{2,3},{3,4},{4,5},{5,6},{6,7},{15,8},{8,9},{9,10... | collective-permute-start | bytes 147464 | tf_op jit(solution)/shard_map/ppermute | solution.py:73
  2.4 21.9 %collective-permute-start.1 = (f32[8,1536]{1,0:T(8,128)}, f32[8,1536]{1,0:T(8,128)S(1)}, u32[]{:S(2)}, u32[]{:S(2)}) collective-permute-start(f32[8,1536]{1,0:T(8,128)} %get-tuple-element.12), channel_id=1, source_target_pairs={{1,0},{2,1},{3,2},{4,3},{5,4},{6,5},{7,6},{0,7},{9,8},{10,9},{11,1... | collective-permute-start | bytes 147464 | tf_op jit(solution)/shard_map/ppermute | solution.py:73
  5.3 18.9 %copy-start.8 = (f32[8,1536]{1,0:T(8,128)S(1)}, f32[8,1536]{1,0:T(8,128)}, u32[]{:S(2)}) copy-start(f32[8,1536]{1,0:T(8,128)} %get-tuple-element.11) | copy-start | bytes 147460
  5.3 33.2 %all-to-all-start = ((f32[64,2,128]{2,1,0:T(2,128)}), f32[64,2,128]{2,1,0:T(2,128)S(1)}, u32[]{:S(2)}, u32[]{:S(2)}) async-start(f32[64,2,128]{2,1,0:T(2,128)} %bitcast.8), calls=%async_computation | async-start | bytes 131072 | tf_op jit(solution)/shard_map/all_to_all | solution.py:359
  24.3 12.6 %collective-permute-start.2 = (f32[8,1536]{1,0:T(8,128)S(1)}, f32[8,1536]{1,0:T(8,128)S(1)}, u32[]{:S(2)}, u32[]{:S(2)}) collective-permute-start(f32[8,1536]{1,0:T(8,128)S(1)} %pad_maximum_fusion), channel_id=1, source_target_pairs={{496,0},{504,8},{0,16},{8,24},{16,32},{24,40},{32,48},{40,56},{48,... | collective-permute-start | bytes 147464 | tf_op jit(solution)/shard_map/ppermute | solution.py:73
  28.3 14.4 %collective-permute-start.4 = (f32[8,4608]{1,0:T(8,128)S(1)}, f32[8,4608]{1,0:T(8,128)S(1)}, u32[]{:S(2)}, u32[]{:S(2)}) collective-permute-start(f32[8,4608]{1,0:T(8,128)S(1)} %constant_dynamic-update-slice_fusion.held_ref), channel_id=1, source_target_pairs={{8,16},{24,32},{40,48},{56,64},{72,80},{88,96},{104,112},{120,128}... | collective-permute-start | bytes 442376 | tf_op jit(solution)/shard_map/ppermute | solution.py:67
  31.1 11.7 %collective-permute-start.3 = (f32[8,4608]{1,0:T(8,128)S(1)}, f32[8,4608]{1,0:T(8,128)S(1)}, u32[]{:S(2)}, u32[]{:S(2)}) collective-permute-start(f32[8,4608]{1,0:T(8,128)S(1)} %constant_dynamic-update-slice_fusion.held_ref), channel_id=1, source_target_pairs={{0,8},{16,24},{32,40},{48,56},{64,72},{80,88},{96,104},{112,120},{... | collective-permute-start | bytes 442376 | tf_op jit(solution)/shard_map/ppermute | solution.py:67
  39.3 8.9 %all-to-all-start.1 = ((f32[8,16,128]{2,1,0:T(8,128)}), f32[8,16,128]{2,1,0:T(8,128)S(1)}, u32[]{:S(2)}, u32[]{:S(2)}) async-start(f32[8,16,128]{2,1,0:T(8,128)} %repack.1), calls=%async_computation.1 | async-start | bytes 131072 | tf_op jit(solution)/shard_map/all_to_all | solution.py:360
  42.7 5.5 %copy-start.4 = (bf16[256,512]{1,0:T(8,128)(2,1)S(1)}, bf16[256,512]{1,0:T(8,128)(2,1)}, u32[]{:S(2)}) copy-start(bf16[256,512]{1,0:T(8,128)(2,1)} %constant.19.clone.scaled_low) | copy-start | bytes 786436
  42.7 5.5 %copy-start.5 = (bf16[256,512]{1,0:T(8,128)(2,1)S(1)}, bf16[256,512]{1,0:T(8,128)(2,1)}, u32[]{:S(2)}) copy-start(bf16[256,512]{1,0:T(8,128)(2,1)} %constant.18.clone.scaled_high) | copy-start | bytes 786436
  42.7 5.5 %copy-start.6 = (bf16[256,512]{1,0:T(8,128)(2,1)S(1)}, bf16[256,512]{1,0:T(8,128)(2,1)}, u32[]{:S(2)}) copy-start(bf16[256,512]{1,0:T(8,128)(2,1)} %constant.17.clone.plain_low) | copy-start | bytes 786436
  42.7 5.5 %copy-start.7 = (bf16[256,512]{1,0:T(8,128)(2,1)S(1)}, bf16[256,512]{1,0:T(8,128)(2,1)}, u32[]{:S(2)}) copy-start(bf16[256,512]{1,0:T(8,128)(2,1)} %constant.16.clone.plain_high) | copy-start | bytes 786436
  50.6 17.7 %copy-start.2 = (bf16[256,1024]{1,0:T(8,128)(2,1)S(1)}, bf16[256,1024]{1,0:T(8,128)(2,1)}, u32[]{:S(2)}) copy-start(bf16[256,1024]{1,0:T(8,128)(2,1)} %constant.21.clone.table_low) | copy-start | bytes 1572868
  50.6 17.7 %copy-start.3 = (bf16[256,1024]{1,0:T(8,128)(2,1)S(1)}, bf16[256,1024]{1,0:T(8,128)(2,1)}, u32[]{:S(2)}) copy-start(bf16[256,1024]{1,0:T(8,128)(2,1)} %constant.20.clone.table_high) | copy-start | bytes 1572868
  69.4 44.7 %copy-start = (bf16[256,1024]{1,0:T(8,128)(2,1)S(1)}, bf16[256,1024]{1,0:T(8,128)(2,1)}, u32[]{:S(2)}) copy-start(bf16[256,1024]{1,0:T(8,128)(2,1)} %constant.23.clone.table_low) | copy-start | bytes 1572868
  69.4 44.7 %copy-start.1 = (bf16[256,1024]{1,0:T(8,128)(2,1)S(1)}, bf16[256,1024]{1,0:T(8,128)(2,1)}, u32[]{:S(2)}) copy-start(bf16[256,1024]{1,0:T(8,128)(2,1)} %constant.22.clone.table_high) | copy-start | bytes 1572868

commit v5 on v4

--- a/solution.py
+++ b/solution.py
@@ -202,8 +202,27 @@
         )
 
 
-def near_kernel(held_ref, inner_ref, outer_ref, below2_ref, out_ref):
+def held_kernel(held_ref, after_ref, out_ref):
     out_ref[...] = jnp.zeros_like(out_ref)
+    for step in range(3):
+        paint(held_ref[:, (3 * step + 1) * CAP : (3 * step + 2) * CAP], out_ref)
+        paint(held_ref[:, 3 * step * CAP : (3 * step + 1) * CAP], out_ref, spill=True)
+
+
+def paint_held(held, after):
+    return pl.pallas_call(
+        held_kernel,
+        out_shape=jax.ShapeDtypeStruct((MAIN, 3 * NG), f32),
+        in_specs=[VMEM, ANY],
+        out_specs=VMEM,
+        compiler_params=PARAMS,
+        cost_estimate=pl.CostEstimate(flops=1_000_000_000, bytes_accessed=1_000_000, transcendentals=0),
+        name="paint_held",
+    )(held, after)
+
+
+def near_kernel(first_ref, inner_ref, outer_ref, below2_ref, out_ref):
+    out_ref[...] = first_ref[...]
     even = lax.axis_index("slab") % 2 == 0
 
     def body(step, carry):
@@ -213,8 +232,6 @@
         def pick(first, then, index):
             return jnp.where(even, group(first, index), group(then, index))
 
-        paint(group(held_ref, 1), out_ref)
-        paint(group(held_ref, 0), out_ref, spill=True)
         paint(pick(inner_ref, outer_ref, 0), out_ref)
         paint(pick(outer_ref, inner_ref, 2), out_ref)
         paint(pick(outer_ref, inner_ref, 1), out_ref, spill=True)
@@ -224,16 +241,16 @@
     lax.fori_loop(0, 3, body, 0)
 
 
-def paint_near(held, inner, outer, below2):
+def paint_near(first, inner, outer, below2):
     return pl.pallas_call(
         near_kernel,
         out_shape=jax.ShapeDtypeStruct((MAIN, 3 * NG), f32),
         in_specs=[VMEM] * 4,
         out_specs=VMEM,
         compiler_params=PARAMS,
-        cost_estimate=pl.CostEstimate(flops=9059696640, bytes_accessed=2_000_000, transcendentals=0),
+        cost_estimate=pl.CostEstimate(flops=4 * NEAR * MAIN * 3 * NG, bytes_accessed=2_000_000, transcendentals=0),
         name="paint_near",
-    )(held, inner, outer, below2)
+    )(first, inner, outer, below2)
 
 
 def tail_kernel(tail_ref, near_ref, plain_high, plain_low, scaled_high, scaled_low, out_ref, values, painted):
@@ -357,8 +374,9 @@
     outer = swapped(held, 1)
     from_below2 = shifted(jnp.concatenate([held[:, (3 * c + 2) * CAP : (3 * c + 3) * CAP] for c in range(3)], axis=1), "slab", 2)
     tail = lax.all_to_all(tail.reshape(N_SLAB, 2, 128), "slab", 0, 0, tiled=True)
-    tail = lax.all_to_all(repack(tail.reshape(2 * N_SLAB, 128), from_below2), "pencil", 0, 0, tiled=True)
-    near = paint_near(held, inner, outer, from_below2)
+    first = paint_held(held, from_below2)
+    tail = lax.all_to_all(repack(tail.reshape(2 * N_SLAB, 128), first), "pencil", 0, 0, tiled=True)
+    near = paint_near(first, inner, outer, from_below2)
     by_rows = paint_tail_transform_z(tail, near, plain, scaled)
     by_rows = lax.all_to_all(by_rows, "pencil", 0, 0, tiled=True)
     by_cols = transform_y(by_rows, table_y)

time: 116 us -> 116 us (level)
    all_to_all x1, waiting for transfers between devices: 1.63 us -> 0.04 us  [local(): lax.all_to_all(tail.reshape(N_SLAB, 2, 128), 'slab', 0, 0, tiled=True)]
    all_to_all x1, blocking collectives: 44.7 us -> 46.3 us  [local(): lax.all_to_all(by_cols.reshape(N_SLAB, 16, 128), 'slab', 0, 0, tiled=True)]
    pallas_call x0 -> x1, Pallas kernels: none -> 1.58 us  [paint_held(): pl.pallas_call(held_kernel, out_shape=jax.ShapeDtypeStruct((MAIN, 3 * NG)...]
    pallas_call x1, Pallas kernels: 4.87 us -> 3.53 us  [paint_near(): pl.pallas_call(near_kernel, out_shape=jax.ShapeDtypeStruct((MAIN, 3 * NG)...]
    all_to_all x1, waiting for transfers between devices: 0.59 us -> 1.94 us  [local(): lax.all_to_all(repack(tail.reshape(2 * N_SLAB, 128), first), 'pencil', 0,...]
    all_to_all x1, blocking collectives: 17.7 us -> 16.3 us  [local(): by_rows = lax.all_to_all(by_rows, 'pencil', 0, 0, tiled=True)]
  transfers between devices with their start and end apart: 7 -> 7, of which waited for: 2 -> 1; matrix products, arithmetic and copies ran while one was open for 0% -> 0% of each run, Pallas kernels for 5% -> 5%
where the time goes in v5:
time: 116 us
  blocking collectives  62.6 us (54%)
  starting transfers between devices  37.7 us (33%)
  Pallas kernels  13.1 us (11%)
  waiting for transfers between devices  1.99 us (2%)
    all_to_all x1, blocking collectives, local(): lax.all_to_all(by_cols.reshape(N_SLAB, 16, 128), 'slab', 0, 0, tiled=True)  46.3 us
    all_to_all x1, starting transfers between devices, local(): lax.all_to_all(tail.reshape(N_SLAB, 2, 128), 'slab', 0, 0, tiled=True)  18.9 us
    all_to_all x1, blocking collectives, local(): by_rows = lax.all_to_all(by_rows, 'pencil', 0, 0, tiled=True)  16.3 us
    ppermute x2, starting transfers between devices, swapped(): return lax.ppermute(block, 'slab', pairs + [(b, a) for a, b in pairs])  8.56 us
    ppermute x3, starting transfers between devices, shifted(): return lax.ppermute(block, axis, route)  6.94 us
    pallas_call x1, Pallas kernels, paint_near(): pl.pallas_call(near_kernel, out_shape=jax.ShapeDtypeStruct((MAIN, 3 * NG)...  3.53 us
    all_to_all x1, starting transfers between devices, local(): lax.all_to_all(repack(tail.reshape(2 * N_SLAB, 128), first), 'pencil', 0,...  3.35 us
    pallas_call x1, Pallas kernels, paint_tail_transform_z(): pl.pallas_call(tail_kernel, out_shape=jax.ShapeDtypeStruct((N_PENCIL, CHU...  2.38 us
  transfers between devices with their start and end apart: 7, of which 1 were waited for; matrix products, arithmetic and copies ran while one was open for 0% of the time, Pallas kernels for 5%

profile of v5, /device:TPU:8, one launch (start us, length us, event | category | flops | bytes accessed | tf_op | source)
XLA Modules:
  0.0 115.7 jit_solution(13654066453912650377)
XLA Ops:
  0.0 2.3 %pack.1 = (f32[128,128]{1,0:T(8,128)}, f32[8,1536]{1,0:T(8,128)}, f32[8,1536]{1,0:T(8,128)}, f32[8,1536]{1,0:T(8,128)}) custom-call(s32[1,521]{1,0:T(1,128)} %counts_hbm.1, s32[1,5632]{1,0:T(1,128)} %cells_hbm.1, f32[3,1,5632]{2,1,0:T(1,128)} %frac_hbm.1, f32[3,1,5632]{2,1,0:T(1,128)} %pos_hbm.1, f32[3,1,5632]{2,1,0:T(1,128)} %vel_hbm.1), custom_call_target="tpu_custom_call" | custom-call | tf_op jit(solution)/shard_map/pack/pallas_call | solution.py:130
  2.3 0.0 collective-permute-start
  2.4 2.9 %collective-permute-start.1 = (f32[8,1536]{1,0:T(8,128)}, f32[8,1536]{1,0:T(8,128)S(1)}, u32[]{:S(2)}, u32[]{:S(2)}) collective-permute-start(f32[8,1536]{1,0:T(8,128)} %get-tuple-element.12), channel_id=1, source_target_pairs={{1,0},{2,1},{3,2},{4,3},{5,4},{6,5},{7,6},{0,7},{9,8},{10,9},{11,1... | collective-permute-start | bytes 147464 | tf_op jit(solution)/shard_map/ppermute | solution.py:73
  5.3 18.9 %all-to-all-start = ((f32[64,2,128]{2,1,0:T(2,128)}), f32[64,2,128]{2,1,0:T(2,128)S(1)}, u32[]{:S(2)}, u32[]{:S(2)}) async-start(f32[64,2,128]{2,1,0:T(2,128)} %bitcast.8), calls=%async_computation | async-start | bytes 131072 | tf_op jit(solution)/shard_map/all_to_all | solution.py:376
  24.3 4.0 %collective-permute-start.2 = (f32[8,1536]{1,0:T(8,128)S(1)}, f32[8,1536]{1,0:T(8,128)S(1)}, u32[]{:S(2)}, u32[]{:S(2)}) collective-permute-start(f32[8,1536]{1,0:T(8,128)S(1)} %pad_maximum_fusion), channel_id=1, source_target_pairs={{496,0},{504,8},{0,16},{8,24},{16,32},{24,40},{32,48},{40,56},{48,... | collective-permute-start | bytes 147464 | tf_op jit(solution)/shard_map/ppermute | solution.py:73
  28.3 2.8 %collective-permute-start.4 = (f32[8,4608]{1,0:T(8,128)S(1)}, f32[8,4608]{1,0:T(8,128)S(1)}, u32[]{:S(2)}, u32[]{:S(2)}) collective-permute-start(f32[8,4608]{1,0:T(8,128)S(1)} %constant_dynamic-update-slice_fusion.held_ref), channel_id=1, source_target_pairs={{8,16},{24,32},{40,48},{56,64},{72,80},{88,96},{104,112},{120,128}... | collective-permute-start | bytes 442376 | tf_op jit(solution)/shard_map/ppermute | solution.py:67
  31.1 5.8 %collective-permute-start.3 = (f32[8,4608]{1,0:T(8,128)S(1)}, f32[8,4608]{1,0:T(8,128)S(1)}, u32[]{:S(2)}, u32[]{:S(2)}) collective-permute-start(f32[8,4608]{1,0:T(8,128)S(1)} %constant_dynamic-update-slice_fusion.held_ref), channel_id=1, source_target_pairs={{0,8},{16,24},{32,40},{48,56},{64,72},{80,88},{96,104},{112,120},{... | collective-permute-start | bytes 442376 | tf_op jit(solution)/shard_map/ppermute | solution.py:67
  36.9 1.6 %paint_held.1.after_ref.first_ref = f32[160,768]{1,0:T(8,128)S(1)} custom-call(f32[8,4608]{1,0:T(8,128)S(1)} %constant_dynamic-update-slice_fusion.held_ref, f32[8,1536]{1,0:T(8,128)S(1)} %collective-permute-done.2.after_ref.below2_ref), custom_call_target="tpu_custom_call" | custom-call | flops 1000000000 | bytes 1000000 | tf_op jit(solution)/shard_map/paint_held/pallas_call | solution.py:213
  38.5 0.0 all-to-all-done
  38.5 0.8 repack.1
  39.3 3.4 %all-to-all-start.1 = ((f32[8,16,128]{2,1,0:T(8,128)}), f32[8,16,128]{2,1,0:T(8,128)S(1)}, u32[]{:S(2)}, u32[]{:S(2)}) async-start(f32[8,16,128]{2,1,0:T(8,128)} %repack.1), calls=%async_computation.1 | async-start | bytes 131072 | tf_op jit(solution)/shard_map/all_to_all | solution.py:378
  42.7 0.0 copy-start.4
  42.7 0.0 copy-start.5
  42.7 0.0 copy-start.6
  42.7 0.0 copy-start.7
  42.7 3.5 %paint_near.1.near_ref = f32[160,768]{1,0:T(8,128)S(1)} custom-call(f32[160,768]{1,0:T(8,128)S(1)} %paint_held.1.after_ref.first_ref, f32[8,4608]{1,0:T(8,128)S(1)} %collective-permute-done.3.inner_ref, f32[8,4608]{1,0:T(8,128)S(1)} %collective-permute-done.4.outer_ref, f32[8,1536]{1,0:T(8,128)S(1)} %collective-permute-done.2.after_ref.below2_ref), custom_call_target="tpu_custom_call" | custom-call | flops 2264924160 | bytes 2000000 | tf_op jit(solution)/shard_map/paint_near/pallas_call | solution.py:245
  46.3 1.9 %all-to-all-done.1.tail_ref = f32[8,16,128]{2,1,0:T(8,128)S(1)} async-done(((f32[8,16,128]{2,1,0:T(8,128)}), f32[8,16,128]{2,1,0:T(8,128)S(1)}, u32[]{:S(2)}, u32[]{:S(2)}) %all-to-all-start.1) | async-done | bytes 65568 | tf_op jit(solution)/shard_map/all_to_all | solution.py:378
  48.2 2.4 %paint_tail_transform_z.1 = f32[8,200,128]{2,1,0:T(8,128)S(1)} custom-call(f32[8,16,128]{2,1,0:T(8,128)S(1)} %all-to-all-done.1.tail_ref, f32[160,768]{1,0:T(8,128)S(1)} %paint_near.1.near_ref, bf16[256,512]{1,0:T(8,128)(2,1)S(1)} %copy-done.7, bf16[256,512]{1,0:T(8,128)(2,1)S(1)} %copy-done.6, bf16[256,512]{1,0:T(8,128)(2,1)S(1)} %copy-done.5, ...), custom_call_target="tpu_custom_call" | custom-call | tf_op jit(solution)/shard_map/paint_tail_transform_z/pallas_call | solution.py:286
  50.6 0.0 copy-start.2
  50.6 0.0 copy-start.3
  50.6 16.3 %all_to_all.20.in_ref = f32[8,200,128]{2,1,0:T(8,128)S(1)} all-to-all(f32[8,200,128]{2,1,0:T(8,128)S(1)} %paint_tail_transform_z.1), channel_id=1, replica_groups=mesh['slab'=64,'pencil'=8] {'pencil'}, dimensions={0} | all-to-all | bytes 1638400 | tf_op jit(solution)/shard_map/all_to_all | solution.py:381
  67.0 1.0 transform_y.1
  68.0 46.3 %all_to_all.21 = f32[64,16,128]{2,1,0:T(8,128)S(1)} all-to-all(f32[64,16,128]{2,1,0:T(8,128)S(1)} %bitcast.6), channel_id=1, replica_groups=mesh['slab'=64,'pencil'=8] {'slab'}, dimensions={0} | all-to-all | bytes 1048576 | tf_op jit(solution)/shard_map/all_to_all | solution.py:383
  114.3 1.4 %transform_x.1 = f32[2,128,256]{2,1,0:T(8,128)} custom-call(f32[1024,128]{1,0:T(8,128)S(1)} %bitcast.5, bf16[256,1024]{1,0:T(8,128)(2,1)S(1)} %copy-done.1, bf16[256,1024]{1,0:T(8,128)(2,1)S(1)} %copy-done), custom_call_target="tpu_custom_call" | custom-call | tf_op jit(solution)/shard_map/transform_x/pallas_call | solution.py:355
  (24 shorter events, 0.1 us)
Async XLA Ops:
  2.3 21.9 %collective-permute-start = (f32[8,1536]{1,0:T(8,128)}, f32[8,1536]{1,0:T(8,128)S(1)}, u32[]{:S(2)}, u32[]{:S(2)}) collective-permute-start(f32[8,1536]{1,0:T(8,128)} %get-tuple-element.10), channel_id=1, source_target_pairs={{7,0},{0,1},{1,2},{2,3},{3,4},{4,5},{5,6},{6,7},{15,8},{8,9},{9,10... | collective-permute-start | bytes 147464 | tf_op jit(solution)/shard_map/ppermute | solution.py:73
  2.4 21.9 %collective-permute-start.1 = (f32[8,1536]{1,0:T(8,128)}, f32[8,1536]{1,0:T(8,128)S(1)}, u32[]{:S(2)}, u32[]{:S(2)}) collective-permute-start(f32[8,1536]{1,0:T(8,128)} %get-tuple-element.12), channel_id=1, source_target_pairs={{1,0},{2,1},{3,2},{4,3},{5,4},{6,5},{7,6},{0,7},{9,8},{10,9},{11,1... | collective-permute-start | bytes 147464 | tf_op jit(solution)/shard_map/ppermute | solution.py:73
  5.3 18.9 %copy-start.8 = (f32[8,1536]{1,0:T(8,128)S(1)}, f32[8,1536]{1,0:T(8,128)}, u32[]{:S(2)}) copy-start(f32[8,1536]{1,0:T(8,128)} %get-tuple-element.11) | copy-start | bytes 147460
  5.3 33.2 %all-to-all-start = ((f32[64,2,128]{2,1,0:T(2,128)}), f32[64,2,128]{2,1,0:T(2,128)S(1)}, u32[]{:S(2)}, u32[]{:S(2)}) async-start(f32[64,2,128]{2,1,0:T(2,128)} %bitcast.8), calls=%async_computation | async-start | bytes 131072 | tf_op jit(solution)/shard_map/all_to_all | solution.py:376
  24.3 12.6 %collective-permute-start.2 = (f32[8,1536]{1,0:T(8,128)S(1)}, f32[8,1536]{1,0:T(8,128)S(1)}, u32[]{:S(2)}, u32[]{:S(2)}) collective-permute-start(f32[8,1536]{1,0:T(8,128)S(1)} %pad_maximum_fusion), channel_id=1, source_target_pairs={{496,0},{504,8},{0,16},{8,24},{16,32},{24,40},{32,48},{40,56},{48,... | collective-permute-start | bytes 147464 | tf_op jit(solution)/shard_map/ppermute | solution.py:73
  28.3 14.4 %collective-permute-start.4 = (f32[8,4608]{1,0:T(8,128)S(1)}, f32[8,4608]{1,0:T(8,128)S(1)}, u32[]{:S(2)}, u32[]{:S(2)}) collective-permute-start(f32[8,4608]{1,0:T(8,128)S(1)} %constant_dynamic-update-slice_fusion.held_ref), channel_id=1, source_target_pairs={{8,16},{24,32},{40,48},{56,64},{72,80},{88,96},{104,112},{120,128}... | collective-permute-start | bytes 442376 | tf_op jit(solution)/shard_map/ppermute | solution.py:67
  31.1 11.7 %collective-permute-start.3 = (f32[8,4608]{1,0:T(8,128)S(1)}, f32[8,4608]{1,0:T(8,128)S(1)}, u32[]{:S(2)}, u32[]{:S(2)}) collective-permute-start(f32[8,4608]{1,0:T(8,128)S(1)} %constant_dynamic-update-slice_fusion.held_ref), channel_id=1, source_target_pairs={{0,8},{16,24},{32,40},{48,56},{64,72},{80,88},{96,104},{112,120},{... | collective-permute-start | bytes 442376 | tf_op jit(solution)/shard_map/ppermute | solution.py:67
  39.3 8.9 %all-to-all-start.1 = ((f32[8,16,128]{2,1,0:T(8,128)}), f32[8,16,128]{2,1,0:T(8,128)S(1)}, u32[]{:S(2)}, u32[]{:S(2)}) async-start(f32[8,16,128]{2,1,0:T(8,128)} %repack.1), calls=%async_computation.1 | async-start | bytes 131072 | tf_op jit(solution)/shard_map/all_to_all | solution.py:378
  42.7 5.5 %copy-start.4 = (bf16[256,512]{1,0:T(8,128)(2,1)S(1)}, bf16[256,512]{1,0:T(8,128)(2,1)}, u32[]{:S(2)}) copy-start(bf16[256,512]{1,0:T(8,128)(2,1)} %constant.19.clone.scaled_low) | copy-start | bytes 786436
  42.7 5.5 %copy-start.5 = (bf16[256,512]{1,0:T(8,128)(2,1)S(1)}, bf16[256,512]{1,0:T(8,128)(2,1)}, u32[]{:S(2)}) copy-start(bf16[256,512]{1,0:T(8,128)(2,1)} %constant.18.clone.scaled_high) | copy-start | bytes 786436
  42.7 5.5 %copy-start.6 = (bf16[256,512]{1,0:T(8,128)(2,1)S(1)}, bf16[256,512]{1,0:T(8,128)(2,1)}, u32[]{:S(2)}) copy-start(bf16[256,512]{1,0:T(8,128)(2,1)} %constant.17.clone.plain_low) | copy-start | bytes 786436
  42.7 5.5 %copy-start.7 = (bf16[256,512]{1,0:T(8,128)(2,1)S(1)}, bf16[256,512]{1,0:T(8,128)(2,1)}, u32[]{:S(2)}) copy-start(bf16[256,512]{1,0:T(8,128)(2,1)} %constant.16.clone.plain_high) | copy-start | bytes 786436
  50.6 16.3 %copy-start.2 = (bf16[256,1024]{1,0:T(8,128)(2,1)S(1)}, bf16[256,1024]{1,0:T(8,128)(2,1)}, u32[]{:S(2)}) copy-start(bf16[256,1024]{1,0:T(8,128)(2,1)} %constant.21.clone.table_low) | copy-start | bytes 1572868
  50.6 16.3 %copy-start.3 = (bf16[256,1024]{1,0:T(8,128)(2,1)S(1)}, bf16[256,1024]{1,0:T(8,128)(2,1)}, u32[]{:S(2)}) copy-start(bf16[256,1024]{1,0:T(8,128)(2,1)} %constant.20.clone.table_high) | copy-start | bytes 1572868
  68.0 46.3 %copy-start = (bf16[256,1024]{1,0:T(8,128)(2,1)S(1)}, bf16[256,1024]{1,0:T(8,128)(2,1)}, u32[]{:S(2)}) copy-start(bf16[256,1024]{1,0:T(8,128)(2,1)} %constant.23.clone.table_low) | copy-start | bytes 1572868
  68.0 46.3 %copy-start.1 = (bf16[256,1024]{1,0:T(8,128)(2,1)S(1)}, bf16[256,1024]{1,0:T(8,128)(2,1)}, u32[]{:S(2)}) copy-start(bf16[256,1024]{1,0:T(8,128)(2,1)} %constant.22.clone.table_high) | copy-start | bytes 1572868

commit v6 on v3

--- a/solution.py
+++ b/solution.py
@@ -171,14 +171,12 @@
     )(tail, after)
 
 
-def paint(values, acc_ref, below=None, spill=False):
+def paint(values, acc_ref, spill=False):
     slots = values.shape[1]
     cell = values[0:1].astype(jnp.int32)
     row = lax.shift_right_logical(cell, 13) * STRIDE + (lax.shift_right_logical(cell, 8) & 31)
     if spill:
         row = row - MAIN
-    if below is not None:
-        row = row - below
     base_z = cell & 255
     next_z = (base_z + 1) & 255
     frac_x, frac_y, frac_z = values[1:2], values[2:3], values[3:4]
@@ -241,19 +239,15 @@
 
 
 def tail_kernel(tail_ref, near_ref, plain_high, plain_low, scaled_high, scaled_low, out_ref, values, painted):
-    turned = tail_ref[...].T
-    for k in range(16):
-        values[:, 128 * k : 128 * k + 128] = turned[8 * k : 8 * k + 8, :]
+    for which in range(2):
+        turned = tail_ref[pl.ds(which, N_SLAB, stride=2), :].T
+        for k in range(0, 16, 2):
+            values[which, :, 64 * k : 64 * k + 128] = jnp.concatenate(
+                [turned[8 * k : 8 * k + 8, :], turned[8 * k + 8 : 8 * k + 16, :]], axis=1
+            )
     painted[...] = near_ref[...]
-    below = lax.broadcasted_iota(jnp.int32, (1, CAP), 1) % 2 * MAIN
-
-    def body(step, carry):
-        for half in range(2):
-            at = pl.ds(pl.multiple_of((2 * step + half) * CAP, CAP), CAP)
-            paint(values[:, at], painted, below)
-        return carry
-
-    lax.fori_loop(0, 2, body, 0)
+    paint(values[0], painted)
+    paint(values[1], painted, spill=True)
     for i in range(3):
         data = painted[:, i * NG : (i + 1) * NG]
         high = data.astype(bf16)
@@ -279,7 +273,7 @@
         out_shape=jax.ShapeDtypeStruct((N_PENCIL, CHUNK, 128), f32),
         in_specs=[VMEM] * 6,
         out_specs=VMEM,
-        scratch_shapes=[pltpu.VMEM((8, 2 * TAILS), f32), pltpu.VMEM((MAIN, 3 * NG), f32)],
+        scratch_shapes=[pltpu.VMEM((2, 8, TAILS), f32), pltpu.VMEM((MAIN, 3 * NG), f32)],
         compiler_params=PARAMS,
         name="paint_tail_transform_z",
     )(tail, near, *plain, *scaled)

time: 116 us -> 116 us (level)
  no operation moved by 1% of the time
where the time goes in v6:
time: 116 us; the launch traced here: 115 us
  blocking collectives  56.8 us (49%)
  starting transfers between devices  36 us (31%)
  Pallas kernels  12.9 us (11%)
  waiting for transfers between devices  9.26 us (8%)
    all_to_all x1, blocking collectives, local(): lax.all_to_all(by_cols.reshape(N_SLAB, 16, 128), 'slab', 0, 0, tiled=True)  38.6 us
    all_to_all x1, blocking collectives, local(): by_rows = lax.all_to_all(by_rows, 'pencil', 0, 0, tiled=True)  18.2 us
    ppermute x2, starting transfers between devices, swapped(): return lax.ppermute(block, 'slab', pairs + [(b, a) for a, b in pairs])  13.9 us
    all_to_all x1, starting transfers between devices, local(): lax.all_to_all(repack(tail, from_below2).reshape(N_SLAB, 2, 128), 'slab',...  11.5 us
    all_to_all x1, waiting for transfers between devices, local(): lax.all_to_all(repack(tail, from_below2).reshape(N_SLAB, 2, 128), 'slab',...  9.24 us
    ppermute x3, starting transfers between devices, shifted(): return lax.ppermute(block, axis, route)  7.19 us
    pallas_call x1, Pallas kernels, paint_near(): pl.pallas_call(near_kernel, out_shape=jax.ShapeDtypeStruct((MAIN, 3 * NG)...  4.87 us
    all_to_all x1, starting transfers between devices, local(): tail = lax.all_to_all(tail, 'pencil', 0, 0, tiled=True)  3.32 us
  transfers between devices with their start and end apart: 7, of which 1 were waited for; matrix products, arithmetic and copies ran while one was open for 0% of the time, Pallas kernels for 5%

profile of v6, /device:TPU:8, one launch (start us, length us, event | category | flops | bytes accessed | tf_op | source)
XLA Modules:
  0.0 115.3 jit_solution(6952797080164230123)
XLA Ops:
  0.0 2.4 %pack.1 = (f32[8,8,128]{2,1,0:T(8,128)}, f32[8,1536]{1,0:T(8,128)}, f32[8,1536]{1,0:T(8,128)}, f32[8,1536]{1,0:T(8,128)}) custom-call(s32[1,521]{1,0:T(1,128)} %counts_hbm.1, s32[1,5632]{1,0:T(1,128)} %cells_hbm.1, f32[3,1,5632]{2,1,0:T(1,128)} %frac_hbm.1, f32[3,1,5632]{2,1,0:T(1,128)} %pos_hbm.1, f32[3,1,5632]{2,1,0:T(1,128)} %vel_hbm.1), custom_call_target="tpu_custom_call" | custom-call | tf_op jit(solution)/shard_map/pack/pallas_call | solution.py:131
  2.5 0.0 collective-permute-start
  2.5 2.9 %collective-permute-start.1 = (f32[8,1536]{1,0:T(8,128)}, f32[8,1536]{1,0:T(8,128)S(1)}, u32[]{:S(2)}, u32[]{:S(2)}) collective-permute-start(f32[8,1536]{1,0:T(8,128)} %get-tuple-element.12), channel_id=1, source_target_pairs={{1,0},{2,1},{3,2},{4,3},{5,4},{6,5},{7,6},{0,7},{9,8},{10,9},{11,1... | collective-permute-start | bytes 147464 | tf_op jit(solution)/shard_map/ppermute | solution.py:73
  5.4 3.3 %all-to-all-start = ((f32[8,8,128]{2,1,0:T(8,128)}), f32[8,8,128]{2,1,0:T(8,128)S(1)}, u32[]{:S(2)}, u32[]{:S(2)}) async-start(f32[8,8,128]{2,1,0:T(8,128)} %get-tuple-element.9), calls=%async_computation | async-start | bytes 65536 | tf_op jit(solution)/shard_map/all_to_all | solution.py:361
  8.8 4.2 %collective-permute-start.2 = (f32[8,1536]{1,0:T(8,128)S(1)}, f32[8,1536]{1,0:T(8,128)S(1)}, u32[]{:S(2)}, u32[]{:S(2)}) collective-permute-start(f32[8,1536]{1,0:T(8,128)S(1)} %pad_maximum_fusion), channel_id=1, source_target_pairs={{496,0},{504,8},{0,16},{8,24},{16,32},{24,40},{32,48},{40,56},{48,... | collective-permute-start | bytes 147464 | tf_op jit(solution)/shard_map/ppermute | solution.py:73
  13.1 2.9 %collective-permute-start.4 = (f32[8,4608]{1,0:T(8,128)S(1)}, f32[8,4608]{1,0:T(8,128)S(1)}, u32[]{:S(2)}, u32[]{:S(2)}) collective-permute-start(f32[8,4608]{1,0:T(8,128)S(1)} %constant_dynamic-update-slice_fusion.held_ref), channel_id=1, source_target_pairs={{8,16},{24,32},{40,48},{56,64},{72,80},{88,96},{104,112},{120,128}... | collective-permute-start | bytes 442376 | tf_op jit(solution)/shard_map/ppermute | solution.py:67
  16.0 11.1 %collective-permute-start.3 = (f32[8,4608]{1,0:T(8,128)S(1)}, f32[8,4608]{1,0:T(8,128)S(1)}, u32[]{:S(2)}, u32[]{:S(2)}) collective-permute-start(f32[8,4608]{1,0:T(8,128)S(1)} %constant_dynamic-update-slice_fusion.held_ref), channel_id=1, source_target_pairs={{0,8},{16,24},{32,40},{48,56},{64,72},{80,88},{96,104},{112,120},{... | collective-permute-start | bytes 442376 | tf_op jit(solution)/shard_map/ppermute | solution.py:67
  27.1 0.8 repack.1
  27.8 11.5 %all-to-all-start.1 = ((f32[64,2,128]{2,1,0:T(2,128)}), f32[64,2,128]{2,1,0:T(2,128)S(1)}, u32[]{:S(2)}, u32[]{:S(2)}) async-start(f32[64,2,128]{2,1,0:T(2,128)} %bitcast), calls=%async_computation.1 | async-start | bytes 131072 | tf_op jit(solution)/shard_map/all_to_all | solution.py:362
  39.4 0.0 copy-start.4
  39.4 0.0 copy-start.5
  39.4 0.0 copy-start.6
  39.4 0.0 copy-start.7
  39.4 4.9 %paint_near.1.near_ref = f32[160,768]{1,0:T(8,128)S(1)} custom-call(f32[8,4608]{1,0:T(8,128)S(1)} %constant_dynamic-update-slice_fusion.held_ref, f32[8,4608]{1,0:T(8,128)S(1)} %collective-permute-done.3.inner_ref, f32[8,4608]{1,0:T(8,128)S(1)} %collective-permute-done.4.outer_ref, f32[8,1536]{1,0:T(8,128)S(1)} %collective-permute-done.2.after_ref.below2_ref), custom_call_target="tpu_custom_call" | custom-call | flops 9059696640 | bytes 2000000 | tf_op jit(solution)/shard_map/paint_near/pallas_call | solution.py:230
  44.3 9.2 %all-to-all-done.1 = f32[64,2,128]{2,1,0:T(2,128)S(1)} async-done(((f32[64,2,128]{2,1,0:T(2,128)}), f32[64,2,128]{2,1,0:T(2,128)S(1)}, u32[]{:S(2)}, u32[]{:S(2)}) %all-to-all-start.1) | async-done | bytes 65568 | tf_op jit(solution)/shard_map/all_to_all | solution.py:362
  53.6 2.4 %paint_tail_transform_z.1 = f32[8,200,128]{2,1,0:T(8,128)S(1)} custom-call(f32[128,128]{1,0:T(8,128)S(1)} %bitcast.7, f32[160,768]{1,0:T(8,128)S(1)} %paint_near.1.near_ref, bf16[256,512]{1,0:T(8,128)(2,1)S(1)} %copy-done.7, bf16[256,512]{1,0:T(8,128)(2,1)S(1)} %copy-done.6, bf16[256,512]{1,0:T(8,128)(2,1)S(1)} %copy-done.5, bf16[256,512]{1,0:T(8,128)(2,1)S(1)} %copy-done.4), custom_call_target="tpu_custom_call" | custom-call | tf_op jit(solution)/shard_map/paint_tail_transform_z/pallas_call | solution.py:271
  56.0 0.0 copy-start.2
  56.0 0.0 copy-start.3
  56.0 18.2 %all_to_all.20.in_ref = f32[8,200,128]{2,1,0:T(8,128)S(1)} all-to-all(f32[8,200,128]{2,1,0:T(8,128)S(1)} %paint_tail_transform_z.1), channel_id=1, replica_groups=mesh['slab'=64,'pencil'=8] {'pencil'}, dimensions={0} | all-to-all | bytes 1638400 | tf_op jit(solution)/shard_map/all_to_all | solution.py:365
  74.2 1.0 transform_y.1
  75.2 0.0 copy-start
  75.3 0.0 copy-start.1
  75.3 38.6 %all_to_all.21 = f32[64,16,128]{2,1,0:T(8,128)S(1)} all-to-all(f32[64,16,128]{2,1,0:T(8,128)S(1)} %bitcast.6), channel_id=1, replica_groups=mesh['slab'=64,'pencil'=8] {'slab'}, dimensions={0} | all-to-all | bytes 1048576 | tf_op jit(solution)/shard_map/all_to_all | solution.py:367
  113.9 1.4 %transform_x.1 = f32[2,128,256]{2,1,0:T(8,128)} custom-call(f32[1024,128]{1,0:T(8,128)S(1)} %bitcast.5, bf16[256,1024]{1,0:T(8,128)(2,1)S(1)} %copy-done.1, bf16[256,1024]{1,0:T(8,128)(2,1)S(1)} %copy-done), custom_call_target="tpu_custom_call" | custom-call | tf_op jit(solution)/shard_map/transform_x/pallas_call | solution.py:340
  (23 shorter events, 0.1 us)
Async XLA Ops:
  2.4 6.3 %copy-start.8 = (f32[8,1536]{1,0:T(8,128)S(1)}, f32[8,1536]{1,0:T(8,128)}, u32[]{:S(2)}) copy-start(f32[8,1536]{1,0:T(8,128)} %get-tuple-element.11) | copy-start | bytes 147460
  2.5 6.3 %collective-permute-start = (f32[8,1536]{1,0:T(8,128)}, f32[8,1536]{1,0:T(8,128)S(1)}, u32[]{:S(2)}, u32[]{:S(2)}) collective-permute-start(f32[8,1536]{1,0:T(8,128)} %get-tuple-element.10), channel_id=1, source_target_pairs={{7,0},{0,1},{1,2},{2,3},{3,4},{4,5},{5,6},{6,7},{15,8},{8,9},{9,10... | collective-permute-start | bytes 147464 | tf_op jit(solution)/shard_map/ppermute | solution.py:73
  2.5 6.3 %collective-permute-start.1 = (f32[8,1536]{1,0:T(8,128)}, f32[8,1536]{1,0:T(8,128)S(1)}, u32[]{:S(2)}, u32[]{:S(2)}) collective-permute-start(f32[8,1536]{1,0:T(8,128)} %get-tuple-element.12), channel_id=1, source_target_pairs={{1,0},{2,1},{3,2},{4,3},{5,4},{6,5},{7,6},{0,7},{9,8},{10,9},{11,1... | collective-permute-start | bytes 147464 | tf_op jit(solution)/shard_map/ppermute | solution.py:73
  5.4 21.6 %all-to-all-start = ((f32[8,8,128]{2,1,0:T(8,128)}), f32[8,8,128]{2,1,0:T(8,128)S(1)}, u32[]{:S(2)}, u32[]{:S(2)}) async-start(f32[8,8,128]{2,1,0:T(8,128)} %get-tuple-element.9), calls=%async_computation | async-start | bytes 65536 | tf_op jit(solution)/shard_map/all_to_all | solution.py:361
  8.8 18.2 %collective-permute-start.2 = (f32[8,1536]{1,0:T(8,128)S(1)}, f32[8,1536]{1,0:T(8,128)S(1)}, u32[]{:S(2)}, u32[]{:S(2)}) collective-permute-start(f32[8,1536]{1,0:T(8,128)S(1)} %pad_maximum_fusion), channel_id=1, source_target_pairs={{496,0},{504,8},{0,16},{8,24},{16,32},{24,40},{32,48},{40,56},{48,... | collective-permute-start | bytes 147464 | tf_op jit(solution)/shard_map/ppermute | solution.py:73
  13.1 26.3 %collective-permute-start.4 = (f32[8,4608]{1,0:T(8,128)S(1)}, f32[8,4608]{1,0:T(8,128)S(1)}, u32[]{:S(2)}, u32[]{:S(2)}) collective-permute-start(f32[8,4608]{1,0:T(8,128)S(1)} %constant_dynamic-update-slice_fusion.held_ref), channel_id=1, source_target_pairs={{8,16},{24,32},{40,48},{56,64},{72,80},{88,96},{104,112},{120,128}... | collective-permute-start | bytes 442376 | tf_op jit(solution)/shard_map/ppermute | solution.py:67
  16.0 23.4 %collective-permute-start.3 = (f32[8,4608]{1,0:T(8,128)S(1)}, f32[8,4608]{1,0:T(8,128)S(1)}, u32[]{:S(2)}, u32[]{:S(2)}) collective-permute-start(f32[8,4608]{1,0:T(8,128)S(1)} %constant_dynamic-update-slice_fusion.held_ref), channel_id=1, source_target_pairs={{0,8},{16,24},{32,40},{48,56},{64,72},{80,88},{96,104},{112,120},{... | collective-permute-start | bytes 442376 | tf_op jit(solution)/shard_map/ppermute | solution.py:67
  27.8 25.7 %all-to-all-start.1 = ((f32[64,2,128]{2,1,0:T(2,128)}), f32[64,2,128]{2,1,0:T(2,128)S(1)}, u32[]{:S(2)}, u32[]{:S(2)}) async-start(f32[64,2,128]{2,1,0:T(2,128)} %bitcast), calls=%async_computation.1 | async-start | bytes 131072 | tf_op jit(solution)/shard_map/all_to_all | solution.py:362
  39.4 14.2 %copy-start.4 = (bf16[256,512]{1,0:T(8,128)(2,1)S(1)}, bf16[256,512]{1,0:T(8,128)(2,1)}, u32[]{:S(2)}) copy-start(bf16[256,512]{1,0:T(8,128)(2,1)} %constant.19.clone.scaled_low) | copy-start | bytes 786436
  39.4 14.2 %copy-start.5 = (bf16[256,512]{1,0:T(8,128)(2,1)S(1)}, bf16[256,512]{1,0:T(8,128)(2,1)}, u32[]{:S(2)}) copy-start(bf16[256,512]{1,0:T(8,128)(2,1)} %constant.18.clone.scaled_high) | copy-start | bytes 786436
  39.4 14.2 %copy-start.6 = (bf16[256,512]{1,0:T(8,128)(2,1)S(1)}, bf16[256,512]{1,0:T(8,128)(2,1)}, u32[]{:S(2)}) copy-start(bf16[256,512]{1,0:T(8,128)(2,1)} %constant.17.clone.plain_low) | copy-start | bytes 786436
  39.4 14.2 %copy-start.7 = (bf16[256,512]{1,0:T(8,128)(2,1)S(1)}, bf16[256,512]{1,0:T(8,128)(2,1)}, u32[]{:S(2)}) copy-start(bf16[256,512]{1,0:T(8,128)(2,1)} %constant.16.clone.plain_high) | copy-start | bytes 786436
  56.0 18.2 %copy-start.2 = (bf16[256,1024]{1,0:T(8,128)(2,1)S(1)}, bf16[256,1024]{1,0:T(8,128)(2,1)}, u32[]{:S(2)}) copy-start(bf16[256,1024]{1,0:T(8,128)(2,1)} %constant.21.clone.table_low) | copy-start | bytes 1572868
  56.0 18.2 %copy-start.3 = (bf16[256,1024]{1,0:T(8,128)(2,1)S(1)}, bf16[256,1024]{1,0:T(8,128)(2,1)}, u32[]{:S(2)}) copy-start(bf16[256,1024]{1,0:T(8,128)(2,1)} %constant.20.clone.table_high) | copy-start | bytes 1572868
  75.2 38.6 %copy-start = (bf16[256,1024]{1,0:T(8,128)(2,1)S(1)}, bf16[256,1024]{1,0:T(8,128)(2,1)}, u32[]{:S(2)}) copy-start(bf16[256,1024]{1,0:T(8,128)(2,1)} %constant.23.clone.table_low) | copy-start | bytes 1572868
  75.3 38.6 %copy-start.1 = (bf16[256,1024]{1,0:T(8,128)(2,1)S(1)}, bf16[256,1024]{1,0:T(8,128)(2,1)}, u32[]{:S(2)}) copy-start(bf16[256,1024]{1,0:T(8,128)(2,1)} %constant.22.clone.table_high) | copy-start | bytes 1572868

commit v7 on v6

--- a/solution.py
+++ b/solution.py
@@ -322,7 +322,7 @@
     return jnp.where(position < NG // 2, position, position - NG).astype(f32)
 
 
-def x_kernel(in_ref, table_high, table_low, out_ref):
+def x_kernel(in_ref, table_high, table_low, out_hbm, out_ref, sems):
     lines = [in_ref[pl.ds(block, NG, stride=4), :] for block in range(4)]
     data = jnp.concatenate([mixed_rhs(lines[0], lines[1]), mixed_rhs(lines[2], lines[3])], axis=0)
     mixed = product(table_high[...], table_low[...], data)
@@ -332,8 +332,13 @@
     wave_x = wavenumber(lax.broadcasted_iota(jnp.int32, (NG, 1), 0))
     wave_sq = wave_x * wave_x + wave_y * wave_y + wave_z * wave_z
     factor = jnp.where(wave_sq > 0, out_scale / jnp.sqrt(jnp.maximum(wave_sq, 1.0)), 0.0) / NG**1.5
-    out_ref[0] = (mixed[:, 128:] * factor).T
-    out_ref[1] = (mixed[:, :128] * -factor).T
+    copies = []
+    for part, block in enumerate((mixed[:, 128:] * factor, mixed[:, :128] * -factor)):
+        out_ref[part] = block.T
+        copies.append(pltpu.make_async_copy(out_ref.at[part], out_hbm.at[part], sems.at[part]))
+        copies[-1].start()
+    for copy in copies:
+        copy.wait()
 
 
 def transform_x(by_cols, table):
@@ -341,7 +346,8 @@
         x_kernel,
         out_shape=jax.ShapeDtypeStruct((2, 128, NG), f32),
         in_specs=[VMEM] * 3,
-        out_specs=VMEM,
+        out_specs=HBM,
+        scratch_shapes=[pltpu.VMEM((2, 128, NG), f32), pltpu.SemaphoreType.DMA((2,))],
         compiler_params=PARAMS,
         name="transform_x",
     )(by_cols, *table)

time: 116 us -> 116 us (level)
  no operation moved by 1% of the time
where the time goes in v7:
time: 116 us; the launch traced here: 115 us
  blocking collectives  56.8 us (49%)
  starting transfers between devices  36 us (31%)
  Pallas kernels  12.9 us (11%)
  waiting for transfers between devices  9.26 us (8%)
    all_to_all x1, blocking collectives, local(): lax.all_to_all(by_cols.reshape(N_SLAB, 16, 128), 'slab', 0, 0, tiled=True)  38.6 us
    all_to_all x1, blocking collectives, local(): by_rows = lax.all_to_all(by_rows, 'pencil', 0, 0, tiled=True)  18.2 us
    ppermute x2, starting transfers between devices, swapped(): return lax.ppermute(block, 'slab', pairs + [(b, a) for a, b in pairs])  13.9 us
    all_to_all x1, starting transfers between devices, local(): lax.all_to_all(repack(tail, from_below2).reshape(N_SLAB, 2, 128), 'slab',...  11.5 us
    all_to_all x1, waiting for transfers between devices, local(): lax.all_to_all(repack(tail, from_below2).reshape(N_SLAB, 2, 128), 'slab',...  9.24 us
    ppermute x3, starting transfers between devices, shifted(): return lax.ppermute(block, axis, route)  7.19 us
    pallas_call x1, Pallas kernels, paint_near(): pl.pallas_call(near_kernel, out_shape=jax.ShapeDtypeStruct((MAIN, 3 * NG)...  4.87 us
    all_to_all x1, starting transfers between devices, local(): tail = lax.all_to_all(tail, 'pencil', 0, 0, tiled=True)  3.32 us
  transfers between devices with their start and end apart: 7, of which 1 were waited for; matrix products, arithmetic and copies ran while one was open for 0% of the time, Pallas kernels for 5%

profile of v7, /device:TPU:8, one launch (start us, length us, event | category | flops | bytes accessed | tf_op | source)
XLA Modules:
  0.0 115.3 jit_solution(482699192896857648)
XLA Ops:
  0.0 2.4 %pack.1 = (f32[8,8,128]{2,1,0:T(8,128)}, f32[8,1536]{1,0:T(8,128)}, f32[8,1536]{1,0:T(8,128)}, f32[8,1536]{1,0:T(8,128)}) custom-call(s32[1,521]{1,0:T(1,128)} %counts_hbm.1, s32[1,5632]{1,0:T(1,128)} %cells_hbm.1, f32[3,1,5632]{2,1,0:T(1,128)} %frac_hbm.1, f32[3,1,5632]{2,1,0:T(1,128)} %pos_hbm.1, f32[3,1,5632]{2,1,0:T(1,128)} %vel_hbm.1), custom_call_target="tpu_custom_call" | custom-call | tf_op jit(solution)/shard_map/pack/pallas_call | solution.py:131
  2.5 0.0 collective-permute-start
  2.5 2.9 %collective-permute-start.1 = (f32[8,1536]{1,0:T(8,128)}, f32[8,1536]{1,0:T(8,128)S(1)}, u32[]{:S(2)}, u32[]{:S(2)}) collective-permute-start(f32[8,1536]{1,0:T(8,128)} %get-tuple-element.12), channel_id=1, source_target_pairs={{1,0},{2,1},{3,2},{4,3},{5,4},{6,5},{7,6},{0,7},{9,8},{10,9},{11,1... | collective-permute-start | bytes 147464 | tf_op jit(solution)/shard_map/ppermute | solution.py:73
  5.4 3.3 %all-to-all-start = ((f32[8,8,128]{2,1,0:T(8,128)}), f32[8,8,128]{2,1,0:T(8,128)S(1)}, u32[]{:S(2)}, u32[]{:S(2)}) async-start(f32[8,8,128]{2,1,0:T(8,128)} %get-tuple-element.9), calls=%async_computation | async-start | bytes 65536 | tf_op jit(solution)/shard_map/all_to_all | solution.py:367
  8.8 4.2 %collective-permute-start.2 = (f32[8,1536]{1,0:T(8,128)S(1)}, f32[8,1536]{1,0:T(8,128)S(1)}, u32[]{:S(2)}, u32[]{:S(2)}) collective-permute-start(f32[8,1536]{1,0:T(8,128)S(1)} %pad_maximum_fusion), channel_id=1, source_target_pairs={{496,0},{504,8},{0,16},{8,24},{16,32},{24,40},{32,48},{40,56},{48,... | collective-permute-start | bytes 147464 | tf_op jit(solution)/shard_map/ppermute | solution.py:73
  13.1 2.9 %collective-permute-start.4 = (f32[8,4608]{1,0:T(8,128)S(1)}, f32[8,4608]{1,0:T(8,128)S(1)}, u32[]{:S(2)}, u32[]{:S(2)}) collective-permute-start(f32[8,4608]{1,0:T(8,128)S(1)} %constant_dynamic-update-slice_fusion.held_ref), channel_id=1, source_target_pairs={{8,16},{24,32},{40,48},{56,64},{72,80},{88,96},{104,112},{120,128}... | collective-permute-start | bytes 442376 | tf_op jit(solution)/shard_map/ppermute | solution.py:67
  16.0 11.1 %collective-permute-start.3 = (f32[8,4608]{1,0:T(8,128)S(1)}, f32[8,4608]{1,0:T(8,128)S(1)}, u32[]{:S(2)}, u32[]{:S(2)}) collective-permute-start(f32[8,4608]{1,0:T(8,128)S(1)} %constant_dynamic-update-slice_fusion.held_ref), channel_id=1, source_target_pairs={{0,8},{16,24},{32,40},{48,56},{64,72},{80,88},{96,104},{112,120},{... | collective-permute-start | bytes 442376 | tf_op jit(solution)/shard_map/ppermute | solution.py:67
  27.1 0.8 repack.1
  27.8 11.5 %all-to-all-start.1 = ((f32[64,2,128]{2,1,0:T(2,128)}), f32[64,2,128]{2,1,0:T(2,128)S(1)}, u32[]{:S(2)}, u32[]{:S(2)}) async-start(f32[64,2,128]{2,1,0:T(2,128)} %bitcast), calls=%async_computation.1 | async-start | bytes 131072 | tf_op jit(solution)/shard_map/all_to_all | solution.py:368
  39.4 0.0 copy-start.4
  39.4 0.0 copy-start.5
  39.4 0.0 copy-start.6
  39.4 0.0 copy-start.7
  39.4 4.9 %paint_near.1.near_ref = f32[160,768]{1,0:T(8,128)S(1)} custom-call(f32[8,4608]{1,0:T(8,128)S(1)} %constant_dynamic-update-slice_fusion.held_ref, f32[8,4608]{1,0:T(8,128)S(1)} %collective-permute-done.3.inner_ref, f32[8,4608]{1,0:T(8,128)S(1)} %collective-permute-done.4.outer_ref, f32[8,1536]{1,0:T(8,128)S(1)} %collective-permute-done.2.after_ref.below2_ref), custom_call_target="tpu_custom_call" | custom-call | flops 9059696640 | bytes 2000000 | tf_op jit(solution)/shard_map/paint_near/pallas_call | solution.py:230
  44.3 9.2 %all-to-all-done.1 = f32[64,2,128]{2,1,0:T(2,128)S(1)} async-done(((f32[64,2,128]{2,1,0:T(2,128)}), f32[64,2,128]{2,1,0:T(2,128)S(1)}, u32[]{:S(2)}, u32[]{:S(2)}) %all-to-all-start.1) | async-done | bytes 65568 | tf_op jit(solution)/shard_map/all_to_all | solution.py:368
  53.6 2.4 %paint_tail_transform_z.1 = f32[8,200,128]{2,1,0:T(8,128)S(1)} custom-call(f32[128,128]{1,0:T(8,128)S(1)} %bitcast.7, f32[160,768]{1,0:T(8,128)S(1)} %paint_near.1.near_ref, bf16[256,512]{1,0:T(8,128)(2,1)S(1)} %copy-done.7, bf16[256,512]{1,0:T(8,128)(2,1)S(1)} %copy-done.6, bf16[256,512]{1,0:T(8,128)(2,1)S(1)} %copy-done.5, bf16[256,512]{1,0:T(8,128)(2,1)S(1)} %copy-done.4), custom_call_target="tpu_custom_call" | custom-call | tf_op jit(solution)/shard_map/paint_tail_transform_z/pallas_call | solution.py:271
  56.0 0.0 copy-start.2
  56.0 0.0 copy-start.3
  56.0 18.2 %all_to_all.20.in_ref = f32[8,200,128]{2,1,0:T(8,128)S(1)} all-to-all(f32[8,200,128]{2,1,0:T(8,128)S(1)} %paint_tail_transform_z.1), channel_id=1, replica_groups=mesh['slab'=64,'pencil'=8] {'pencil'}, dimensions={0} | all-to-all | bytes 1638400 | tf_op jit(solution)/shard_map/all_to_all | solution.py:371
  74.2 1.0 transform_y.1
  75.2 0.0 copy-start
  75.3 0.0 copy-start.1
  75.3 38.6 %all_to_all.21 = f32[64,16,128]{2,1,0:T(8,128)S(1)} all-to-all(f32[64,16,128]{2,1,0:T(8,128)S(1)} %bitcast.6), channel_id=1, replica_groups=mesh['slab'=64,'pencil'=8] {'slab'}, dimensions={0} | all-to-all | bytes 1048576 | tf_op jit(solution)/shard_map/all_to_all | solution.py:373
  113.9 1.4 %transform_x.1 = f32[2,128,256]{2,1,0:T(8,128)} custom-call(f32[1024,128]{1,0:T(8,128)S(1)} %bitcast.5, bf16[256,1024]{1,0:T(8,128)(2,1)S(1)} %copy-done.1, bf16[256,1024]{1,0:T(8,128)(2,1)S(1)} %copy-done), custom_call_target="tpu_custom_call" | custom-call | tf_op jit(solution)/shard_map/transform_x/pallas_call | solution.py:345
  (23 shorter events, 0.1 us)
Async XLA Ops:
  2.4 6.3 %copy-start.8 = (f32[8,1536]{1,0:T(8,128)S(1)}, f32[8,1536]{1,0:T(8,128)}, u32[]{:S(2)}) copy-start(f32[8,1536]{1,0:T(8,128)} %get-tuple-element.11) | copy-start | bytes 147460
  2.5 6.3 %collective-permute-start = (f32[8,1536]{1,0:T(8,128)}, f32[8,1536]{1,0:T(8,128)S(1)}, u32[]{:S(2)}, u32[]{:S(2)}) collective-permute-start(f32[8,1536]{1,0:T(8,128)} %get-tuple-element.10), channel_id=1, source_target_pairs={{7,0},{0,1},{1,2},{2,3},{3,4},{4,5},{5,6},{6,7},{15,8},{8,9},{9,10... | collective-permute-start | bytes 147464 | tf_op jit(solution)/shard_map/ppermute | solution.py:73
  2.5 6.3 %collective-permute-start.1 = (f32[8,1536]{1,0:T(8,128)}, f32[8,1536]{1,0:T(8,128)S(1)}, u32[]{:S(2)}, u32[]{:S(2)}) collective-permute-start(f32[8,1536]{1,0:T(8,128)} %get-tuple-element.12), channel_id=1, source_target_pairs={{1,0},{2,1},{3,2},{4,3},{5,4},{6,5},{7,6},{0,7},{9,8},{10,9},{11,1... | collective-permute-start | bytes 147464 | tf_op jit(solution)/shard_map/ppermute | solution.py:73
  5.4 21.6 %all-to-all-start = ((f32[8,8,128]{2,1,0:T(8,128)}), f32[8,8,128]{2,1,0:T(8,128)S(1)}, u32[]{:S(2)}, u32[]{:S(2)}) async-start(f32[8,8,128]{2,1,0:T(8,128)} %get-tuple-element.9), calls=%async_computation | async-start | bytes 65536 | tf_op jit(solution)/shard_map/all_to_all | solution.py:367
  8.8 18.2 %collective-permute-start.2 = (f32[8,1536]{1,0:T(8,128)S(1)}, f32[8,1536]{1,0:T(8,128)S(1)}, u32[]{:S(2)}, u32[]{:S(2)}) collective-permute-start(f32[8,1536]{1,0:T(8,128)S(1)} %pad_maximum_fusion), channel_id=1, source_target_pairs={{496,0},{504,8},{0,16},{8,24},{16,32},{24,40},{32,48},{40,56},{48,... | collective-permute-start | bytes 147464 | tf_op jit(solution)/shard_map/ppermute | solution.py:73
  13.1 26.3 %collective-permute-start.4 = (f32[8,4608]{1,0:T(8,128)S(1)}, f32[8,4608]{1,0:T(8,128)S(1)}, u32[]{:S(2)}, u32[]{:S(2)}) collective-permute-start(f32[8,4608]{1,0:T(8,128)S(1)} %constant_dynamic-update-slice_fusion.held_ref), channel_id=1, source_target_pairs={{8,16},{24,32},{40,48},{56,64},{72,80},{88,96},{104,112},{120,128}... | collective-permute-start | bytes 442376 | tf_op jit(solution)/shard_map/ppermute | solution.py:67
  16.0 23.4 %collective-permute-start.3 = (f32[8,4608]{1,0:T(8,128)S(1)}, f32[8,4608]{1,0:T(8,128)S(1)}, u32[]{:S(2)}, u32[]{:S(2)}) collective-permute-start(f32[8,4608]{1,0:T(8,128)S(1)} %constant_dynamic-update-slice_fusion.held_ref), channel_id=1, source_target_pairs={{0,8},{16,24},{32,40},{48,56},{64,72},{80,88},{96,104},{112,120},{... | collective-permute-start | bytes 442376 | tf_op jit(solution)/shard_map/ppermute | solution.py:67
  27.8 25.7 %all-to-all-start.1 = ((f32[64,2,128]{2,1,0:T(2,128)}), f32[64,2,128]{2,1,0:T(2,128)S(1)}, u32[]{:S(2)}, u32[]{:S(2)}) async-start(f32[64,2,128]{2,1,0:T(2,128)} %bitcast), calls=%async_computation.1 | async-start | bytes 131072 | tf_op jit(solution)/shard_map/all_to_all | solution.py:368
  39.4 14.2 %copy-start.4 = (bf16[256,512]{1,0:T(8,128)(2,1)S(1)}, bf16[256,512]{1,0:T(8,128)(2,1)}, u32[]{:S(2)}) copy-start(bf16[256,512]{1,0:T(8,128)(2,1)} %constant.19.clone.scaled_low) | copy-start | bytes 786436
  39.4 14.2 %copy-start.5 = (bf16[256,512]{1,0:T(8,128)(2,1)S(1)}, bf16[256,512]{1,0:T(8,128)(2,1)}, u32[]{:S(2)}) copy-start(bf16[256,512]{1,0:T(8,128)(2,1)} %constant.18.clone.scaled_high) | copy-start | bytes 786436
  39.4 14.2 %copy-start.6 = (bf16[256,512]{1,0:T(8,128)(2,1)S(1)}, bf16[256,512]{1,0:T(8,128)(2,1)}, u32[]{:S(2)}) copy-start(bf16[256,512]{1,0:T(8,128)(2,1)} %constant.17.clone.plain_low) | copy-start | bytes 786436
  39.4 14.2 %copy-start.7 = (bf16[256,512]{1,0:T(8,128)(2,1)S(1)}, bf16[256,512]{1,0:T(8,128)(2,1)}, u32[]{:S(2)}) copy-start(bf16[256,512]{1,0:T(8,128)(2,1)} %constant.16.clone.plain_high) | copy-start | bytes 786436
  56.0 18.2 %copy-start.2 = (bf16[256,1024]{1,0:T(8,128)(2,1)S(1)}, bf16[256,1024]{1,0:T(8,128)(2,1)}, u32[]{:S(2)}) copy-start(bf16[256,1024]{1,0:T(8,128)(2,1)} %constant.21.clone.table_low) | copy-start | bytes 1572868
  56.0 18.2 %copy-start.3 = (bf16[256,1024]{1,0:T(8,128)(2,1)S(1)}, bf16[256,1024]{1,0:T(8,128)(2,1)}, u32[]{:S(2)}) copy-start(bf16[256,1024]{1,0:T(8,128)(2,1)} %constant.20.clone.table_high) | copy-start | bytes 1572868
  75.2 38.6 %copy-start = (bf16[256,1024]{1,0:T(8,128)(2,1)S(1)}, bf16[256,1024]{1,0:T(8,128)(2,1)}, u32[]{:S(2)}) copy-start(bf16[256,1024]{1,0:T(8,128)(2,1)} %constant.23.clone.table_low) | copy-start | bytes 1572868
  75.3 38.6 %copy-start.1 = (bf16[256,1024]{1,0:T(8,128)(2,1)S(1)}, bf16[256,1024]{1,0:T(8,128)(2,1)}, u32[]{:S(2)}) copy-start(bf16[256,1024]{1,0:T(8,128)(2,1)} %constant.22.clone.table_high) | copy-start | bytes 1572868

commit v8 on v6

--- a/solution.py
+++ b/solution.py
@@ -171,7 +171,7 @@
     )(tail, after)
 
 
-def paint(values, acc_ref, spill=False):
+def paint(values, acc_ref, spill=False, base_ref=None):
     slots = values.shape[1]
     cell = values[0:1].astype(jnp.int32)
     row = lax.shift_right_logical(cell, 13) * STRIDE + (lax.shift_right_logical(cell, 8) & 31)
@@ -199,9 +199,10 @@
         weight = values[4 + i : 5 + i]
         line = jnp.where(at_low, short(weight * rest_z), zero)
         line = jnp.where(at_high, short(weight * frac_z), line)
-        acc_ref[:count, i * NG : (i + 1) * NG] += lax.dot_general(
-            corner, line, (((1,), (1,)), ((), ())), preferred_element_type=f32
-        )
+        columns = slice(i * NG, (i + 1) * NG)
+        product_i = lax.dot_general(corner, line, (((1,), (1,)), ((), ())), preferred_element_type=f32)
+        base = acc_ref if base_ref is None else base_ref
+        acc_ref[:count, columns] = base[:count, columns] + product_i
 
 
 def near_kernel(held_ref, inner_ref, outer_ref, below2_ref, out_ref):
@@ -245,8 +246,7 @@
             values[which, :, 64 * k : 64 * k + 128] = jnp.concatenate(
                 [turned[8 * k : 8 * k + 8, :], turned[8 * k + 8 : 8 * k + 16, :]], axis=1
             )
-    painted[...] = near_ref[...]
-    paint(values[0], painted)
+    paint(values[0], painted, base_ref=near_ref)
     paint(values[1], painted, spill=True)
     for i in range(3):
         data = painted[:, i * NG : (i + 1) * NG]

time: 116 us -> 116 us (level)
  no operation moved by 1% of the time
where the time goes in v8:
time: 116 us; the launch traced here: 115 us
  blocking collectives  56.8 us (49%)
  starting transfers between devices  36 us (31%)
  Pallas kernels  12.9 us (11%)
  waiting for transfers between devices  9.26 us (8%)
    all_to_all x1, blocking collectives, local(): lax.all_to_all(by_cols.reshape(N_SLAB, 16, 128), 'slab', 0, 0, tiled=True)  38.6 us
    all_to_all x1, blocking collectives, local(): by_rows = lax.all_to_all(by_rows, 'pencil', 0, 0, tiled=True)  18.2 us
    ppermute x2, starting transfers between devices, swapped(): return lax.ppermute(block, 'slab', pairs + [(b, a) for a, b in pairs])  13.9 us
    all_to_all x1, starting transfers between devices, local(): lax.all_to_all(repack(tail, from_below2).reshape(N_SLAB, 2, 128), 'slab',...  11.5 us
    all_to_all x1, waiting for transfers between devices, local(): lax.all_to_all(repack(tail, from_below2).reshape(N_SLAB, 2, 128), 'slab',...  9.24 us
    ppermute x3, starting transfers between devices, shifted(): return lax.ppermute(block, axis, route)  7.19 us
    pallas_call x1, Pallas kernels, paint_near(): pl.pallas_call(near_kernel, out_shape=jax.ShapeDtypeStruct((MAIN, 3 * NG)...  4.87 us
    all_to_all x1, starting transfers between devices, local(): tail = lax.all_to_all(tail, 'pencil', 0, 0, tiled=True)  3.32 us
  transfers between devices with their start and end apart: 7, of which 1 were waited for; matrix products, arithmetic and copies ran while one was open for 0% of the time, Pallas kernels for 5%

profile of v8, /device:TPU:8, one launch (start us, length us, event | category | flops | bytes accessed | tf_op | source)
XLA Modules:
  0.0 115.3 jit_solution(6980214875605647667)
XLA Ops:
  0.0 2.4 %pack.1 = (f32[8,8,128]{2,1,0:T(8,128)}, f32[8,1536]{1,0:T(8,128)}, f32[8,1536]{1,0:T(8,128)}, f32[8,1536]{1,0:T(8,128)}) custom-call(s32[1,521]{1,0:T(1,128)} %counts_hbm.1, s32[1,5632]{1,0:T(1,128)} %cells_hbm.1, f32[3,1,5632]{2,1,0:T(1,128)} %frac_hbm.1, f32[3,1,5632]{2,1,0:T(1,128)} %pos_hbm.1, f32[3,1,5632]{2,1,0:T(1,128)} %vel_hbm.1), custom_call_target="tpu_custom_call" | custom-call | tf_op jit(solution)/shard_map/pack/pallas_call | solution.py:131
  2.5 0.0 collective-permute-start
  2.5 2.9 %collective-permute-start.1 = (f32[8,1536]{1,0:T(8,128)}, f32[8,1536]{1,0:T(8,128)S(1)}, u32[]{:S(2)}, u32[]{:S(2)}) collective-permute-start(f32[8,1536]{1,0:T(8,128)} %get-tuple-element.12), channel_id=1, source_target_pairs={{1,0},{2,1},{3,2},{4,3},{5,4},{6,5},{7,6},{0,7},{9,8},{10,9},{11,1... | collective-permute-start | bytes 147464 | tf_op jit(solution)/shard_map/ppermute | solution.py:73
  5.4 3.3 %all-to-all-start = ((f32[8,8,128]{2,1,0:T(8,128)}), f32[8,8,128]{2,1,0:T(8,128)S(1)}, u32[]{:S(2)}, u32[]{:S(2)}) async-start(f32[8,8,128]{2,1,0:T(8,128)} %get-tuple-element.9), calls=%async_computation | async-start | bytes 65536 | tf_op jit(solution)/shard_map/all_to_all | solution.py:361
  8.8 4.2 %collective-permute-start.2 = (f32[8,1536]{1,0:T(8,128)S(1)}, f32[8,1536]{1,0:T(8,128)S(1)}, u32[]{:S(2)}, u32[]{:S(2)}) collective-permute-start(f32[8,1536]{1,0:T(8,128)S(1)} %pad_maximum_fusion), channel_id=1, source_target_pairs={{496,0},{504,8},{0,16},{8,24},{16,32},{24,40},{32,48},{40,56},{48,... | collective-permute-start | bytes 147464 | tf_op jit(solution)/shard_map/ppermute | solution.py:73
  13.1 2.9 %collective-permute-start.4 = (f32[8,4608]{1,0:T(8,128)S(1)}, f32[8,4608]{1,0:T(8,128)S(1)}, u32[]{:S(2)}, u32[]{:S(2)}) collective-permute-start(f32[8,4608]{1,0:T(8,128)S(1)} %constant_dynamic-update-slice_fusion.held_ref), channel_id=1, source_target_pairs={{8,16},{24,32},{40,48},{56,64},{72,80},{88,96},{104,112},{120,128}... | collective-permute-start | bytes 442376 | tf_op jit(solution)/shard_map/ppermute | solution.py:67
  16.0 11.1 %collective-permute-start.3 = (f32[8,4608]{1,0:T(8,128)S(1)}, f32[8,4608]{1,0:T(8,128)S(1)}, u32[]{:S(2)}, u32[]{:S(2)}) collective-permute-start(f32[8,4608]{1,0:T(8,128)S(1)} %constant_dynamic-update-slice_fusion.held_ref), channel_id=1, source_target_pairs={{0,8},{16,24},{32,40},{48,56},{64,72},{80,88},{96,104},{112,120},{... | collective-permute-start | bytes 442376 | tf_op jit(solution)/shard_map/ppermute | solution.py:67
  27.1 0.8 repack.1
  27.8 11.5 %all-to-all-start.1 = ((f32[64,2,128]{2,1,0:T(2,128)}), f32[64,2,128]{2,1,0:T(2,128)S(1)}, u32[]{:S(2)}, u32[]{:S(2)}) async-start(f32[64,2,128]{2,1,0:T(2,128)} %bitcast), calls=%async_computation.1 | async-start | bytes 131072 | tf_op jit(solution)/shard_map/all_to_all | solution.py:362
  39.4 0.0 copy-start.4
  39.4 0.0 copy-start.5
  39.4 0.0 copy-start.6
  39.4 0.0 copy-start.7
  39.4 4.9 %paint_near.1.near_ref = f32[160,768]{1,0:T(8,128)S(1)} custom-call(f32[8,4608]{1,0:T(8,128)S(1)} %constant_dynamic-update-slice_fusion.held_ref, f32[8,4608]{1,0:T(8,128)S(1)} %collective-permute-done.3.inner_ref, f32[8,4608]{1,0:T(8,128)S(1)} %collective-permute-done.4.outer_ref, f32[8,1536]{1,0:T(8,128)S(1)} %collective-permute-done.2.after_ref.below2_ref), custom_call_target="tpu_custom_call" | custom-call | flops 9059696640 | bytes 2000000 | tf_op jit(solution)/shard_map/paint_near/pallas_call | solution.py:231
  44.3 9.2 %all-to-all-done.1 = f32[64,2,128]{2,1,0:T(2,128)S(1)} async-done(((f32[64,2,128]{2,1,0:T(2,128)}), f32[64,2,128]{2,1,0:T(2,128)S(1)}, u32[]{:S(2)}, u32[]{:S(2)}) %all-to-all-start.1) | async-done | bytes 65568 | tf_op jit(solution)/shard_map/all_to_all | solution.py:362
  53.6 2.4 %paint_tail_transform_z.1 = f32[8,200,128]{2,1,0:T(8,128)S(1)} custom-call(f32[128,128]{1,0:T(8,128)S(1)} %bitcast.7, f32[160,768]{1,0:T(8,128)S(1)} %paint_near.1.near_ref, bf16[256,512]{1,0:T(8,128)(2,1)S(1)} %copy-done.7, bf16[256,512]{1,0:T(8,128)(2,1)S(1)} %copy-done.6, bf16[256,512]{1,0:T(8,128)(2,1)S(1)} %copy-done.5, bf16[256,512]{1,0:T(8,128)(2,1)S(1)} %copy-done.4), custom_call_target="tpu_custom_call" | custom-call | tf_op jit(solution)/shard_map/paint_tail_transform_z/pallas_call | solution.py:271
  56.0 0.0 copy-start.2
  56.0 0.0 copy-start.3
  56.0 18.2 %all_to_all.20.in_ref = f32[8,200,128]{2,1,0:T(8,128)S(1)} all-to-all(f32[8,200,128]{2,1,0:T(8,128)S(1)} %paint_tail_transform_z.1), channel_id=1, replica_groups=mesh['slab'=64,'pencil'=8] {'pencil'}, dimensions={0} | all-to-all | bytes 1638400 | tf_op jit(solution)/shard_map/all_to_all | solution.py:365
  74.2 1.0 transform_y.1
  75.2 0.0 copy-start
  75.3 0.0 copy-start.1
  75.3 38.6 %all_to_all.21 = f32[64,16,128]{2,1,0:T(8,128)S(1)} all-to-all(f32[64,16,128]{2,1,0:T(8,128)S(1)} %bitcast.6), channel_id=1, replica_groups=mesh['slab'=64,'pencil'=8] {'slab'}, dimensions={0} | all-to-all | bytes 1048576 | tf_op jit(solution)/shard_map/all_to_all | solution.py:367
  113.9 1.4 %transform_x.1 = f32[2,128,256]{2,1,0:T(8,128)} custom-call(f32[1024,128]{1,0:T(8,128)S(1)} %bitcast.5, bf16[256,1024]{1,0:T(8,128)(2,1)S(1)} %copy-done.1, bf16[256,1024]{1,0:T(8,128)(2,1)S(1)} %copy-done), custom_call_target="tpu_custom_call" | custom-call | tf_op jit(solution)/shard_map/transform_x/pallas_call | solution.py:340
  (23 shorter events, 0.1 us)
Async XLA Ops:
  2.4 6.3 %copy-start.8 = (f32[8,1536]{1,0:T(8,128)S(1)}, f32[8,1536]{1,0:T(8,128)}, u32[]{:S(2)}) copy-start(f32[8,1536]{1,0:T(8,128)} %get-tuple-element.11) | copy-start | bytes 147460
  2.5 6.3 %collective-permute-start = (f32[8,1536]{1,0:T(8,128)}, f32[8,1536]{1,0:T(8,128)S(1)}, u32[]{:S(2)}, u32[]{:S(2)}) collective-permute-start(f32[8,1536]{1,0:T(8,128)} %get-tuple-element.10), channel_id=1, source_target_pairs={{7,0},{0,1},{1,2},{2,3},{3,4},{4,5},{5,6},{6,7},{15,8},{8,9},{9,10... | collective-permute-start | bytes 147464 | tf_op jit(solution)/shard_map/ppermute | solution.py:73
  2.5 6.3 %collective-permute-start.1 = (f32[8,1536]{1,0:T(8,128)}, f32[8,1536]{1,0:T(8,128)S(1)}, u32[]{:S(2)}, u32[]{:S(2)}) collective-permute-start(f32[8,1536]{1,0:T(8,128)} %get-tuple-element.12), channel_id=1, source_target_pairs={{1,0},{2,1},{3,2},{4,3},{5,4},{6,5},{7,6},{0,7},{9,8},{10,9},{11,1... | collective-permute-start | bytes 147464 | tf_op jit(solution)/shard_map/ppermute | solution.py:73
  5.4 21.6 %all-to-all-start = ((f32[8,8,128]{2,1,0:T(8,128)}), f32[8,8,128]{2,1,0:T(8,128)S(1)}, u32[]{:S(2)}, u32[]{:S(2)}) async-start(f32[8,8,128]{2,1,0:T(8,128)} %get-tuple-element.9), calls=%async_computation | async-start | bytes 65536 | tf_op jit(solution)/shard_map/all_to_all | solution.py:361
  8.8 18.2 %collective-permute-start.2 = (f32[8,1536]{1,0:T(8,128)S(1)}, f32[8,1536]{1,0:T(8,128)S(1)}, u32[]{:S(2)}, u32[]{:S(2)}) collective-permute-start(f32[8,1536]{1,0:T(8,128)S(1)} %pad_maximum_fusion), channel_id=1, source_target_pairs={{496,0},{504,8},{0,16},{8,24},{16,32},{24,40},{32,48},{40,56},{48,... | collective-permute-start | bytes 147464 | tf_op jit(solution)/shard_map/ppermute | solution.py:73
  13.1 26.3 %collective-permute-start.4 = (f32[8,4608]{1,0:T(8,128)S(1)}, f32[8,4608]{1,0:T(8,128)S(1)}, u32[]{:S(2)}, u32[]{:S(2)}) collective-permute-start(f32[8,4608]{1,0:T(8,128)S(1)} %constant_dynamic-update-slice_fusion.held_ref), channel_id=1, source_target_pairs={{8,16},{24,32},{40,48},{56,64},{72,80},{88,96},{104,112},{120,128}... | collective-permute-start | bytes 442376 | tf_op jit(solution)/shard_map/ppermute | solution.py:67
  16.0 23.4 %collective-permute-start.3 = (f32[8,4608]{1,0:T(8,128)S(1)}, f32[8,4608]{1,0:T(8,128)S(1)}, u32[]{:S(2)}, u32[]{:S(2)}) collective-permute-start(f32[8,4608]{1,0:T(8,128)S(1)} %constant_dynamic-update-slice_fusion.held_ref), channel_id=1, source_target_pairs={{0,8},{16,24},{32,40},{48,56},{64,72},{80,88},{96,104},{112,120},{... | collective-permute-start | bytes 442376 | tf_op jit(solution)/shard_map/ppermute | solution.py:67
  27.8 25.7 %all-to-all-start.1 = ((f32[64,2,128]{2,1,0:T(2,128)}), f32[64,2,128]{2,1,0:T(2,128)S(1)}, u32[]{:S(2)}, u32[]{:S(2)}) async-start(f32[64,2,128]{2,1,0:T(2,128)} %bitcast), calls=%async_computation.1 | async-start | bytes 131072 | tf_op jit(solution)/shard_map/all_to_all | solution.py:362
  39.4 14.2 %copy-start.4 = (bf16[256,512]{1,0:T(8,128)(2,1)S(1)}, bf16[256,512]{1,0:T(8,128)(2,1)}, u32[]{:S(2)}) copy-start(bf16[256,512]{1,0:T(8,128)(2,1)} %constant.19.clone.scaled_low) | copy-start | bytes 786436
  39.4 14.2 %copy-start.5 = (bf16[256,512]{1,0:T(8,128)(2,1)S(1)}, bf16[256,512]{1,0:T(8,128)(2,1)}, u32[]{:S(2)}) copy-start(bf16[256,512]{1,0:T(8,128)(2,1)} %constant.18.clone.scaled_high) | copy-start | bytes 786436
  39.4 14.2 %copy-start.6 = (bf16[256,512]{1,0:T(8,128)(2,1)S(1)}, bf16[256,512]{1,0:T(8,128)(2,1)}, u32[]{:S(2)}) copy-start(bf16[256,512]{1,0:T(8,128)(2,1)} %constant.17.clone.plain_low) | copy-start | bytes 786436
  39.4 14.2 %copy-start.7 = (bf16[256,512]{1,0:T(8,128)(2,1)S(1)}, bf16[256,512]{1,0:T(8,128)(2,1)}, u32[]{:S(2)}) copy-start(bf16[256,512]{1,0:T(8,128)(2,1)} %constant.16.clone.plain_high) | copy-start | bytes 786436
  56.0 18.2 %copy-start.2 = (bf16[256,1024]{1,0:T(8,128)(2,1)S(1)}, bf16[256,1024]{1,0:T(8,128)(2,1)}, u32[]{:S(2)}) copy-start(bf16[256,1024]{1,0:T(8,128)(2,1)} %constant.21.clone.table_low) | copy-start | bytes 1572868
  56.0 18.2 %copy-start.3 = (bf16[256,1024]{1,0:T(8,128)(2,1)S(1)}, bf16[256,1024]{1,0:T(8,128)(2,1)}, u32[]{:S(2)}) copy-start(bf16[256,1024]{1,0:T(8,128)(2,1)} %constant.20.clone.table_high) | copy-start | bytes 1572868
  75.2 38.6 %copy-start = (bf16[256,1024]{1,0:T(8,128)(2,1)S(1)}, bf16[256,1024]{1,0:T(8,128)(2,1)}, u32[]{:S(2)}) copy-start(bf16[256,1024]{1,0:T(8,128)(2,1)} %constant.23.clone.table_low) | copy-start | bytes 1572868
  75.3 38.6 %copy-start.1 = (bf16[256,1024]{1,0:T(8,128)(2,1)S(1)}, bf16[256,1024]{1,0:T(8,128)(2,1)}, u32[]{:S(2)}) copy-start(bf16[256,1024]{1,0:T(8,128)(2,1)} %constant.22.clone.table_high) | copy-start | bytes 1572868
